TPU v7x, 256 devices: a whole 4x4x8 slice. The times are simulated.
256 devices in a mesh: clip: 16 (over x, z_hi, core), seq: 16 (over y, z_lo).
Axes of the slice: x: 4, y: 4, z: 8 (z_hi: 2, z_lo: 4; z = z_hi * 4 + z_lo), core: 2. Of those that a mesh axis runs over, the one named last changes fastest.
Arguments:
- video_query: bfloat16 [32768, 4096], P(('clip', 'seq')), parts along dimension 0
- video_key: bfloat16 [32768, 4096], P(('clip', 'seq')), parts along dimension 0
- video_value: bfloat16 [32768, 4096], P(('clip', 'seq')), parts along dimension 0, may hold values from -6 to 6
- cross_query: bfloat16 [32768, 4096], P(('clip', 'seq')), parts along dimension 0
- text_rows: bfloat16 [8192, 4096], P(('clip', 'seq')), parts along dimension 0, may hold values from -6 to 6
- text_block: int32 [256], P('clip'), parts along dimension 0, may hold values from 0 to 15, each once
- text_length: int32 [16], P('clip'), parts along dimension 0, may hold values from 64 to 512
- key_weight: bfloat16 [4096, 4096], P(None, 'seq'), may hold values from -0.09375 to 0.09375
- value_weight: bfloat16 [4096, 4096], P(None, 'seq'), may hold values from -0.09375 to 0.09375
Outputs:
- self_out: bfloat16 [32768, 4096], P(('clip', 'seq')), parts along dimension 0
- cross_out: bfloat16 [32768, 4096], P(('clip', 'seq')), parts along dimension 0
There are 16 independent parts, one for each index of `clip`. A program takes and returns all parts, laid end to end along the dimension named above; an argument that names none is the same for every part. Nothing has to cross between parts.
Inputs may be any that keep to these rules, and one draw needn't show every extreme that they name: A permutation: arrival block j holds prompt rows text_block[j] * 32 onward.
All inputs are finite; a program needn't handle non-finite values.
Results may differ from a plain program's by a relative error of at most 0.012.
The roundings to bfloat16 on the way count: a program that leaves them out, or rounds other values in their place, can miss the bound.
Values may be sent and summed in bfloat16 or wider, within the bound.
No kernel may reach another device: no remote copies, remote signals or barrier semaphores. Data moves between devices by JAX's collectives and lax.ppermute only.
A program may use at most 128 MiB of HBM per device.

v0:
```python
import math

import jax
import jax.numpy as jnp
from jax import lax
from jax.sharding import PartitionSpec as P

HEAD_DIM = 128


def attend(queries, key_rows, value_rows, key_valid):
    query_count = queries.shape[0]
    key_count = key_rows.shape[0]
    head_count = queries.shape[1] // HEAD_DIM
    block_size = query_count if query_count <= 1024 else math.gcd(query_count, 512)
    score_scale = HEAD_DIM ** (-0.5)
    key_heads = key_rows.reshape(key_count, head_count, HEAD_DIM)
    value_heads = value_rows.reshape(key_count, head_count, HEAD_DIM)
    query_blocks = queries.reshape(query_count // block_size, block_size, head_count, HEAD_DIM)

    def one_block(block_rows):
        scores = (
            jnp.einsum("qhd,khd->hqk", block_rows, key_heads, preferred_element_type=jnp.float32)
            * score_scale
        )
        if key_valid is not None:
            scores = jnp.where(key_valid[None, None, :], scores, -jnp.inf)
        highest = jnp.max(scores, axis=-1, keepdims=True)
        exponent = jnp.exp(scores - highest)
        weights = (exponent / jnp.sum(exponent, axis=-1, keepdims=True)).astype(jnp.bfloat16)
        return jnp.einsum(
            "hqk,khd->qhd", weights, value_heads, preferred_element_type=jnp.float32
        ).astype(jnp.bfloat16)

    outputs = lax.map(one_block, query_blocks)
    return outputs.reshape(query_count, head_count * HEAD_DIM)


def body(
    video_query,
    video_key,
    video_value,
    cross_query,
    text_rows,
    text_block,
    text_length,
    key_weight,
    value_weight,
):
    group_size = lax.axis_size("seq")
    text_shard = text_rows.shape[0]
    local_width = key_weight.shape[1]
    piece = lax.all_gather(text_rows, "seq", axis=0, tiled=True)
    keys_part = jnp.dot(piece, key_weight, preferred_element_type=jnp.float32).astype(jnp.bfloat16)
    values_part = jnp.dot(piece, value_weight, preferred_element_type=jnp.float32).astype(
        jnp.bfloat16
    )
    projected = jnp.concatenate([keys_part, values_part], axis=1)
    text_keys = projected[:, :local_width]
    text_values = projected[:, local_width:]
    total_text = projected.shape[0]
    arrival = jnp.arange(total_text, dtype=jnp.int32)
    owners = arrival // text_shard
    matches = owners[:, None] == jnp.arange(group_size, dtype=jnp.int32)[None, :]
    blocks_held = jnp.sum(jnp.where(matches, text_block[None, :], 0), axis=1)
    key_valid = blocks_held * text_shard + arrival % text_shard < text_length[0]
    head_query, head_key, head_value = (
        lax.all_to_all(video_query, "seq", split_axis=1, concat_axis=0, tiled=True),
        lax.all_to_all(video_key, "seq", split_axis=1, concat_axis=0, tiled=True),
        lax.all_to_all(video_value, "seq", split_axis=1, concat_axis=0, tiled=True),
    )
    self_heads = attend(head_query, head_key, head_value, None)
    self_out = lax.all_to_all(self_heads, "seq", split_axis=0, concat_axis=1, tiled=True)
    all_keys, all_values = (
        lax.all_gather(text_keys, "seq", axis=1, tiled=True),
        lax.all_gather(text_values, "seq", axis=1, tiled=True),
    )
    cross_out = attend(cross_query, all_keys, all_values, key_valid)
    return (self_out, cross_out)


def solution(mesh):
    return jax.shard_map(
        body,
        mesh=mesh,
        in_specs=(
            P(("clip", "seq"), None),
            P(("clip", "seq"), None),
            P(("clip", "seq"), None),
            P(("clip", "seq"), None),
            P(("clip", "seq"), None),
            P("clip"),
            P("clip"),
            P(None, "seq"),
            P(None, "seq"),
        ),
        out_specs=(P(("clip", "seq"), None), P(("clip", "seq"), None)),
        check_vma=False,
    )
```

profile of v0, /device:TPU:2, one launch (start us, length us, event | category | flops | bytes accessed | tf_op | source)
XLA Modules:
  0.0 442.1 jit_solution(319796284348654734)
XLA Ops:
  7.2 0.7 all-gather.4.cloned.1.call-update
  8.0 106.8 %all-gather.4.cloned.1.call-done = bf16[512,4096]{1,0:T(8,128)(2,1)} async-done(((bf16[32,4096]{1,0:T(8,128)(2,1)}), bf16[512,4096]{1,0:T(8,128)(2,1)}) %all-gather.4.cloned.1.call-update) | async-done | bytes 4194320 | tf_op jit(solution)/shard_map/all_gather | solution.py:53
  114.8 4.1 convolution_convert_fusion
  119.0 1.3 copy.59
  120.3 4.4 all-to-all-start.1
  124.7 1.3 copy.61
  126.0 46.8 %all-to-all-done.1 = bf16[128,16,256]{0,2,1:T(8,128)(2,1)S(1)} async-done(((bf16[128,16,256]{0,2,1:T(8,128)(2,1)}), bf16[128,16,256]{0,2,1:T(8,128)(2,1)S(1)}, u32[]{:S(2)}, u32[]{:S(2)}) %all-to-all-start.1) | async-done | bytes 1048608 | tf_op jit(solution)/shard_map/all_to_all | solution.py:69
  172.8 4.2 all-to-all-start.2
  177.0 1.1 copy.103
  178.1 49.1 %all-to-all-done.2 = bf16[128,16,256]{0,2,1:T(8,128)(2,1)S(1)} async-done(((bf16[128,16,256]{0,2,1:T(8,128)(2,1)}), bf16[128,16,256]{0,2,1:T(8,128)(2,1)S(1)}, u32[]{:S(2)}, u32[]{:S(2)}) %all-to-all-start.2) | async-done | bytes 1048608 | tf_op jit(solution)/shard_map/all_to_all | solution.py:70
  227.2 5.0 %all-to-all-start = ((bf16[128,16,256]{2,0,1:T(8,128)(2,1)}), bf16[128,16,256]{2,0,1:T(8,128)(2,1)S(1)}, u32[]{:S(2)}, u32[]{:S(2)}) async-start(bf16[128,16,256]{2,0,1:T(8,128)(2,1)} %bitcast.68), calls=%async_computation | async-start | bytes 2097152 | tf_op jit(solution)/shard_map/all_to_all | solution.py:68
  232.3 1.6 copy.60
  233.9 1.5 reshape.75
  235.4 1.3 copy.64
  236.7 0.7 copy.62
  237.4 0.5 reshape.76
  237.9 1.3 copy.65
  239.2 37.9 %all-to-all-done = bf16[128,16,256]{2,0,1:T(8,128)(2,1)S(1)} async-done(((bf16[128,16,256]{2,0,1:T(8,128)(2,1)}), bf16[128,16,256]{2,0,1:T(8,128)(2,1)S(1)}, u32[]{:S(2)}, u32[]{:S(2)}) %all-to-all-start) | async-done | bytes 1048608 | tf_op jit(solution)/shard_map/all_to_all | solution.py:68
  277.2 0.3 reshape.74
  277.5 4.9 %convolution_convert_fusion.1 = bf16[512,256]{1,0:T(8,128)(2,1)} fusion(bf16[512,4096]{1,0:T(8,128)(2,1)} %all-gather.4.cloned.1.call-done, bf16[4096,256]{1,0:T(8,128)(2,1)} %param.19), kind=kOutput, calls=%fused_computation.31 | convolution fusion | flops 1073872896 | bytes 6553600 | tf_op jit(solution)/shard_map/dot_general | solution.py:55
  282.4 44.6 %while.2 = (s32[]{:T(128)}, bf16[4,512,2,128]{3,2,1,0:T(2,128)(2,1)}, bf16[4,512,2,128]{3,2,1,0:T(2,128)(2,1)S(1)}, bf16[2048,2,128]{2,0,1:T(8,128)(2,1)S(1)}, bf16[2048,2,128]{2,0,1:T(8,128)(2,1)}, /*index=5*/s32[]{:T(128)}) while((s32[]{:T(128)}, bf16[4,512,2,128]{3,2,1,0:T(2,128)(2,1)}, bf16[4,512,2,128]{3,2,1,0:T(2,128)(2,1)S(1)}, ...), condition=%wide.region_3.4_spmd, body=%wide.region_0.3_spmd.sunk | while | flops 1084360704 | bytes 20456008 | solution.py:35
  282.4 0.2 constant_dynamic-slice_fusion.2
  282.6 5.0 %fusion.56 = (f32[2,512]{1,0:T(2,128)S(1)}, f32[2,512,2048]{2,1,0:T(8,128)}) fusion(bf16[2048,2,128]{2,0,1:T(8,128)(2,1)S(1)} %get-tuple-element.142, bf16[1,512,2,128]{3,2,1,0:T(2,128)(2,1)S(1)} %constant_dynamic-slice_fusion.2), kind=kOutput, calls=%fused_computation.52.clone.1 | convolution fusion | flops 543164416 | bytes 9703424 | tf_op jit(solution)/shard_map/while/body/eval_jaxpr/sub | solution.py:29
  287.6 4.9 %fusion.57 = bf16[1,512,2,128]{3,1,2,0:T(8,128)(2,1)S(1)} fusion(bf16[2048,2,128]{2,0,1:T(8,128)(2,1)} %get-tuple-element.143, f32[2,512,2048]{2,1,0:T(8,128)} %get-tuple-element.125, f32[2,512]{1,0:T(2,128)S(1)} %get-tuple-element.126), kind=kOutput, calls=%fused_computation.8.clone.1 | convolution fusion | flops 541196288 | bytes 9703424 | tf_op jit(solution)/shard_map/while/body/eval_jaxpr/hqk,khd->qhd/dot_general | solution.py:31
  292.5 1.0 copy_dynamic-update-slice_fusion.2
  293.5 0.2 constant_dynamic-slice_fusion.2
  293.7 5.0 %fusion.56 = (f32[2,512]{1,0:T(2,128)S(1)}, f32[2,512,2048]{2,1,0:T(8,128)}) fusion(bf16[2048,2,128]{2,0,1:T(8,128)(2,1)S(1)} %get-tuple-element.142, bf16[1,512,2,128]{3,2,1,0:T(2,128)(2,1)S(1)} %constant_dynamic-slice_fusion.2), kind=kOutput, calls=%fused_computation.52.clone.1 | convolution fusion | flops 543164416 | bytes 9703424 | tf_op jit(solution)/shard_map/while/body/eval_jaxpr/sub | solution.py:29
  298.7 5.0 %fusion.57 = bf16[1,512,2,128]{3,1,2,0:T(8,128)(2,1)S(1)} fusion(bf16[2048,2,128]{2,0,1:T(8,128)(2,1)} %get-tuple-element.143, f32[2,512,2048]{2,1,0:T(8,128)} %get-tuple-element.125, f32[2,512]{1,0:T(2,128)S(1)} %get-tuple-element.126), kind=kOutput, calls=%fused_computation.8.clone.1 | convolution fusion | flops 541196288 | bytes 9703424 | tf_op jit(solution)/shard_map/while/body/eval_jaxpr/hqk,khd->qhd/dot_general | solution.py:31
  303.7 1.0 copy_dynamic-update-slice_fusion.2
  304.7 0.2 constant_dynamic-slice_fusion.2
  304.9 5.0 %fusion.56 = (f32[2,512]{1,0:T(2,128)S(1)}, f32[2,512,2048]{2,1,0:T(8,128)}) fusion(bf16[2048,2,128]{2,0,1:T(8,128)(2,1)S(1)} %get-tuple-element.142, bf16[1,512,2,128]{3,2,1,0:T(2,128)(2,1)S(1)} %constant_dynamic-slice_fusion.2), kind=kOutput, calls=%fused_computation.52.clone.1 | convolution fusion | flops 543164416 | bytes 9703424 | tf_op jit(solution)/shard_map/while/body/eval_jaxpr/sub | solution.py:29
  309.9 4.9 %fusion.57 = bf16[1,512,2,128]{3,1,2,0:T(8,128)(2,1)S(1)} fusion(bf16[2048,2,128]{2,0,1:T(8,128)(2,1)} %get-tuple-element.143, f32[2,512,2048]{2,1,0:T(8,128)} %get-tuple-element.125, f32[2,512]{1,0:T(2,128)S(1)} %get-tuple-element.126), kind=kOutput, calls=%fused_computation.8.clone.1 | convolution fusion | flops 541196288 | bytes 9703424 | tf_op jit(solution)/shard_map/while/body/eval_jaxpr/hqk,khd->qhd/dot_general | solution.py:31
  314.8 1.0 copy_dynamic-update-slice_fusion.2
  315.8 0.2 constant_dynamic-slice_fusion.2
  316.0 5.0 %fusion.56 = (f32[2,512]{1,0:T(2,128)S(1)}, f32[2,512,2048]{2,1,0:T(8,128)}) fusion(bf16[2048,2,128]{2,0,1:T(8,128)(2,1)S(1)} %get-tuple-element.142, bf16[1,512,2,128]{3,2,1,0:T(2,128)(2,1)S(1)} %constant_dynamic-slice_fusion.2), kind=kOutput, calls=%fused_computation.52.clone.1 | convolution fusion | flops 543164416 | bytes 9703424 | tf_op jit(solution)/shard_map/while/body/eval_jaxpr/sub | solution.py:29
  321.0 5.0 %fusion.57 = bf16[1,512,2,128]{3,1,2,0:T(8,128)(2,1)S(1)} fusion(bf16[2048,2,128]{2,0,1:T(8,128)(2,1)} %get-tuple-element.143, f32[2,512,2048]{2,1,0:T(8,128)} %get-tuple-element.125, f32[2,512]{1,0:T(2,128)S(1)} %get-tuple-element.126), kind=kOutput, calls=%fused_computation.8.clone.1 | convolution fusion | flops 541196288 | bytes 9703424 | tf_op jit(solution)/shard_map/while/body/eval_jaxpr/hqk,khd->qhd/dot_general | solution.py:31
  326.0 1.0 copy_dynamic-update-slice_fusion.2
  327.0 2.6 all_to_all.59
  329.6 4.3 all-to-all-start.3
  334.7 48.0 %all-to-all-done.3 = bf16[16,128,256]{2,1,0:T(8,128)(2,1)S(1)} async-done(((bf16[16,128,256]{2,1,0:T(8,128)(2,1)}), bf16[16,128,256]{2,1,0:T(8,128)(2,1)S(1)}, u32[]{:S(2)}, u32[]{:S(2)}) %all-to-all-start.3) | async-done | bytes 1048608 | tf_op jit(solution)/shard_map/all_to_all | solution.py:73
  382.6 0.7 copy.67
  383.3 1.3 copy.72
  384.6 3.4 fusion.17
  388.1 4.7 %fusion.39 = (f32[32,128]{1,0:T(8,128)S(1)}, f32[32,128,512]{1,2,0:T(8,128)}) fusion(f32[32,512,128]{2,1,0:T(8,128)S(1)} %fusion.17, pred[512]{0:T(512)(128)(4,1)S(1)} %fusion.32), kind=kOutput, calls=%fused_computation.53 | output fusion | flops 12583423 | bytes 16794112 | tf_op jit(solution)/shard_map/while/body/eval_jaxpr/sub | solution.py:29
  392.8 28.9 %all-gather.6.cloned.1.call-done = bf16[512,4096]{1,0:T(8,128)(2,1)} async-done(((bf16[512,256]{1,0:T(8,128)(2,1)}), bf16[512,4096]{1,0:T(8,128)(2,1)}) %all-gather.6.cloned.1.call-update) | async-done | bytes 4194320 | tf_op jit(solution)/shard_map/all_gather | solution.py:76
  421.7 6.5 %copy.75 = bf16[512,4096]{0,1:T(8,128)(2,1)} copy(bf16[512,4096]{1,0:T(8,128)(2,1)} %all-gather.6.cloned.1.call-done) | data formatting | bytes 8388608 | tf_op jit(solution)/shard_map/reshape | solution.py:18
  428.2 6.0 %fusion.24 = bf16[32,128,128]{2,1,0:T(8,128)(2,1)S(1)} fusion(bf16[512,32,128]{0,2,1:T(8,128)(2,1)} %bitcast.78, f32[32,128,512]{1,2,0:T(8,128)} %get-tuple-element.91, f32[32,128]{1,0:T(8,128)S(1)} %get-tuple-element.90), kind=kOutput, calls=%fused_computation.29 | convolution fusion | flops 541589504 | bytes 13647872 | tf_op jit(solution)/shard_map/while/body/eval_jaxpr/hqk,khd->qhd/dot_general | solution.py:31
  434.2 1.3 copy.73
  (26 shorter events, 0.3 us)
Async XLA Ops:
  7.2 107.6 %copy-start = (bf16[4096,256]{1,0:T(8,128)(2,1)S(1)}, bf16[4096,256]{1,0:T(8,128)(2,1)}, u32[]{:S(2)}) copy-start(bf16[4096,256]{1,0:T(8,128)(2,1)} %param.18) | copy-start | bytes 6291460
  7.2 111.8 %copy-start.2 = (bf16[128,4096]{1,0:T(8,128)(2,1)S(1)}, bf16[128,4096]{1,0:T(8,128)(2,1)}, u32[]{:S(2)}) copy-start(bf16[128,4096]{1,0:T(8,128)(2,1)} %param.12) | copy-start | bytes 3145732
  7.2 107.6 %all-gather.4.cloned.1.call-start = ((), (), s32[]{:S(2)}) async-start(), calls=%async_computation.4 | async-start | bytes 4456448 | tf_op jit(solution)/shard_map/all_gather | solution.py:53
  7.9 376.7 %all-gather.8.cloned.1.call-start = ((), (), s32[]{:S(2)}) async-start(), calls=%async_computation.6 | async-start | bytes 4456448 | tf_op jit(solution)/shard_map/all_gather | solution.py:75
  119.0 5.7 %copy-start.3 = (bf16[128,4096]{1,0:T(8,128)(2,1)S(1)}, bf16[128,4096]{1,0:T(8,128)(2,1)}, u32[]{:S(2)}) copy-start(bf16[128,4096]{1,0:T(8,128)(2,1)} %param.13) | copy-start | bytes 3145732
  120.3 56.7 %copy-start.4 = (bf16[128,4096]{1,0:T(8,128)(2,1)S(1)}, bf16[128,4096]{1,0:T(8,128)(2,1)}, u32[]{:S(2)}) copy-start(bf16[128,4096]{1,0:T(8,128)(2,1)} %param.11) | copy-start | bytes 3145732
  120.3 52.5 %all-to-all-start.1 = ((bf16[128,16,256]{0,2,1:T(8,128)(2,1)}), bf16[128,16,256]{0,2,1:T(8,128)(2,1)S(1)}, u32[]{:S(2)}, u32[]{:S(2)}) async-start(bf16[128,16,256]{0,2,1:T(8,128)(2,1)} %bitcast.4), calls=%async_computation.1 | async-start | bytes 2097152 | tf_op jit(solution)/shard_map/all_to_all | solution.py:69
  172.8 54.4 %all-to-all-start.2 = ((bf16[128,16,256]{0,2,1:T(8,128)(2,1)}), bf16[128,16,256]{0,2,1:T(8,128)(2,1)S(1)}, u32[]{:S(2)}, u32[]{:S(2)}) async-start(bf16[128,16,256]{0,2,1:T(8,128)(2,1)} %bitcast.6), calls=%async_computation.2 | async-start | bytes 2097152 | tf_op jit(solution)/shard_map/all_to_all | solution.py:70
  227.2 50.0 %all-to-all-start = ((bf16[128,16,256]{2,0,1:T(8,128)(2,1)}), bf16[128,16,256]{2,0,1:T(8,128)(2,1)S(1)}, u32[]{:S(2)}, u32[]{:S(2)}) async-start(bf16[128,16,256]{2,0,1:T(8,128)(2,1)} %bitcast.68), calls=%async_computation | async-start | bytes 2097152 | tf_op jit(solution)/shard_map/all_to_all | solution.py:68
  232.2 189.5 %all-gather.6.cloned.1.call-start = ((), (), s32[]{:S(2)}) async-start(), calls=%async_computation.5 | async-start | bytes 4456448 | tf_op jit(solution)/shard_map/all_gather | solution.py:76
  277.5 4.9 %copy-start.5 = (bf16[2048,2,128]{2,0,1:T(8,128)(2,1)S(1)}, bf16[2048,2,128]{2,0,1:T(8,128)(2,1)}, u32[]{:S(2)}) copy-start(bf16[2048,2,128]{2,0,1:T(8,128)(2,1)} %copy.64) | copy-start | bytes 3145732
  327.0 7.6 %copy-start.7 = (s32[16]{0:T(128)S(1)}, s32[16]{0:T(128)}, u32[]{:S(2)}) copy-start(s32[16]{0:T(128)} %param.16) | copy-start | bytes 196
  327.0 57.7 %copy-start.6 = (bf16[128,4096]{1,0:T(8,128)(2,1)S(1)}, bf16[128,4096]{1,0:T(8,128)(2,1)}, u32[]{:S(2)}) copy-start(bf16[128,4096]{1,0:T(8,128)(2,1)} %param.14) | copy-start | bytes 3145732
  329.6 53.1 %all-to-all-start.3 = ((bf16[16,128,256]{2,1,0:T(8,128)(2,1)}), bf16[16,128,256]{2,1,0:T(8,128)(2,1)S(1)}, u32[]{:S(2)}, u32[]{:S(2)}) async-start(bf16[16,128,256]{2,1,0:T(8,128)(2,1)} %all_to_all.59), calls=%async_computation.3 | async-start | bytes 2097152 | tf_op jit(solution)/shard_map/all_to_all | solution.py:73
  428.2 7.4 %copy-start.1 = (bf16[4096,256]{1,0:T(8,128)(2,1)S(1)}, bf16[4096,256]{1,0:T(8,128)(2,1)}, u32[]{:S(2)}) copy-start(bf16[4096,256]{1,0:T(8,128)(2,1)} %param.18) | copy-start | bytes 6291460
Sparse Core Ops, SparseCore 0:
  9.8 104.9 all-gather.3
  119.1 166.5 all-gather.7
  287.4 134.2 all-gather.5
where the time goes:
time: 444 us; the launch traced here: 442 us
  waiting for transfers between devices  318 us (72%)
  matrix products  58.4 us (13%)
  local copies, waits for them, and re-layouts  27.9 us (6%)
  starting transfers between devices  18 us (4%)
  between operations  14.6 us (3%)
  other arithmetic  4.85 us (1%)
    all_gather x1, waiting for transfers between devices, body(): piece = lax.all_gather(text_rows, 'seq', axis=0, tiled=True)  107 us
    all_to_all x1, waiting for transfers between devices, body(): lax.all_to_all(video_value, 'seq', split_axis=1, concat_axis=0, tiled=True)  49.1 us
    all_to_all x1, waiting for transfers between devices, body(): lax.all_to_all(self_heads, 'seq', split_axis=0, concat_axis=1, tiled=True)  48 us
    all_to_all x1, waiting for transfers between devices, body(): lax.all_to_all(video_key, 'seq', split_axis=1, concat_axis=0, tiled=True)  46.8 us
    all_to_all x1, waiting for transfers between devices, body(): lax.all_to_all(video_query, 'seq', split_axis=1, concat_axis=0, tiled=True)  37.9 us
    all_gather x1, waiting for transfers between devices, body(): lax.all_gather(text_values, 'seq', axis=1, tiled=True)  28.9 us
    dot_general x5, matrix products, one_block(): jnp.einsum('hqk,khd->qhd', weights, value_heads, preferred_element_type=j...  25.8 us
    sub x4, matrix products, one_block(): exponent = jnp.exp(scores - highest)  20.1 us
  transfers between devices with their start and end apart: 7, of which 6 were waited for; matrix products, arithmetic and copies ran while one was open for 16% of the time, Pallas kernels for 0%

commit v1 on v0

v1 whole, which is shorter than its diff:
```python
import functools
import math

import jax
import jax.numpy as jnp
from jax import lax
from jax.experimental import pallas as pl
from jax.experimental.pallas import tpu as pltpu
from jax.sharding import PartitionSpec as P

HEAD_DIM = 128
EXP2_SCALE = HEAD_DIM**-0.5 * math.log2(math.e)


def attend_kernel(*refs, heads, sub_blocks, masked):
    if masked:
        query_ref, key_ref, value_ref, bias_ref, out_ref, wide_ref = refs
    else:
        query_ref, key_ref, value_ref, out_ref, wide_ref = refs
    width = query_ref.shape[-1]
    key_count = math.prod(key_ref.shape[:-1])

    @pl.when(pl.program_id(0) == 0)
    def _():
        values = value_ref[...].reshape(key_count, width)
        for head in range(heads):
            wide_ref[head, :, :HEAD_DIM] = values[:, head * HEAD_DIM : (head + 1) * HEAD_DIM]
            wide_ref[head, :, HEAD_DIM:] = jnp.ones((key_count, HEAD_DIM), jnp.bfloat16)

    queries = query_ref[...].reshape(-1, width)
    keys = key_ref[...].reshape(key_count, width)
    rows = queries.shape[0] // sub_blocks
    for block in range(sub_blocks):
        for head in range(heads):
            columns = slice(head * HEAD_DIM, (head + 1) * HEAD_DIM)
            scores = lax.dot_general(
                queries[block * rows : (block + 1) * rows, columns],
                keys[:, columns],
                (((1,), (1,)), ((), ())),
                preferred_element_type=jnp.float32,
            )
            if masked:
                scores = scores + bias_ref[...]
            highest = jnp.max(scores, axis=1, keepdims=True)
            weights = jnp.exp2((scores - highest) * EXP2_SCALE).astype(jnp.bfloat16)
            both = jnp.dot(weights, wide_ref[head], preferred_element_type=jnp.float32)
            result = (both[:, :HEAD_DIM] / both[:, HEAD_DIM:]).astype(jnp.bfloat16)
            per = out_ref.shape[1]
            for piece in range(rows // per):
                out_ref[block * (rows // per) + piece, :, columns] = result[
                    piece * per : (piece + 1) * per
                ]


def attend(arrays, specs, bias, shape, key_count, block_pieces, sub_blocks):
    pieces, per, width = shape
    heads = width // HEAD_DIM
    in_specs = list(specs)
    operands = list(arrays)
    if bias is not None:
        operands.append(bias)
        in_specs.append(pl.BlockSpec(bias.shape, lambda i: (0, 0)))
    queries = pieces * per
    return pl.pallas_call(
        functools.partial(
            attend_kernel, heads=heads, sub_blocks=sub_blocks, masked=bias is not None
        ),
        grid=(pieces // block_pieces,),
        in_specs=in_specs,
        out_specs=pl.BlockSpec((block_pieces, per, width), lambda i: (i, 0, 0)),
        out_shape=jax.ShapeDtypeStruct(shape, jnp.bfloat16),
        scratch_shapes=[pltpu.VMEM((heads, key_count, 2 * HEAD_DIM), jnp.bfloat16)],
        compiler_params=pltpu.CompilerParams(vmem_limit_bytes=48 * 1024 * 1024),
        cost_estimate=pl.CostEstimate(
            flops=4 * queries * key_count * width,
            bytes_accessed=2 * width * 2 * (queries + key_count),
            transcendentals=queries * key_count * heads,
        ),
    )(*operands)


def body(
    video_query,
    video_key,
    video_value,
    cross_query,
    text_rows,
    text_block,
    text_length,
    key_weight,
    value_weight,
):
    group_size = lax.axis_size("seq")
    tokens, inner = video_query.shape
    width = inner // group_size
    text_shard = text_rows.shape[0]
    total_text = group_size * text_shard

    piece = lax.all_gather(text_rows, "seq", axis=0, tiled=True)
    stacked = jnp.stack(
        [
            a.reshape(tokens, group_size, width).transpose(1, 0, 2)
            for a in (video_query, video_key, video_value, cross_query)
        ],
        axis=1,
    )
    by_head = lax.all_to_all(stacked, "seq", split_axis=0, concat_axis=0, tiled=True)

    block_pieces = 8
    self_heads = attend(
        (by_head, by_head, by_head),
        (
            pl.BlockSpec((block_pieces, None, tokens, width), lambda i: (i, 0, 0, 0)),
            pl.BlockSpec((group_size, None, tokens, width), lambda i: (0, 1, 0, 0)),
            pl.BlockSpec((group_size, None, tokens, width), lambda i: (0, 2, 0, 0)),
        ),
        None,
        (group_size, tokens, width),
        group_size * tokens,
        block_pieces,
        4,
    )
    self_out = lax.all_to_all(self_heads, "seq", split_axis=0, concat_axis=0, tiled=True)

    text_keys = jnp.dot(piece, key_weight, preferred_element_type=jnp.float32).astype(jnp.bfloat16)
    text_values = jnp.dot(piece, value_weight, preferred_element_type=jnp.float32).astype(
        jnp.bfloat16
    )
    position = (
        text_block[:, None] * text_shard + jnp.arange(text_shard, dtype=jnp.int32)[None, :]
    ).reshape(1, total_text)
    bias = jnp.where(position < text_length[0], 0.0, -jnp.inf).astype(jnp.float32)
    cross_heads = attend(
        (by_head, text_keys, text_values),
        (
            pl.BlockSpec((block_pieces, None, tokens, width), lambda i: (i, 3, 0, 0)),
            pl.BlockSpec((total_text, width), lambda i: (0, 0)),
            pl.BlockSpec((total_text, width), lambda i: (0, 0)),
        ),
        bias,
        (group_size, tokens, width),
        total_text,
        block_pieces,
        4,
    )
    cross_out = lax.all_to_all(cross_heads, "seq", split_axis=0, concat_axis=0, tiled=True)
    return tuple(
        a.transpose(1, 0, 2).reshape(tokens, inner) for a in (self_out, cross_out)
    )


def solution(mesh):
    rows = P(("clip", "seq"), None)
    return jax.shard_map(
        body,
        mesh=mesh,
        in_specs=(
            rows,
            rows,
            rows,
            rows,
            rows,
            P("clip"),
            P("clip"),
            P(None, "seq"),
            P(None, "seq"),
        ),
        out_specs=(rows, rows),
        check_vma=False,
    )
```

time: 444 us -> 282 us (0.64)
  waiting for transfers between devices: 318 us -> 203 us
  matrix products: 58.4 us -> 4.83 us
  Pallas kernels: 0 us -> 18.9 us
  local copies, waits for them, and re-layouts: 27.9 us -> 18.9 us
    all_to_all x4 -> x3, waiting for transfers between devices: 182 us -> 40.1 us  [the longest x1 23.5 us: body(): lax.all_to_all(self_heads, 'seq', split_axis=0, concat_axis=0, tiled=True)]
    all_gather x1, waiting for transfers between devices: 107 us -> 162 us  [body(): piece = lax.all_gather(text_rows, 'seq', axis=0, tiled=True)]
    dot_general x6 -> x0, matrix products: 29.2 us -> none  [the longest x5 25.8 us: one_block(): jnp.einsum('hqk,khd->qhd', weights, value_heads, preferred_element_type=j...]
    all_gather x2 -> x0, waiting for transfers between devices: 28.9 us -> none  [the longest x1 28.9 us: body(): lax.all_gather(text_values, 'seq', axis=1, tiled=True)]
    sub x4 -> x0, matrix products: 20.1 us -> none  [one_block(): exponent = jnp.exp(scores - highest)]
    pallas_call x0 -> x2, Pallas kernels: none -> 18.9 us  [attend(): pl.pallas_call(functools.partial(attend_kernel, heads=heads, sub_blocks=s...]
    all_to_all x5 -> x0, local copies, waits for them, and re-layouts: 6.65 us -> none  [the longest x2 3.26 us: body(): lax.all_to_all(self_heads, 'seq', split_axis=0, concat_axis=1, tiled=True)]
    unnamed x20 -> x14, local copies, waits for them, and re-layouts: 5.28 us -> 10.6 us
  transfers between devices with their start and end apart: 7 -> 4, of which waited for: 6 -> 4; matrix products, arithmetic and copies ran while one was open for 16% -> 9% of each run, Pallas kernels for 0% -> 5%
where the time goes in v1:
time: 282 us; the launch traced here: 281 us
  waiting for transfers between devices  203 us (72%)
  local copies, waits for them, and re-layouts  18.9 us (7%)
  Pallas kernels  18.9 us (7%)
  starting transfers between devices  17.5 us (6%)
  between operations  14.8 us (5%)
  matrix products  4.83 us (2%)
  other arithmetic  3.82 us (1%)
    all_gather x1, waiting for transfers between devices, body(): piece = lax.all_gather(text_rows, 'seq', axis=0, tiled=True)  162 us
    all_to_all x1, waiting for transfers between devices, body(): lax.all_to_all(self_heads, 'seq', split_axis=0, concat_axis=0, tiled=True)  23.5 us
    pallas_call x2, Pallas kernels, attend(): pl.pallas_call(functools.partial(attend_kernel, heads=heads, sub_blocks=s...  18.9 us
    all_to_all x1, waiting for transfers between devices, body(): lax.all_to_all(cross_heads, 'seq', split_axis=0, concat_axis=0, tiled=True)  13.7 us
    unnamed x14, local copies, waits for them, and re-layouts  10.6 us
    all_to_all x1, starting transfers between devices, body(): lax.all_to_all(stacked, 'seq', split_axis=0, concat_axis=0, tiled=True)  8.88 us
  transfers between devices with their start and end apart: 4, of which 4 were waited for; matrix products, arithmetic and copies ran while one was open for 9% of the time, Pallas kernels for 5%

profile of v1, /device:TPU:2, one launch (start us, length us, event | category | flops | bytes accessed | tf_op | source)
XLA Modules:
  0.0 281.4 jit_solution(7206072396309042237)
XLA Ops:
  7.2 0.0 copy-start
  7.2 0.0 all-gather.2.cloned.1.call-start
  7.2 0.7 all-gather.2.cloned.1.call-update
  7.9 1.6 copy.17
  9.5 1.3 copy.18
  10.9 1.6 copy.11
  12.5 1.3 copy.12
  13.8 1.6 copy.13
  15.4 1.4 copy.14
  16.8 1.6 copy.15
  18.4 1.3 copy.16
  19.7 3.7 %pad_maximum_fusion = bf16[16,4,128,256]{3,2,1,0:T(8,128)(2,1)} fusion(bf16[16,1,128,256]{3,2,1,0:T(8,128)(2,1)} %bitcast.33, bf16[16,1,128,256]{3,2,1,0:T(8,128)(2,1)} %bitcast.36, bf16[16,1,128,256]{3,2,1,0:T(8,128)(2,1)} %bitcast.35, bf16[16,1,128,256]{3,2,1,0:T(8,128)(2,1)} %bitcast.34), kind=kLoop, calls=%fused_computation | loop fusion | flops 6291456 | bytes 8388608 | tf_op jit(solution)/shard_map/stack | solution.py:100
  23.5 0.0 copy-start.3
  23.5 8.9 %all-to-all-start = ((bf16[16,4,128,256]{3,2,1,0:T(8,128)(2,1)}), bf16[16,4,128,256]{3,2,1,0:T(8,128)(2,1)}, u32[]{:S(2)}, u32[]{:S(2)}) async-start(bf16[16,4,128,256]{3,2,1,0:T(8,128)(2,1)} %pad_maximum_fusion), calls=%async_computation | async-start | bytes 8388608 | tf_op jit(solution)/shard_map/all_to_all | solution.py:107
  33.0 0.0 copy-done.3
  33.0 0.1 fusion
  33.1 0.1 select_n.7.refs_3_
  33.2 161.8 %all-gather.2.cloned.1.call-done = bf16[512,4096]{1,0:T(8,128)(2,1)} async-done(((bf16[32,4096]{1,0:T(8,128)(2,1)}), bf16[512,4096]{1,0:T(8,128)(2,1)}) %all-gather.2.cloned.1.call-update) | async-done | bytes 4194320 | tf_op jit(solution)/shard_map/all_gather | solution.py:99
  195.0 0.0 copy-done
  195.0 0.0 copy-start.1
  195.0 0.0 copy-start.2
  195.0 3.6 %convolution_convert_fusion.refs_2_ = bf16[512,256]{1,0:T(8,128)(2,1)S(1)} fusion(bf16[512,4096]{1,0:T(8,128)(2,1)} %all-gather.2.cloned.1.call-done, bf16[4096,256]{1,0:T(8,128)(2,1)S(1)} %copy-done), kind=kOutput, calls=%fused_computation.1 | convolution fusion | flops 1073872896 | bytes 6553600 | tf_op jit(solution)/shard_map/dot_general | solution.py:126
  198.6 0.0 copy-done.1
  198.6 0.5 copy-done.2
  199.1 1.2 convolution_convert_fusion.1.refs_1_
  200.4 2.9 %all-to-all-done.refs_0_.refs_1_.refs_2_ = bf16[16,4,128,256]{3,2,1,0:T(8,128)(2,1)} async-done(((bf16[16,4,128,256]{3,2,1,0:T(8,128)(2,1)}), bf16[16,4,128,256]{3,2,1,0:T(8,128)(2,1)}, u32[]{:S(2)}, u32[]{:S(2)}) %all-to-all-start) | async-done | bytes 4194336 | tf_op jit(solution)/shard_map/all_to_all | solution.py:107
  203.3 5.1 %shard_map.105 = bf16[16,128,256]{2,1,0:T(8,128)(2,1)} custom-call(bf16[16,4,128,256]{3,2,1,0:T(8,128)(2,1)} %all-to-all-done.refs_0_.refs_1_.refs_2_, bf16[512,256]{1,0:T(8,128)(2,1)S(1)} %convolution_convert_fusion.1.refs_1_, bf16[512,256]{1,0:T(8,128)(2,1)S(1)} %convolution_convert_fusion.refs_2_, f32[1,512]{1,0:T(1,128)S(1)} %select_n.7.refs_3_), custom_call_target="tpu_custom_call" | custom-call | flops 1073741824 | bytes 2621440 | tf_op jit(solution)/shard_map/pallas_call | solution.py:64
  208.4 4.2 %all-to-all-start.2 = ((bf16[16,128,256]{2,1,0:T(8,128)(2,1)}), bf16[16,128,256]{2,1,0:T(8,128)(2,1)S(1)}, u32[]{:S(2)}, u32[]{:S(2)}) async-start(bf16[16,128,256]{2,1,0:T(8,128)(2,1)} %shard_map.105), calls=%async_computation.2 | async-start | bytes 2097152 | tf_op jit(solution)/shard_map/all_to_all | solution.py:146
  212.6 13.8 %shard_map.104 = bf16[16,128,256]{2,1,0:T(8,128)(2,1)} custom-call(bf16[16,4,128,256]{3,2,1,0:T(8,128)(2,1)} %all-to-all-done.refs_0_.refs_1_.refs_2_, bf16[16,4,128,256]{3,2,1,0:T(8,128)(2,1)} %all-to-all-done.refs_0_.refs_1_.refs_2_, bf16[16,4,128,256]{3,2,1,0:T(8,128)(2,1)} %all-to-all-done.refs_0_.refs_1_.refs_2_), custom_call_target="tpu_custom_call" | custom-call | flops 4294967296 | bytes 4194304 | tf_op jit(solution)/shard_map/pallas_call | solution.py:64
  226.4 13.7 %all-to-all-done.2 = bf16[16,128,256]{2,1,0:T(8,128)(2,1)S(1)} async-done(((bf16[16,128,256]{2,1,0:T(8,128)(2,1)}), bf16[16,128,256]{2,1,0:T(8,128)(2,1)S(1)}, u32[]{:S(2)}, u32[]{:S(2)}) %all-to-all-start.2) | async-done | bytes 1048608 | tf_op jit(solution)/shard_map/all_to_all | solution.py:146
  240.1 4.4 %all-to-all-start.1 = ((bf16[16,128,256]{2,1,0:T(8,128)(2,1)}), bf16[16,128,256]{2,1,0:T(8,128)(2,1)}, u32[]{:S(2)}, u32[]{:S(2)}) async-start(bf16[16,128,256]{2,1,0:T(8,128)(2,1)} %shard_map.104), calls=%async_computation.1 | async-start | bytes 2097152 | tf_op jit(solution)/shard_map/all_to_all | solution.py:123
  244.5 1.3 copy.20
  245.8 2.3 copy.22
  248.1 23.5 %all-to-all-done.1 = bf16[16,128,256]{2,1,0:T(8,128)(2,1)} async-done(((bf16[16,128,256]{2,1,0:T(8,128)(2,1)}), bf16[16,128,256]{2,1,0:T(8,128)(2,1)}, u32[]{:S(2)}, u32[]{:S(2)}) %all-to-all-start.1) | async-done | bytes 1048608 | tf_op jit(solution)/shard_map/all_to_all | solution.py:123
  271.6 1.6 copy.19
  273.2 1.3 copy.21
  (1 shorter events, 0.0 us)
Async XLA Ops:
  7.2 187.8 %copy-start = (bf16[4096,256]{1,0:T(8,128)(2,1)S(1)}, bf16[4096,256]{1,0:T(8,128)(2,1)}, u32[]{:S(2)}) copy-start(bf16[4096,256]{1,0:T(8,128)(2,1)} %param.17) | copy-start | bytes 6291460
  7.2 187.8 %all-gather.2.cloned.1.call-start = ((), (), s32[]{:S(2)}) async-start(), calls=%async_computation.3 | async-start | bytes 4456448 | tf_op jit(solution)/shard_map/all_gather | solution.py:99
  23.5 9.5 %copy-start.3 = (s32[16]{0:T(128)S(1)}, s32[16]{0:T(128)}, u32[]{:S(2)}) copy-start(s32[16]{0:T(128)} %param.14) | copy-start | bytes 196
  23.5 179.9 %all-to-all-start = ((bf16[16,4,128,256]{3,2,1,0:T(8,128)(2,1)}), bf16[16,4,128,256]{3,2,1,0:T(8,128)(2,1)}, u32[]{:S(2)}, u32[]{:S(2)}) async-start(bf16[16,4,128,256]{3,2,1,0:T(8,128)(2,1)} %pad_maximum_fusion), calls=%async_computation | async-start | bytes 8388608 | tf_op jit(solution)/shard_map/all_to_all | solution.py:107
  195.0 3.6 %copy-start.1 = (bf16[512,4096]{1,0:T(8,128)(2,1)S(1)}, bf16[512,4096]{1,0:T(8,128)(2,1)}, u32[]{:S(2)}) copy-start(bf16[512,4096]{1,0:T(8,128)(2,1)} %all-gather.2.cloned.1.call-done) | copy-start | bytes 12582916
  195.0 4.1 %copy-start.2 = (bf16[4096,256]{1,0:T(8,128)(2,1)S(1)}, bf16[4096,256]{1,0:T(8,128)(2,1)}, u32[]{:S(2)}) copy-start(bf16[4096,256]{1,0:T(8,128)(2,1)} %param.16) | copy-start | bytes 6291460
  208.4 31.7 %all-to-all-start.2 = ((bf16[16,128,256]{2,1,0:T(8,128)(2,1)}), bf16[16,128,256]{2,1,0:T(8,128)(2,1)S(1)}, u32[]{:S(2)}, u32[]{:S(2)}) async-start(bf16[16,128,256]{2,1,0:T(8,128)(2,1)} %shard_map.105), calls=%async_computation.2 | async-start | bytes 2097152 | tf_op jit(solution)/shard_map/all_to_all | solution.py:146
  240.1 31.4 %all-to-all-start.1 = ((bf16[16,128,256]{2,1,0:T(8,128)(2,1)}), bf16[16,128,256]{2,1,0:T(8,128)(2,1)}, u32[]{:S(2)}, u32[]{:S(2)}) async-start(bf16[16,128,256]{2,1,0:T(8,128)(2,1)} %shard_map.104), calls=%async_computation.1 | async-start | bytes 2097152 | tf_op jit(solution)/shard_map/all_to_all | solution.py:123
Sparse Core Ops, SparseCore 0:
  9.8 185.1 all-gather.1

commit v2 on v0

v2 whole, which is shorter than its diff:
```python
import functools
import math

import jax
import jax.numpy as jnp
from jax import lax
from jax.experimental import pallas as pl
from jax.experimental.pallas import tpu as pltpu
from jax.sharding import PartitionSpec as P

HEAD_DIM = 128
EXP2_SCALE = HEAD_DIM**-0.5 * math.log2(math.e)
SIDE = 4
BF16 = jnp.bfloat16
F32 = jnp.float32
MIB = 1024 * 1024


def shift_z(array, step):
    pairs = [(y * SIDE + z, y * SIDE + (z + step) % SIDE) for y in range(SIDE) for z in range(SIDE)]
    return lax.ppermute(array, "seq", pairs)


def shift_y(array, step):
    pairs = [(y * SIDE + z, (y + step) % SIDE * SIDE + z) for y in range(SIDE) for z in range(SIDE)]
    return lax.ppermute(array, "seq", pairs)


def whole(shape):
    return pl.BlockSpec(shape, lambda *_: (0,) * len(shape))


def cut_kernel(*refs, head):
    *in_refs, out_ref = refs
    width = in_refs[0].shape[1] // out_ref.shape[0]
    for piece in range(out_ref.shape[0]):
        start = piece * width + head * HEAD_DIM
        for which, ref in enumerate(in_refs):
            out_ref[piece, which] = ref[:, start : start + HEAD_DIM]


def cut(arrays, head):
    tokens, inner = arrays[0].shape
    shape = (SIDE * SIDE, len(arrays), tokens, HEAD_DIM)
    vmem = pl.BlockSpec(memory_space=pltpu.VMEM)
    return pl.pallas_call(
        functools.partial(cut_kernel, head=head),
        in_specs=[vmem] * len(arrays),
        out_specs=vmem,
        out_shape=jax.ShapeDtypeStruct(shape, BF16),
        compiler_params=pltpu.CompilerParams(vmem_limit_bytes=40 * MIB),
        cost_estimate=pl.CostEstimate(
            flops=0, bytes_accessed=4 * len(arrays) * tokens * inner, transcendentals=0
        ),
    )(*arrays)


def join_kernel(*refs):
    in_refs, out_refs = refs[:-2], refs[-2:]
    heads = len(in_refs)
    for head, ref in enumerate(in_refs):
        for piece in range(ref.shape[0]):
            start = (piece * heads + head) * HEAD_DIM
            for which, out_ref in enumerate(out_refs):
                out_ref[:, start : start + HEAD_DIM] = ref[piece, which]


def join(parts):
    count, outputs, tokens, width = parts[0].shape
    shape = jax.ShapeDtypeStruct((tokens, count * len(parts) * width), BF16)
    vmem = pl.BlockSpec(memory_space=pltpu.VMEM)
    return pl.pallas_call(
        join_kernel,
        in_specs=[vmem] * len(parts),
        out_specs=[vmem] * outputs,
        out_shape=[shape] * outputs,
        compiler_params=pltpu.CompilerParams(vmem_limit_bytes=40 * MIB),
        cost_estimate=pl.CostEstimate(
            flops=0, bytes_accessed=4 * count * outputs * tokens * width * len(parts),
            transcendentals=0,
        ),
    )(*parts)


def head_output(queries, keys, wide_values, bias):
    scores = lax.dot_general(
        queries, keys, (((1,), (1,)), ((), ())), preferred_element_type=F32
    )
    if bias is not None:
        scores = scores + bias
    highest = jnp.max(scores, axis=1, keepdims=True)
    weights = jnp.exp2((scores - highest) * EXP2_SCALE).astype(BF16)
    both = jnp.dot(weights, wide_values, preferred_element_type=F32)
    return (both[:, :HEAD_DIM] / both[:, HEAD_DIM:]).astype(BF16)


def attend_kernel(
    query_ref, key_ref, value_ref, cross_ref, text_ref, bias_ref, out_ref, wide_all, *, head, blocks
):
    count = key_ref.shape[0] * key_ref.shape[1]

    @pl.when(pl.program_id(0) == 0)
    def _():
        wide_all[:, :HEAD_DIM] = value_ref[...].reshape(count, HEAD_DIM)
        wide_all[:, HEAD_DIM:] = jnp.ones((count, HEAD_DIM), BF16)

    pieces, _, tokens, _ = out_ref.shape
    width = text_ref.shape[1] // 2
    keys = key_ref[...].reshape(count, HEAD_DIM)
    text_keys = text_ref[:, head * HEAD_DIM : (head + 1) * HEAD_DIM]
    text_values = text_ref[:, width + head * HEAD_DIM : width + (head + 1) * HEAD_DIM]
    wide_text = jnp.concatenate([text_values, jnp.ones_like(text_values)], axis=1)
    step = pieces // blocks
    for block in range(blocks):
        at = slice(block * step, (block + 1) * step)
        queries = query_ref[at].reshape(step * tokens, HEAD_DIM)
        result = head_output(queries, keys, wide_all[...], None)
        out_ref[at, 0] = result.reshape(step, tokens, HEAD_DIM)
        queries = cross_ref[at].reshape(step * tokens, HEAD_DIM)
        result = head_output(queries, text_keys, wide_text, bias_ref[...])
        out_ref[at, 1] = result.reshape(step, tokens, HEAD_DIM)


def attend(by_head, text, bias, head):
    group, _, tokens, _ = by_head.shape
    count = group * tokens
    step = group // 2
    return pl.pallas_call(
        functools.partial(attend_kernel, head=head, blocks=4),
        grid=(group // step,),
        in_specs=[
            pl.BlockSpec((step, None, tokens, HEAD_DIM), lambda i: (i, 0, 0, 0)),
            pl.BlockSpec((group, None, tokens, HEAD_DIM), lambda i: (0, 1, 0, 0)),
            pl.BlockSpec((group, None, tokens, HEAD_DIM), lambda i: (0, 2, 0, 0)),
            pl.BlockSpec((step, None, tokens, HEAD_DIM), lambda i: (i, 3, 0, 0)),
            pl.BlockSpec(text.shape, lambda i: (0, 0)),
            pl.BlockSpec(bias.shape, lambda i: (0, 0)),
        ],
        out_specs=pl.BlockSpec((step, 2, tokens, HEAD_DIM), lambda i: (i, 0, 0, 0)),
        out_shape=jax.ShapeDtypeStruct((group, 2, tokens, HEAD_DIM), BF16),
        scratch_shapes=[pltpu.VMEM((count, 2 * HEAD_DIM), BF16)],
        compiler_params=pltpu.CompilerParams(vmem_limit_bytes=40 * MIB),
        cost_estimate=pl.CostEstimate(
            flops=8 * count * (count + text.shape[0]) * HEAD_DIM,
            bytes_accessed=12 * count * HEAD_DIM,
            transcendentals=count * (count + text.shape[0]),
        ),
    )(by_head, by_head, by_head, by_head, text, bias)


def project_kernel(*refs):
    *text_refs, key_weight_ref, value_weight_ref, out_ref, total = refs
    rows = text_refs[0].shape[0]
    width = key_weight_ref.shape[1]

    @pl.when(pl.program_id(0) == 0)
    def _():
        total[...] = jnp.zeros_like(total)

    for s, ref in enumerate(text_refs):
        for which, weight_ref in enumerate((key_weight_ref, value_weight_ref)):
            total[s * rows : (s + 1) * rows, which * width : (which + 1) * width] += jnp.dot(
                ref[...], weight_ref[...], preferred_element_type=F32
            )

    @pl.when(pl.program_id(0) == pl.num_programs(0) - 1)
    def _():
        out_ref[...] = total[...].astype(BF16)


def project(texts, key_weight, value_weight):
    rows, depth = texts[0].shape
    width = key_weight.shape[1]
    step = 1024
    shape = (len(texts) * rows, 2 * width)
    return pl.pallas_call(
        project_kernel,
        grid=(depth // step,),
        in_specs=[pl.BlockSpec((rows, step), lambda i: (0, i))] * len(texts)
        + [pl.BlockSpec((step, width), lambda i: (i, 0))] * 2,
        out_specs=pl.BlockSpec(shape, lambda i: (0, 0)),
        out_shape=jax.ShapeDtypeStruct(shape, BF16),
        scratch_shapes=[pltpu.VMEM(shape, F32)],
        compiler_params=pltpu.CompilerParams(vmem_limit_bytes=40 * MIB),
        cost_estimate=pl.CostEstimate(
            flops=2 * shape[0] * shape[1] * depth,
            bytes_accessed=2 * depth * (shape[0] + shape[1]),
            transcendentals=0,
        ),
    )(*texts, key_weight, value_weight)


def after(array, *earlier):
    return lax.optimization_barrier((array, *earlier))[0]


def body(
    video_query,
    video_key,
    video_value,
    cross_query,
    text_rows,
    text_block,
    text_length,
    key_weight,
    value_weight,
):
    index = lax.axis_index("seq")
    y, z = index // SIDE, index % SIDE
    text_shard = text_rows.shape[0]
    steps = range(1, SIDE)

    text_from = [shift_z(text_rows, t) for t in steps]
    text_z = jnp.concatenate([text_rows] + text_from, axis=0)
    texts = [text_z] + [shift_y(text_z, s) for s in steps]
    text_own = project(texts, key_weight, value_weight)

    near = jnp.arange(SIDE, dtype=jnp.int32)
    holder = ((y - near) % SIDE * SIDE)[:, None] + ((z - near) % SIDE)[None, :]
    matches = holder[..., None] == jnp.arange(SIDE * SIDE, dtype=jnp.int32)
    blocks = jnp.sum(jnp.where(matches, text_block, 0), axis=-1)
    position = blocks[..., None] * text_shard + jnp.arange(text_shard, dtype=jnp.int32)
    bias = jnp.where(position < text_length[0], 0.0, -jnp.inf).astype(F32).reshape(1, -1)

    arrays = (video_query, video_key, video_value, cross_query)
    swap = functools.partial(
        lax.all_to_all, axis_name="seq", split_axis=0, concat_axis=0, tiled=True
    )
    first = swap(after(cut(arrays, 0), text_z))
    second = swap(after(cut(arrays, 1), first, *texts[1:]))
    first_heads = attend(first, text_own, bias, 0)
    second_heads = attend(after(second, first_heads), text_own, bias, 1)
    self_out, cross_out = join([swap(first_heads), swap(second_heads)])
    return self_out, cross_out


def solution(mesh):
    rows = P(("clip", "seq"), None)
    return jax.shard_map(
        body,
        mesh=mesh,
        in_specs=(
            rows,
            rows,
            rows,
            rows,
            rows,
            P("clip"),
            P("clip"),
            P(None, "seq"),
            P(None, "seq"),
        ),
        out_specs=(rows, rows),
        check_vma=False,
    )
```

time: 444 us -> 229 us (0.52)
  waiting for transfers between devices: 318 us -> 117 us
  matrix products: 58.4 us -> 0 us
  blocking collectives: 0 us -> 31.1 us
  Pallas kernels: 0 us -> 28.7 us
  starting transfers between devices: 18 us -> 32.1 us
  between operations: 14.6 us -> 1.4 us
  local copies, waits for them, and re-layouts: 27.9 us -> 17 us
  other arithmetic: 4.85 us -> 0.38 us
    all_gather x3 -> x0, waiting for transfers between devices: 136 us -> none  [the longest x1 107 us: body(): piece = lax.all_gather(text_rows, 'seq', axis=0, tiled=True)]
    all_to_all x4 -> x3, waiting for transfers between devices: 182 us -> 48.9 us  [the longest x1 30.3 us: body(): second = swap(after(cut(arrays, 1), first, *texts[1:]))]
    ppermute x0 -> x6, waiting for transfers between devices: none -> 68.6 us  [the longest x3 60.4 us: shift_y(): return lax.ppermute(array, 'seq', pairs)]
    dot_general x8 -> x0, matrix products: 38.3 us -> none  [the longest x5 25.8 us: one_block(): jnp.einsum('hqk,khd->qhd', weights, value_heads, preferred_element_type=j...]
    all_to_all x0 -> x1, blocking collectives: none -> 31.1 us  [body(): self_out, cross_out = join([swap(first_heads), swap(second_heads)])]
    pallas_call x0 -> x6, Pallas kernels: none -> 28.7 us  [the longest x2 19.1 us: attend(): pl.pallas_call(functools.partial(attend_kernel, head=head, blocks=4), gri...]
    sub x4 -> x0, matrix products: 20.1 us -> none  [one_block(): exponent = jnp.exp(scores - highest)]
    ppermute x0 -> x6, starting transfers between devices: none -> 12.3 us  [the longest x3 6.27 us: shift_z(): return lax.ppermute(array, 'seq', pairs)]
  transfers between devices with their start and end apart: 7 -> 9, of which waited for: 6 -> 5; matrix products, arithmetic and copies ran while one was open for 16% -> 1% of each run, Pallas kernels for 0% -> 12%
where the time goes in v2:
time: 229 us; the launch traced here: 228 us
  waiting for transfers between devices  117 us (51%)
  starting transfers between devices  32.1 us (14%)
  blocking collectives  31.1 us (14%)
  Pallas kernels  28.7 us (13%)
  local copies, waits for them, and re-layouts  17 us (7%)
    ppermute x3, waiting for transfers between devices, shift_y(): return lax.ppermute(array, 'seq', pairs)  60.4 us
    all_to_all x1, blocking collectives, body(): self_out, cross_out = join([swap(first_heads), swap(second_heads)])  31.1 us
    all_to_all x1, waiting for transfers between devices, body(): second = swap(after(cut(arrays, 1), first, *texts[1:]))  30.3 us
    pallas_call x2, Pallas kernels, attend(): pl.pallas_call(functools.partial(attend_kernel, head=head, blocks=4), gri...  19.1 us
    all_to_all x1, waiting for transfers between devices, body(): self_out, cross_out = join([swap(first_heads), swap(second_heads)])  18.5 us
    unnamed x43, local copies, waits for them, and re-layouts  16.1 us
    all_to_all x1, starting transfers between devices, body(): first = swap(after(cut(arrays, 0), text_z))  11.1 us
    ppermute x3, waiting for transfers between devices, shift_z(): return lax.ppermute(array, 'seq', pairs)  8.24 us
  transfers between devices with their start and end apart: 9, of which 5 were waited for; matrix products, arithmetic and copies ran while one was open for 1% of the time, Pallas kernels for 12%

profile of v2, /device:TPU:2, one launch (start us, length us, event | category | flops | bytes accessed | tf_op | source)
XLA Modules:
  0.0 228.1 jit_solution(13420742811931988318)
XLA Ops:
  0.6 2.0 collective-permute-start
  2.6 3.3 %collective-permute-start.1 = (bf16[32,4096]{1,0:T(8,128)(2,1)}, bf16[32,4096]{1,0:T(8,128)(2,1)S(1)}, u32[]{:S(2)}, u32[]{:S(2)}) collective-permute-start(bf16[32,4096]{1,0:T(8,128)(2,1)} %param.13), channel_id=1, source_target_pairs={{0,2},{1,3},{2,0},{3,1},{4,6},{5,7},{6,4},{7,5},{8,10},{9,11},{10,... | collective-permute-start | bytes 786440 | tf_op jit(solution)/shard_map/ppermute | solution.py:21
  5.9 1.0 collective-permute-start.2
  6.9 1.2 copy-done
  8.1 1.2 copy-done.2
  9.4 1.2 copy-done.4
  10.6 1.2 copy-done.6
  11.8 1.7 shard_map.104
  13.5 0.0 copy-done.18
  13.5 0.7 constant_dynamic-update-slice_fusion.3
  14.3 0.0 collective-permute-done
  14.3 0.7 constant_dynamic-update-slice_fusion.2
  15.0 8.2 %collective-permute-done.1 = bf16[32,4096]{1,0:T(8,128)(2,1)S(1)} collective-permute-done((bf16[32,4096]{1,0:T(8,128)(2,1)}, bf16[32,4096]{1,0:T(8,128)(2,1)S(1)}, u32[]{:S(2)}, u32[]{:S(2)}) %collective-permute-start.1) | collective-permute-done | bytes 262176 | tf_op jit(solution)/shard_map/ppermute | solution.py:21
  23.2 0.7 constant_dynamic-update-slice_fusion.1
  23.9 0.0 collective-permute-done.2
  23.9 0.7 constant_dynamic-update-slice_fusion.refs_0_
  24.7 11.1 %all-to-all-start = ((bf16[16,4,128,128]{3,2,1,0:T(8,128)(2,1)}), bf16[16,4,128,128]{3,2,1,0:T(8,128)(2,1)}, u32[]{:S(2)}, u32[]{:S(2)}) async-start(bf16[16,4,128,128]{3,2,1,0:T(8,128)(2,1)} %shard_map.104), calls=%async_computation | async-start | bytes 4194304 | tf_op jit(solution)/shard_map/all_to_all | solution.py:229
  35.8 1.9 collective-permute-start.3
  37.6 2.7 %collective-permute-start.4 = (bf16[128,4096]{1,0:T(8,128)(2,1)}, bf16[128,4096]{1,0:T(8,128)(2,1)S(1)}, u32[]{:S(2)}, u32[]{:S(2)}) collective-permute-start(bf16[128,4096]{1,0:T(8,128)(2,1)} %constant_dynamic-update-slice_fusion.refs_0_), channel_id=1, source_target_pairs={{0,8},{1,9},{2,10},{3,11},{4,12},{5,13},{6,14},{7,15},{8,0},{9,1},... | collective-permute-start | bytes 3145736 | tf_op jit(solution)/shard_map/ppermute | solution.py:26
  40.3 1.5 collective-permute-start.5
  41.8 0.0 copy-done.1
  41.8 1.2 copy-done.7
  43.0 1.7 shard_map.107
  44.7 36.5 %collective-permute-done.3.refs_1_ = bf16[128,4096]{1,0:T(8,128)(2,1)S(1)} collective-permute-done((bf16[128,4096]{1,0:T(8,128)(2,1)}, bf16[128,4096]{1,0:T(8,128)(2,1)S(1)}, u32[]{:S(2)}, u32[]{:S(2)}) %collective-permute-start.3) | collective-permute-done | bytes 1048608 | tf_op jit(solution)/shard_map/ppermute | solution.py:26
  81.2 1.0 copy-done.10
  82.2 23.8 %collective-permute-done.4.refs_2_ = bf16[128,4096]{1,0:T(8,128)(2,1)S(1)} collective-permute-done((bf16[128,4096]{1,0:T(8,128)(2,1)}, bf16[128,4096]{1,0:T(8,128)(2,1)S(1)}, u32[]{:S(2)}, u32[]{:S(2)}) %collective-permute-start.4) | collective-permute-done | bytes 1048608 | tf_op jit(solution)/shard_map/ppermute | solution.py:26
  106.0 1.0 copy-done.12
  107.0 0.0 collective-permute-done.5.refs_3_
  107.0 1.1 copy-done.14
  108.1 0.0 all-to-all-done.query_ref.key_ref.value_ref.cross_ref
  108.1 4.8 %all-to-all-start.2 = ((bf16[16,4,128,128]{3,2,1,0:T(8,128)(2,1)}), bf16[16,4,128,128]{3,2,1,0:T(8,128)(2,1)}, u32[]{:S(2)}, u32[]{:S(2)}) async-start(bf16[16,4,128,128]{3,2,1,0:T(8,128)(2,1)} %shard_map.107), calls=%async_computation.2 | async-start | bytes 4194304 | tf_op jit(solution)/shard_map/all_to_all | solution.py:230
  113.5 0.1 broadcast_add_fusion
  113.6 0.2 select_reduce_fusion
  113.8 0.1 fusion
  113.9 0.1 select_n.53.bias_ref
  114.0 0.0 copy-start.9
  114.0 1.6 copy-done.9
  115.6 1.2 copy-done.13
  116.8 1.2 copy-done.15
  118.0 4.3 %shard_map.105.text_ref = bf16[512,512]{1,0:T(8,128)(2,1)S(1)} custom-call(bf16[128,4096]{1,0:T(8,128)(2,1)} %constant_dynamic-update-slice_fusion.refs_0_, bf16[128,4096]{1,0:T(8,128)(2,1)S(1)} %copy-done.11, bf16[128,4096]{1,0:T(8,128)(2,1)S(1)} %copy-done.13, bf16[128,4096]{1,0:T(8,128)(2,1)S(1)} %copy-done.15, bf16[4096,256]{1,0:T(8,128)(2,1)S(1)} %copy-done.8, ...), custom_call_target="tpu_custom_call" | custom-call | flops 2147483648 | bytes 8388608 | tf_op jit(solution)/shard_map/pallas_call | solution.py:176
  122.3 9.9 %shard_map.106 = bf16[16,2,128,128]{3,2,1,0:T(8,128)(2,1)} custom-call(bf16[16,4,128,128]{3,2,1,0:T(8,128)(2,1)} %all-to-all-done.query_ref.key_ref.value_ref.cross_ref, bf16[16,4,128,128]{3,2,1,0:T(8,128)(2,1)} %all-to-all-done.query_ref.key_ref.value_ref.cross_ref, bf16[16,4,128,128]{3,2,1,0:T(8,128)(2,1)} %all-to-all-done.query_ref.key_ref.value_ref.cross_ref, ...), custom_call_target="tpu_custom_call" | custom-call | flops 5368709120 | bytes 3145728 | tf_op jit(solution)/shard_map/pallas_call | solution.py:128
  132.3 0.8 copy-done.16
  133.1 30.3 %all-to-all-done.2.query_ref.key_ref.value_ref.cross_ref = bf16[16,4,128,128]{3,2,1,0:T(8,128)(2,1)} async-done(((bf16[16,4,128,128]{3,2,1,0:T(8,128)(2,1)}), bf16[16,4,128,128]{3,2,1,0:T(8,128)(2,1)}, u32[]{:S(2)}, u32[]{:S(2)}) %all-to-all-start.2) | async-done | bytes 2097184 | tf_op jit(solution)/shard_map/all_to_all | solution.py:230
  163.4 4.0 %all-to-all-start.1 = ((bf16[16,2,128,128]{3,2,1,0:T(8,128)(2,1)}), bf16[16,2,128,128]{3,2,1,0:T(8,128)(2,1)S(1)}, u32[]{:S(2)}, u32[]{:S(2)}) async-start(bf16[16,2,128,128]{3,2,1,0:T(8,128)(2,1)} %shard_map.106), calls=%async_computation.1 | async-start | bytes 2097152 | tf_op jit(solution)/shard_map/all_to_all | solution.py:233
  167.4 9.2 %shard_map.108 = bf16[16,2,128,128]{3,2,1,0:T(8,128)(2,1)S(1)} custom-call(bf16[16,4,128,128]{3,2,1,0:T(8,128)(2,1)} %all-to-all-done.2.query_ref.key_ref.value_ref.cross_ref, bf16[16,4,128,128]{3,2,1,0:T(8,128)(2,1)} %all-to-all-done.2.query_ref.key_ref.value_ref.cross_ref, bf16[16,4,128,128]{3,2,1,0:T(8,128)(2,1)} %all-to-all-done.2.query_ref.key_ref.value_ref.cross_ref, ...), custom_call_target="tpu_custom_call" | custom-call | flops 5368709120 | bytes 3145728 | tf_op jit(solution)/shard_map/pallas_call | solution.py:128
  176.5 18.5 %all-to-all-done.1.refs_0_ = bf16[16,2,128,128]{3,2,1,0:T(8,128)(2,1)S(1)} async-done(((bf16[16,2,128,128]{3,2,1,0:T(8,128)(2,1)}), bf16[16,2,128,128]{3,2,1,0:T(8,128)(2,1)S(1)}, u32[]{:S(2)}, u32[]{:S(2)}) %all-to-all-start.1) | async-done | bytes 1048608 | tf_op jit(solution)/shard_map/all_to_all | solution.py:233
  195.1 31.1 %all_to_all.20.refs_1_ = bf16[16,2,128,128]{3,2,1,0:T(8,128)(2,1)S(1)} all-to-all(bf16[16,2,128,128]{3,2,1,0:T(8,128)(2,1)S(1)} %shard_map.108), channel_id=1, replica_groups=mesh['clip'=16,'seq'=16] {'seq'}, dimensions={0} | all-to-all | bytes 2097152 | tf_op jit(solution)/shard_map/all_to_all | solution.py:233
  226.2 1.9 shard_map.109
  (27 shorter events, 0.1 us)
Async XLA Ops:
  0.6 13.6 %collective-permute-start = (bf16[32,4096]{1,0:T(8,128)(2,1)}, bf16[32,4096]{1,0:T(8,128)(2,1)S(1)}, u32[]{:S(2)}, u32[]{:S(2)}) collective-permute-start(bf16[32,4096]{1,0:T(8,128)(2,1)} %param.13), channel_id=1, source_target_pairs={{0,1},{1,2},{2,3},{3,0},{4,5},{5,6},{6,7},{7,4},{8,9},{9,10},{10,1... | collective-permute-start | bytes 786440 | tf_op jit(solution)/shard_map/ppermute | solution.py:21
  2.6 20.6 %collective-permute-start.1 = (bf16[32,4096]{1,0:T(8,128)(2,1)}, bf16[32,4096]{1,0:T(8,128)(2,1)S(1)}, u32[]{:S(2)}, u32[]{:S(2)}) collective-permute-start(bf16[32,4096]{1,0:T(8,128)(2,1)} %param.13), channel_id=1, source_target_pairs={{0,2},{1,3},{2,0},{3,1},{4,6},{5,7},{6,4},{7,5},{8,10},{9,11},{10,... | collective-permute-start | bytes 786440 | tf_op jit(solution)/shard_map/ppermute | solution.py:21
  5.9 18.0 %collective-permute-start.2 = (bf16[32,4096]{1,0:T(8,128)(2,1)}, bf16[32,4096]{1,0:T(8,128)(2,1)S(1)}, u32[]{:S(2)}, u32[]{:S(2)}) collective-permute-start(bf16[32,4096]{1,0:T(8,128)(2,1)} %param.13), channel_id=1, source_target_pairs={{0,3},{1,0},{2,1},{3,2},{4,7},{5,4},{6,5},{7,6},{8,11},{9,8},{10,9... | collective-permute-start | bytes 786440 | tf_op jit(solution)/shard_map/ppermute | solution.py:21
  6.9 1.2 copy-start
  8.1 1.2 copy-start.2
  9.4 1.2 copy-start.4
  10.6 1.2 copy-start.6
  11.8 1.7 copy-start.18
  24.7 17.1 %copy-start.1 = (bf16[128,4096]{1,0:T(8,128)(2,1)S(1)}, bf16[128,4096]{1,0:T(8,128)(2,1)}, u32[]{:S(2)}) copy-start(bf16[128,4096]{1,0:T(8,128)(2,1)} %refs_0_.3) | copy-start | bytes 3145732
  24.7 17.1 %copy-start.3 = (bf16[128,4096]{1,0:T(8,128)(2,1)S(1)}, bf16[128,4096]{1,0:T(8,128)(2,1)}, u32[]{:S(2)}) copy-start(bf16[128,4096]{1,0:T(8,128)(2,1)} %refs_1_.3) | copy-start | bytes 3145732
  24.7 17.1 %copy-start.5 = (bf16[128,4096]{1,0:T(8,128)(2,1)S(1)}, bf16[128,4096]{1,0:T(8,128)(2,1)}, u32[]{:S(2)}) copy-start(bf16[128,4096]{1,0:T(8,128)(2,1)} %refs_2_.3) | copy-start | bytes 3145732
  24.7 83.4 %all-to-all-start = ((bf16[16,4,128,128]{3,2,1,0:T(8,128)(2,1)}), bf16[16,4,128,128]{3,2,1,0:T(8,128)(2,1)}, u32[]{:S(2)}, u32[]{:S(2)}) async-start(bf16[16,4,128,128]{3,2,1,0:T(8,128)(2,1)} %shard_map.104), calls=%async_computation | async-start | bytes 4194304 | tf_op jit(solution)/shard_map/all_to_all | solution.py:229
  35.8 45.4 %collective-permute-start.3 = (bf16[128,4096]{1,0:T(8,128)(2,1)}, bf16[128,4096]{1,0:T(8,128)(2,1)S(1)}, u32[]{:S(2)}, u32[]{:S(2)}) collective-permute-start(bf16[128,4096]{1,0:T(8,128)(2,1)} %constant_dynamic-update-slice_fusion.refs_0_), channel_id=1, source_target_pairs={{0,4},{1,5},{2,6},{3,7},{4,8},{5,9},{6,10},{7,11},{8,12},{9,13},{1... | collective-permute-start | bytes 3145736 | tf_op jit(solution)/shard_map/ppermute | solution.py:26
  37.6 68.4 %collective-permute-start.4 = (bf16[128,4096]{1,0:T(8,128)(2,1)}, bf16[128,4096]{1,0:T(8,128)(2,1)S(1)}, u32[]{:S(2)}, u32[]{:S(2)}) collective-permute-start(bf16[128,4096]{1,0:T(8,128)(2,1)} %constant_dynamic-update-slice_fusion.refs_0_), channel_id=1, source_target_pairs={{0,8},{1,9},{2,10},{3,11},{4,12},{5,13},{6,14},{7,15},{8,0},{9,1},... | collective-permute-start | bytes 3145736 | tf_op jit(solution)/shard_map/ppermute | solution.py:26
  40.3 66.7 %collective-permute-start.5 = (bf16[128,4096]{1,0:T(8,128)(2,1)}, bf16[128,4096]{1,0:T(8,128)(2,1)S(1)}, u32[]{:S(2)}, u32[]{:S(2)}) collective-permute-start(bf16[128,4096]{1,0:T(8,128)(2,1)} %constant_dynamic-update-slice_fusion.refs_0_), channel_id=1, source_target_pairs={{0,12},{1,13},{2,14},{3,15},{4,0},{5,1},{6,2},{7,3},{8,4},{9,5},{1... | collective-permute-start | bytes 3145736 | tf_op jit(solution)/shard_map/ppermute | solution.py:26
  41.8 1.2 copy-start.7
  44.7 68.9 %copy-start.19 = (s32[16]{0:T(128)S(1)}, s32[16]{0:T(128)}, u32[]{:S(2)}) copy-start(s32[16]{0:T(128)} %param.14) | copy-start | bytes 196
  44.7 69.3 %copy-start.8 = (bf16[4096,256]{1,0:T(8,128)(2,1)S(1)}, bf16[4096,256]{1,0:T(8,128)(2,1)}, u32[]{:S(2)}) copy-start(bf16[4096,256]{1,0:T(8,128)(2,1)} %refs_4_.1) | copy-start | bytes 6291460
  81.2 1.0 copy-start.10
  106.0 1.0 copy-start.12
  107.0 7.0 %copy-start.11 = (bf16[128,4096]{1,0:T(8,128)(2,1)S(1)}, bf16[128,4096]{1,0:T(8,128)(2,1)}, u32[]{:S(2)}) copy-start(bf16[128,4096]{1,0:T(8,128)(2,1)} %copy-done.10) | copy-start | bytes 3145732
  107.0 1.1 copy-start.14
  108.1 55.3 %all-to-all-start.2 = ((bf16[16,4,128,128]{3,2,1,0:T(8,128)(2,1)}), bf16[16,4,128,128]{3,2,1,0:T(8,128)(2,1)}, u32[]{:S(2)}, u32[]{:S(2)}) async-start(bf16[16,4,128,128]{3,2,1,0:T(8,128)(2,1)} %shard_map.107), calls=%async_computation.2 | async-start | bytes 4194304 | tf_op jit(solution)/shard_map/all_to_all | solution.py:230
  114.0 1.6 copy-start.9
  115.6 1.2 copy-start.13
  116.8 1.2 copy-start.15
  132.3 0.8 copy-start.16
  163.4 4.0 %copy-start.17 = (bf16[512,512]{1,0:T(8,128)(2,1)S(1)}, bf16[512,512]{1,0:T(8,128)(2,1)}, u32[]{:S(2)}) copy-start(bf16[512,512]{1,0:T(8,128)(2,1)} %copy-done.16) | copy-start | bytes 1572868
  163.4 31.7 %all-to-all-start.1 = ((bf16[16,2,128,128]{3,2,1,0:T(8,128)(2,1)}), bf16[16,2,128,128]{3,2,1,0:T(8,128)(2,1)S(1)}, u32[]{:S(2)}, u32[]{:S(2)}) async-start(bf16[16,2,128,128]{3,2,1,0:T(8,128)(2,1)} %shard_map.106), calls=%async_computation.1 | async-start | bytes 2097152 | tf_op jit(solution)/shard_map/all_to_all | solution.py:233

commit v3 on v2

v3 whole, which is shorter than its diff:
```python
import functools
import math

import jax
import jax.numpy as jnp
from jax import lax
from jax.experimental import pallas as pl
from jax.experimental.pallas import tpu as pltpu
from jax.sharding import PartitionSpec as P

HEAD_DIM = 128
EXP2_SCALE = HEAD_DIM**-0.5 * math.log2(math.e)
SIDE = 4
BF16 = jnp.bfloat16
F32 = jnp.float32
MIB = 1024 * 1024


def shift_z(array, step):
    pairs = [(y * SIDE + z, y * SIDE + (z + step) % SIDE) for y in range(SIDE) for z in range(SIDE)]
    return lax.ppermute(array, "seq", pairs)


def shift_y(array, step):
    pairs = [(y * SIDE + z, (y + step) % SIDE * SIDE + z) for y in range(SIDE) for z in range(SIDE)]
    return lax.ppermute(array, "seq", pairs)


def swap_y(array):
    groups = [[y * SIDE + z for y in range(SIDE)] for z in range(SIDE)]
    return lax.all_to_all(
        array, "seq", split_axis=0, concat_axis=0, axis_index_groups=groups, tiled=True
    )


def pack_kernel(place_ref, *refs, sources):
    in_refs, second_ref, first_refs = refs[:sources], refs[sources], refs[sources + 1 :]
    z = place_ref[1]
    width = in_refs[0].shape[1] // (SIDE * SIDE)
    for y in range(SIDE):
        for t in range(SIDE):
            column = (y * SIDE + lax.rem(z + t, SIDE)) * width
            for which, ref in enumerate(in_refs):
                at = pl.ds(pl.multiple_of(column, HEAD_DIM), HEAD_DIM)
                first_refs[t][y, which] = ref[:, at]
                at = pl.ds(pl.multiple_of(column + HEAD_DIM, HEAD_DIM), HEAD_DIM)
                second_ref[y, t, which] = ref[:, at]


def pack(place, arrays):
    tokens, inner = arrays[0].shape
    piece = (len(arrays), tokens, HEAD_DIM)
    shapes = [jax.ShapeDtypeStruct((SIDE, SIDE, *piece), BF16)]
    shapes += [jax.ShapeDtypeStruct((SIDE, *piece), BF16)] * SIDE
    vmem = pl.BlockSpec(memory_space=pltpu.VMEM)
    second, *first = pl.pallas_call(
        functools.partial(pack_kernel, sources=len(arrays)),
        in_specs=[pl.BlockSpec(memory_space=pltpu.SMEM)] + [vmem] * len(arrays),
        out_specs=[vmem] * len(shapes),
        out_shape=shapes,
        compiler_params=pltpu.CompilerParams(vmem_limit_bytes=20 * MIB),
        cost_estimate=pl.CostEstimate(
            flops=0, bytes_accessed=4 * len(arrays) * tokens * inner, transcendentals=0
        ),
    )(place, *arrays)
    return first, second


def join_kernel(place_ref, *refs):
    z = place_ref[1]
    first_ref, second_refs, out_refs = refs[0], refs[1 : SIDE + 1], refs[SIDE + 1 :]
    for y in range(SIDE):
        for t in range(SIDE):
            for head in range(2):
                column = (y * SIDE + lax.rem(z + t, SIDE)) * 2 + head
                at = pl.ds(pl.multiple_of(column * HEAD_DIM, HEAD_DIM), HEAD_DIM)
                for which, out_ref in enumerate(out_refs):
                    if head == 0:
                        out_ref[:, at] = first_ref[y, t, which]
                    else:
                        out_ref[:, at] = second_refs[t][y, which]


def join(place, first, second, shape):
    vmem = pl.BlockSpec(memory_space=pltpu.VMEM)
    return pl.pallas_call(
        join_kernel,
        in_specs=[pl.BlockSpec(memory_space=pltpu.SMEM)] + [vmem] * (SIDE + 1),
        out_specs=[vmem] * 2,
        out_shape=[jax.ShapeDtypeStruct(shape, BF16)] * 2,
        compiler_params=pltpu.CompilerParams(vmem_limit_bytes=20 * MIB),
        cost_estimate=pl.CostEstimate(
            flops=0, bytes_accessed=8 * shape[0] * shape[1], transcendentals=0
        ),
    )(place, first, *second)


def head_output(queries, keys, wide_values, bias):
    scores = lax.dot_general(
        queries, keys, (((1,), (1,)), ((), ())), preferred_element_type=F32
    )
    if bias is not None:
        scores = scores + bias
    highest = jnp.max(scores, axis=1, keepdims=True)
    weights = jnp.exp2((scores - highest) * EXP2_SCALE).astype(BF16)
    both = jnp.dot(weights, wide_values, preferred_element_type=F32)
    return (both[:, :HEAD_DIM] / both[:, HEAD_DIM:]).astype(BF16)


def attend_kernel(*refs, head, blocks):
    *piece_refs, text_ref, bias_ref, out_ref, query_all, key_all, wide_all, cross_all = refs
    _, far_count, _, tokens, _ = out_ref.shape

    @pl.when(pl.program_id(0) == 0)
    def _():
        for far in range(SIDE):
            for near in range(SIDE):
                index = far * SIDE + near
                rows = slice(index * tokens, (index + 1) * tokens)
                ref = piece_refs[0].at[far, near] if len(piece_refs) == 1 else piece_refs[far].at[near]
                query_all[rows] = ref[0]
                key_all[rows] = ref[1]
                wide_all[rows, :HEAD_DIM] = ref[2]
                wide_all[rows, HEAD_DIM:] = jnp.ones((tokens, HEAD_DIM), BF16)
                cross_all[rows] = ref[3]

    width = text_ref.shape[1] // 2
    text_keys = text_ref[:, head * HEAD_DIM : (head + 1) * HEAD_DIM]
    text_values = text_ref[:, width + head * HEAD_DIM : width + (head + 1) * HEAD_DIM]
    wide_text = jnp.concatenate([text_values, jnp.ones_like(text_values)], axis=1)
    rows = far_count * SIDE * tokens // blocks
    start = pl.program_id(0) * (far_count * SIDE * tokens)
    for block in range(blocks):
        at = pl.ds(pl.multiple_of(start + block * rows, rows), rows)
        results = (
            head_output(query_all[at, :], key_all[...], wide_all[...], None),
            head_output(cross_all[at, :], text_keys, wide_text, bias_ref[...]),
        )
        for piece in range(rows // tokens):
            index = block * (rows // tokens) + piece
            for which, result in enumerate(results):
                out_ref[index % SIDE, index // SIDE, which] = result[
                    piece * tokens : (piece + 1) * tokens
                ]


def attend(pieces, specs, text, bias, head):
    tokens = pieces[0].shape[-2]
    count = SIDE * SIDE * tokens
    return pl.pallas_call(
        functools.partial(attend_kernel, head=head, blocks=4),
        grid=(2,),
        in_specs=specs
        + [
            pl.BlockSpec(text.shape, lambda i: (0, 0)),
            pl.BlockSpec(bias.shape, lambda i: (0, 0)),
        ],
        out_specs=pl.BlockSpec(
            (SIDE, SIDE // 2, 2, tokens, HEAD_DIM), lambda i: (0, i, 0, 0, 0)
        ),
        out_shape=jax.ShapeDtypeStruct((SIDE, SIDE, 2, tokens, HEAD_DIM), BF16),
        scratch_shapes=[
            pltpu.VMEM((count, HEAD_DIM), BF16),
            pltpu.VMEM((count, HEAD_DIM), BF16),
            pltpu.VMEM((count, 2 * HEAD_DIM), BF16),
            pltpu.VMEM((count, HEAD_DIM), BF16),
        ],
        compiler_params=pltpu.CompilerParams(vmem_limit_bytes=20 * MIB),
        cost_estimate=pl.CostEstimate(
            flops=8 * count * (count + text.shape[0]) * HEAD_DIM,
            bytes_accessed=12 * count * HEAD_DIM,
            transcendentals=count * (count + text.shape[0]),
        ),
    )(*pieces, text, bias)


def project_kernel(*refs):
    *text_refs, key_weight_ref, value_weight_ref, out_ref, total = refs
    rows = text_refs[0].shape[0]
    width = key_weight_ref.shape[1]

    @pl.when(pl.program_id(0) == 0)
    def _():
        total[...] = jnp.zeros_like(total)

    for s, ref in enumerate(text_refs):
        for which, weight_ref in enumerate((key_weight_ref, value_weight_ref)):
            total[s * rows : (s + 1) * rows, which * width : (which + 1) * width] += jnp.dot(
                ref[...], weight_ref[...], preferred_element_type=F32
            )

    @pl.when(pl.program_id(0) == pl.num_programs(0) - 1)
    def _():
        out_ref[...] = total[...].astype(BF16)


def project(texts, key_weight, value_weight):
    rows, depth = texts[0].shape
    width = key_weight.shape[1]
    step = 1024
    shape = (len(texts) * rows, 2 * width)
    return pl.pallas_call(
        project_kernel,
        grid=(depth // step,),
        in_specs=[pl.BlockSpec((rows, step), lambda i: (0, i))] * len(texts)
        + [pl.BlockSpec((step, width), lambda i: (i, 0))] * 2,
        out_specs=pl.BlockSpec(shape, lambda i: (0, 0)),
        out_shape=jax.ShapeDtypeStruct(shape, BF16),
        scratch_shapes=[pltpu.VMEM(shape, F32)],
        compiler_params=pltpu.CompilerParams(vmem_limit_bytes=20 * MIB),
        cost_estimate=pl.CostEstimate(
            flops=2 * shape[0] * shape[1] * depth,
            bytes_accessed=2 * depth * (shape[0] + shape[1]),
            transcendentals=0,
        ),
    )(*texts, key_weight, value_weight)


def after(array, *earlier):
    return lax.optimization_barrier((array, *earlier))[0]


def body(
    video_query,
    video_key,
    video_value,
    cross_query,
    text_rows,
    text_block,
    text_length,
    key_weight,
    value_weight,
):
    index = lax.axis_index("seq")
    y, z = index // SIDE, index % SIDE
    place = jnp.stack([y, z]).astype(jnp.int32)
    text_shard = text_rows.shape[0]
    side = range(SIDE)
    steps = range(1, SIDE)

    text_from = {t: shift_z(text_rows, t) for t in steps}
    text_z = jnp.concatenate([text_rows] + [text_from[t] for t in steps], axis=0)

    arrays = (video_query, video_key, video_value, cross_query)
    first, second = pack(place, arrays)
    second_y = swap_y(second)
    first_z = {0: first[0]}
    for t in steps:
        first_z[t] = shift_z(after(first[t], text_from[t]), t)

    text_y = {0: text_z, 2: shift_y(text_z, 2), 1: shift_y(text_z, 1), 3: shift_y(text_z, 3)}
    text_own = project([text_y[s] for s in side], key_weight, value_weight)

    second_z = {t: shift_z(after(second_y[:, t], first_z[t]), t) for t in steps}
    first_y = swap_y(after(jnp.stack([first_z[t] for t in side], axis=1), *[text_y[s] for s in steps]))

    near = jnp.arange(SIDE, dtype=jnp.int32)
    holder = ((y - near) % SIDE * SIDE)[:, None] + ((z - near) % SIDE)[None, :]
    matches = holder[..., None] == jnp.arange(SIDE * SIDE, dtype=jnp.int32)
    blocks = jnp.sum(jnp.where(matches, text_block, 0), axis=-1)
    position = blocks[..., None] * text_shard + jnp.arange(text_shard, dtype=jnp.int32)
    bias = jnp.where(position < text_length[0], 0.0, -jnp.inf).astype(F32).reshape(1, -1)

    tokens = video_query.shape[0]
    piece = (len(arrays), tokens, HEAD_DIM)
    first_heads = attend(
        [first_y],
        [pl.BlockSpec((SIDE, SIDE, *piece), lambda i: (0, 0, 0, 0, 0))],
        text_own,
        bias,
        0,
    )
    second_heads = attend(
        [second_y] + [second_z[t] for t in steps],
        [pl.BlockSpec((SIDE, None, *piece), lambda i: (0, 0, 0, 0, 0))]
        + [pl.BlockSpec((SIDE, *piece), lambda i: (0, 0, 0, 0))] * (SIDE - 1),
        text_own,
        bias,
        1,
    )
    first_back = {0: first_heads[0]}
    for t in steps:
        first_back[t] = shift_z(first_heads[t], -t)
    second_back = swap_y(second_heads)
    second_home = {0: second_back[:, 0]}
    for t in steps:
        second_home[t] = shift_z(after(second_back[:, t], first_back[t]), -t)
    first_home = swap_y(
        after(jnp.stack([first_back[t] for t in side], axis=1), second_back)
    )
    self_out, cross_out = join(
        place, first_home, [second_home[t] for t in side], video_query.shape
    )
    return self_out, cross_out


def solution(mesh):
    rows = P(("clip", "seq"), None)
    return jax.shard_map(
        body,
        mesh=mesh,
        in_specs=(
            rows,
            rows,
            rows,
            rows,
            rows,
            P("clip"),
            P("clip"),
            P(None, "seq"),
            P(None, "seq"),
        ),
        out_specs=(rows, rows),
        check_vma=False,
    )
```

time: 229 us -> 233 us (1.017)
  starting transfers between devices: 32.1 us -> 76.2 us
  blocking collectives: 31.1 us -> 0 us
  waiting for transfers between devices: 117 us -> 99.7 us
  local copies, waits for them, and re-layouts: 17 us -> 24.5 us
  other arithmetic: 0.38 us -> 3.14 us
    ppermute x3 -> x15, waiting for transfers between devices: 8.24 us -> 92.3 us  [shift_z(): return lax.ppermute(array, 'seq', pairs)]
    ppermute x3, waiting for transfers between devices: 60.4 us -> 7.42 us  [shift_y(): return lax.ppermute(array, 'seq', pairs)]
    all_to_all x3 -> x4, waiting for transfers between devices: 48.9 us -> 0.01 us  [swap_y(): lax.all_to_all(array, 'seq', split_axis=0, concat_axis=0, axis_index_grou...]
    ppermute x3 -> x15, starting transfers between devices: 6.27 us -> 53.4 us  [shift_z(): return lax.ppermute(array, 'seq', pairs)]
    all_to_all x1 -> x0, blocking collectives: 31.1 us -> none  [body(): self_out, cross_out = join([swap(first_heads), swap(second_heads)])]
    unnamed x43 -> x51, local copies, waits for them, and re-layouts: 16.1 us -> 22 us
    another operation x0 -> x3, other arithmetic: none -> 2.77 us  [the longest x1 1.6 us: body(): jnp.stack([first_z[t] for t in side], axis=1)]
    all_to_all x3 -> x4, starting transfers between devices: 19.8 us -> 18.1 us  [swap_y(): lax.all_to_all(array, 'seq', split_axis=0, concat_axis=0, axis_index_grou...]
  transfers between devices with their start and end apart: 9 -> 22, of which waited for: 5 -> 8; matrix products, arithmetic and copies ran while one was open for 1% -> 3% of each run, Pallas kernels for 12% -> 11%
where the time goes in v3:
time: 233 us; the launch traced here: 232 us
  waiting for transfers between devices  99.7 us (43%)
  starting transfers between devices  76.2 us (33%)
  Pallas kernels  26.9 us (12%)
  local copies, waits for them, and re-layouts  24.5 us (11%)
  other arithmetic  3.14 us (1%)
    ppermute x15, waiting for transfers between devices, shift_z(): return lax.ppermute(array, 'seq', pairs)  92.3 us
    ppermute x15, starting transfers between devices, shift_z(): return lax.ppermute(array, 'seq', pairs)  53.4 us
    unnamed x51, local copies, waits for them, and re-layouts  22 us
    pallas_call x2, Pallas kernels, attend(): pl.pallas_call(functools.partial(attend_kernel, head=head, blocks=4), gri...  19.5 us
    all_to_all x4, starting transfers between devices, swap_y(): lax.all_to_all(array, 'seq', split_axis=0, concat_axis=0, axis_index_grou...  18.1 us
    ppermute x3, waiting for transfers between devices, shift_y(): return lax.ppermute(array, 'seq', pairs)  7.42 us
    ppermute x3, starting transfers between devices, shift_y(): return lax.ppermute(array, 'seq', pairs)  4.69 us
  transfers between devices with their start and end apart: 22, of which 8 were waited for; matrix products, arithmetic and copies ran while one was open for 3% of the time, Pallas kernels for 11%

profile of v3, /device:TPU:2, one launch (start us, length us, event | category | flops | bytes accessed | tf_op | source)
XLA Modules:
  0.0 231.9 jit_solution(4337272428880203777)
XLA Ops:
  0.6 3.4 %collective-permute-start.2 = (bf16[32,4096]{1,0:T(8,128)(2,1)}, bf16[32,4096]{1,0:T(8,128)(2,1)}, u32[]{:S(2)}, u32[]{:S(2)}) collective-permute-start(bf16[32,4096]{1,0:T(8,128)(2,1)} %param.13), channel_id=1, source_target_pairs={{0,2},{1,3},{2,0},{3,1},{4,6},{5,7},{6,4},{7,5},{8,10},{9,11},{10,... | collective-permute-start | bytes 786440 | tf_op jit(solution)/shard_map/ppermute | solution.py:21
  4.0 1.9 collective-permute-start
  5.9 1.9 collective-permute-start.4
  7.9 1.2 copy-done.3
  9.1 1.2 copy-done.4
  10.3 1.2 copy-done.5
  11.6 1.2 copy-done.6
  12.8 1.6 shard_map.104
  14.4 1.3 copy-done.2
  19.0 4.6 %all-to-all-start.1 = ((bf16[4,4,4,128,128]{4,3,2,1,0:T(8,128)(2,1)}), bf16[4,4,4,128,128]{4,3,2,1,0:T(8,128)(2,1)S(1)}, u32[]{:S(2)}, u32[]{:S(2)}) async-start(bf16[4,4,4,128,128]{4,3,2,1,0:T(8,128)(2,1)} %copy-done.2), calls=%async_computation.1 | async-start | bytes 4194304 | tf_op jit(solution)/shard_map/all_to_all | solution.py:31
  23.6 1.9 collective-permute-start.5
  26.5 1.0 constant_dynamic-update-slice_fusion.1
  27.5 1.0 constant_dynamic-update-slice_fusion.refs_0_
  28.5 3.1 %collective-permute-start.8 = (bf16[128,4096]{1,0:T(8,128)(2,1)S(1)}, bf16[128,4096]{1,0:T(8,128)(2,1)S(1)}, u32[]{:S(2)}, u32[]{:S(2)}) collective-permute-start(bf16[128,4096]{1,0:T(8,128)(2,1)S(1)} %constant_dynamic-update-slice_fusion.refs_0_), channel_id=1, source_target_pairs={{0,12},{1,13},{2,14},{3,15},{4,0},{5,1},{6,2},{7,3},{8,4},{9,5},{1... | collective-permute-start | bytes 3145736 | tf_op jit(solution)/shard_map/ppermute | solution.py:26
  32.2 1.0 collective-permute-start.6
  33.2 15.8 %collective-permute-start.3 = (bf16[4,4,128,128]{3,2,1,0:T(8,128)(2,1)S(1)}, bf16[4,4,128,128]{3,2,1,0:T(8,128)(2,1)S(1)}, u32[]{:S(2)}, u32[]{:S(2)}) collective-permute-start(bf16[4,4,128,128]{3,2,1,0:T(8,128)(2,1)S(1)} %copy-done.20), channel_id=1, source_target_pairs={{0,2},{1,3},{2,0},{3,1},{4,6},{5,7},{6,4},{7,5},{8,10},{9,11},{10,... | collective-permute-start | bytes 1572872 | tf_op jit(solution)/shard_map/ppermute | solution.py:21
  49.0 33.7 %collective-permute-done.3 = bf16[4,4,128,128]{3,2,1,0:T(8,128)(2,1)S(1)} collective-permute-done((bf16[4,4,128,128]{3,2,1,0:T(8,128)(2,1)S(1)}, bf16[4,4,128,128]{3,2,1,0:T(8,128)(2,1)S(1)}, u32[]{:S(2)}, u32[]{:S(2)}) %collective-permute-start.3) | collective-permute-done | bytes 524320 | tf_op jit(solution)/shard_map/ppermute | solution.py:21
  82.7 1.6 pad_maximum_fusion
  84.3 1.0 copy-done.7
  85.3 1.0 copy-done.9
  86.3 7.4 %collective-permute-done.6.refs_1_ = bf16[128,4096]{1,0:T(8,128)(2,1)S(1)} collective-permute-done((bf16[128,4096]{1,0:T(8,128)(2,1)S(1)}, bf16[128,4096]{1,0:T(8,128)(2,1)S(1)}, u32[]{:S(2)}, u32[]{:S(2)}) %collective-permute-start.6) | collective-permute-done | bytes 1048608 | tf_op jit(solution)/shard_map/ppermute | solution.py:26
  93.7 1.0 copy-done.11
  94.7 4.4 %all-to-all-start = ((bf16[4,4,4,128,128]{4,3,2,1,0:T(8,128)(2,1)}), bf16[4,4,4,128,128]{4,3,2,1,0:T(8,128)(2,1)}, u32[]{:S(2)}, u32[]{:S(2)}) async-start(bf16[4,4,4,128,128]{4,3,2,1,0:T(8,128)(2,1)} %pad_maximum_fusion), calls=%async_computation | async-start | bytes 4194304 | tf_op jit(solution)/shard_map/all_to_all | solution.py:31
  99.4 1.2 slice_bitcast_fusion
  100.7 1.0 collective-permute-start.12
  101.7 1.4 collective-permute-start.13
  103.1 2.9 %collective-permute-start.14 = (bf16[4,4,128,128]{3,2,1,0:T(8,128)(2,1)}, bf16[4,4,128,128]{3,2,1,0:T(8,128)(2,1)}, u32[]{:S(2)}, u32[]{:S(2)}) collective-permute-start(bf16[4,4,128,128]{3,2,1,0:T(8,128)(2,1)} %get-tuple-element.29), channel_id=1, source_target_pairs={{0,3},{1,0},{2,1},{3,2},{4,7},{5,4},{6,5},{7,6},{8,11},{9,8},{10,9... | collective-permute-start | bytes 1572872 | tf_op jit(solution)/shard_map/ppermute | solution.py:21
  106.8 1.6 copy-done
  108.4 1.6 copy-done.1
  110.0 1.2 copy-done.8
  111.2 1.2 copy-done.10
  112.5 1.2 copy-done.12
  113.7 3.4 %shard_map.105.refs_1_.refs_4_ = bf16[512,512]{1,0:T(8,128)(2,1)S(1)} custom-call(bf16[128,4096]{1,0:T(8,128)(2,1)S(1)} %constant_dynamic-update-slice_fusion.refs_0_, bf16[128,4096]{1,0:T(8,128)(2,1)S(1)} %copy-done.12, bf16[128,4096]{1,0:T(8,128)(2,1)S(1)} %copy-done.10, bf16[128,4096]{1,0:T(8,128)(2,1)S(1)} %copy-done.8, bf16[4096,256]{1,0:T(8,128)(2,1)S(1)} %copy-done, ...), custom_call_target="tpu_custom_call" | custom-call | flops 2147483648 | bytes 8388608 | tf_op jit(solution)/shard_map/pallas_call | solution.py:202
  117.8 19.2 %collective-permute-done.13.refs_2_ = bf16[4,4,128,128]{3,2,1,0:T(8,128)(2,1)} collective-permute-done((bf16[4,4,128,128]{3,2,1,0:T(8,128)(2,1)}, bf16[4,4,128,128]{3,2,1,0:T(8,128)(2,1)}, u32[]{:S(2)}, u32[]{:S(2)}) %collective-permute-start.13) | collective-permute-done | bytes 524320 | tf_op jit(solution)/shard_map/ppermute | solution.py:21
  137.0 10.0 %shard_map.107 = bf16[4,4,2,128,128]{4,3,2,1,0:T(8,128)(2,1)} custom-call(bf16[4,4,4,128,128]{4,3,2,1,0:T(8,128)(2,1)S(1)} %all-to-all-done.1.refs_0_, bf16[4,4,128,128]{3,2,1,0:T(8,128)(2,1)} %collective-permute-done.12.refs_1_, bf16[4,4,128,128]{3,2,1,0:T(8,128)(2,1)} %collective-permute-done.13.refs_2_, ...), custom_call_target="tpu_custom_call" | custom-call | flops 5368709120 | bytes 3145728 | tf_op jit(solution)/shard_map/pallas_call | solution.py:150
  147.8 4.6 %all-to-all-start.2 = ((bf16[4,4,2,128,128]{4,3,2,1,0:T(8,128)(2,1)}), bf16[4,4,2,128,128]{4,3,2,1,0:T(8,128)(2,1)S(1)}, u32[]{:S(2)}, u32[]{:S(2)}) async-start(bf16[4,4,2,128,128]{4,3,2,1,0:T(8,128)(2,1)} %shard_map.107), calls=%async_computation.2 | async-start | bytes 2097152 | tf_op jit(solution)/shard_map/all_to_all | solution.py:31
  152.4 9.5 %shard_map.106 = bf16[4,4,2,128,128]{4,3,2,1,0:T(8,128)(2,1)S(1)} custom-call(bf16[4,4,4,128,128]{4,3,2,1,0:T(8,128)(2,1)} %all-to-all-done.refs_0_, bf16[512,512]{1,0:T(8,128)(2,1)S(1)} %copy-done.14, f32[1,512]{1,0:T(1,128)S(1)} %select_n.53.refs_2_.refs_5_), custom_call_target="tpu_custom_call" | custom-call | flops 5368709120 | bytes 3145728 | tf_op jit(solution)/shard_map/pallas_call | solution.py:150
  162.0 12.1 %collective-permute-start.11 = (bf16[4,2,128,128]{3,2,1,0:T(8,128)(2,1)S(1)}, bf16[4,2,128,128]{3,2,1,0:T(8,128)(2,1)S(1)}, u32[]{:S(2)}, u32[]{:S(2)}) collective-permute-start(bf16[4,2,128,128]{3,2,1,0:T(8,128)(2,1)S(1)} %get-tuple-element.42), channel_id=1, source_target_pairs={{0,1},{1,2},{2,3},{3,0},{4,5},{5,6},{6,7},{7,4},{8,9},{9,10},{10,1... | collective-permute-start | bytes 786440 | tf_op jit(solution)/shard_map/ppermute | solution.py:21
  174.1 3.4 %collective-permute-start.10 = (bf16[4,2,128,128]{3,2,1,0:T(8,128)(2,1)S(1)}, bf16[4,2,128,128]{3,2,1,0:T(8,128)(2,1)S(1)}, u32[]{:S(2)}, u32[]{:S(2)}) collective-permute-start(bf16[4,2,128,128]{3,2,1,0:T(8,128)(2,1)S(1)} %get-tuple-element.43), channel_id=1, source_target_pairs={{0,2},{1,3},{2,0},{3,1},{4,6},{5,7},{6,4},{7,5},{8,10},{9,11},{10,... | collective-permute-start | bytes 786440 | tf_op jit(solution)/shard_map/ppermute | solution.py:21
  177.5 6.8 %collective-permute-done.11 = bf16[4,2,128,128]{3,2,1,0:T(8,128)(2,1)S(1)} collective-permute-done((bf16[4,2,128,128]{3,2,1,0:T(8,128)(2,1)S(1)}, bf16[4,2,128,128]{3,2,1,0:T(8,128)(2,1)S(1)}, u32[]{:S(2)}, u32[]{:S(2)}) %collective-permute-start.11) | collective-permute-done | bytes 262176 | tf_op jit(solution)/shard_map/ppermute | solution.py:21
  184.3 9.1 %collective-permute-done.10 = bf16[4,2,128,128]{3,2,1,0:T(8,128)(2,1)S(1)} collective-permute-done((bf16[4,2,128,128]{3,2,1,0:T(8,128)(2,1)S(1)}, bf16[4,2,128,128]{3,2,1,0:T(8,128)(2,1)S(1)}, u32[]{:S(2)}, u32[]{:S(2)}) %collective-permute-start.10) | collective-permute-done | bytes 262176 | tf_op jit(solution)/shard_map/ppermute | solution.py:21
  193.3 1.1 pad_maximum_fusion.1
  194.4 4.5 %all-to-all-start.3 = ((bf16[4,4,2,128,128]{4,3,2,1,0:T(8,128)(2,1)}), bf16[4,4,2,128,128]{4,3,2,1,0:T(8,128)(2,1)S(1)}, u32[]{:S(2)}, u32[]{:S(2)}) async-start(bf16[4,4,2,128,128]{4,3,2,1,0:T(8,128)(2,1)} %pad_maximum_fusion.1), calls=%async_computation.3 | async-start | bytes 2097152 | tf_op jit(solution)/shard_map/all_to_all | solution.py:31
  199.0 6.0 %collective-permute-start.15 = (bf16[4,2,128,128]{3,2,1,0:T(8,128)(2,1)S(1)}, bf16[4,2,128,128]{3,2,1,0:T(8,128)(2,1)S(1)}, u32[]{:S(2)}, u32[]{:S(2)}) collective-permute-start(bf16[4,2,128,128]{3,2,1,0:T(8,128)(2,1)S(1)} %get-tuple-element.31), channel_id=1, source_target_pairs={{0,3},{1,0},{2,1},{3,2},{4,7},{5,4},{6,5},{7,6},{8,11},{9,8},{10,9... | collective-permute-start | bytes 786440 | tf_op jit(solution)/shard_map/ppermute | solution.py:21
  205.0 1.7 collective-permute-start.16
  206.6 5.0 %collective-permute-done.15.refs_2_ = bf16[4,2,128,128]{3,2,1,0:T(8,128)(2,1)S(1)} collective-permute-done((bf16[4,2,128,128]{3,2,1,0:T(8,128)(2,1)S(1)}, bf16[4,2,128,128]{3,2,1,0:T(8,128)(2,1)S(1)}, u32[]{:S(2)}, u32[]{:S(2)}) %collective-permute-start.15) | collective-permute-done | bytes 262176 | tf_op jit(solution)/shard_map/ppermute | solution.py:21
  211.7 17.7 %collective-permute-done.16.refs_3_ = bf16[4,2,128,128]{3,2,1,0:T(8,128)(2,1)S(1)} collective-permute-done((bf16[4,2,128,128]{3,2,1,0:T(8,128)(2,1)S(1)}, bf16[4,2,128,128]{3,2,1,0:T(8,128)(2,1)S(1)}, u32[]{:S(2)}, u32[]{:S(2)}) %collective-permute-start.16) | collective-permute-done | bytes 262176 | tf_op jit(solution)/shard_map/ppermute | solution.py:21
  229.4 2.5 %shard_map.108 = (bf16[128,4096]{1,0:T(8,128)(2,1)}, bf16[128,4096]{1,0:T(8,128)(2,1)}) custom-call(s32[2]{0:T(128)S(1)} %pad_add_fusion.place_ref, bf16[4,4,2,128,128]{4,3,2,1,0:T(8,128)(2,1)S(1)} %all-to-all-done.3.refs_0_, bf16[4,2,128,128]{3,2,1,0:T(8,128)(2,1)S(1)} %get-tuple-element.40.refs_1_, ...), custom_call_target="tpu_custom_call" | custom-call | bytes 4194304 | tf_op jit(solution)/shard_map/pallas_call | solution.py:86
  (65 shorter events, 7.1 us)
Async XLA Ops:
  0.6 25.9 %collective-permute-start.2 = (bf16[32,4096]{1,0:T(8,128)(2,1)}, bf16[32,4096]{1,0:T(8,128)(2,1)}, u32[]{:S(2)}, u32[]{:S(2)}) collective-permute-start(bf16[32,4096]{1,0:T(8,128)(2,1)} %param.13), channel_id=1, source_target_pairs={{0,2},{1,3},{2,0},{3,1},{4,6},{5,7},{6,4},{7,5},{8,10},{9,11},{10,... | collective-permute-start | bytes 786440 | tf_op jit(solution)/shard_map/ppermute | solution.py:21
  4.0 21.5 %collective-permute-start = (bf16[32,4096]{1,0:T(8,128)(2,1)}, bf16[32,4096]{1,0:T(8,128)(2,1)}, u32[]{:S(2)}, u32[]{:S(2)}) collective-permute-start(bf16[32,4096]{1,0:T(8,128)(2,1)} %param.13), channel_id=1, source_target_pairs={{0,1},{1,2},{2,3},{3,0},{4,5},{5,6},{6,7},{7,4},{8,9},{9,10},{10,1... | collective-permute-start | bytes 786440 | tf_op jit(solution)/shard_map/ppermute | solution.py:21
  5.9 17.7 %collective-permute-start.4 = (bf16[32,4096]{1,0:T(8,128)(2,1)}, bf16[32,4096]{1,0:T(8,128)(2,1)}, u32[]{:S(2)}, u32[]{:S(2)}) collective-permute-start(bf16[32,4096]{1,0:T(8,128)(2,1)} %param.13), channel_id=1, source_target_pairs={{0,3},{1,0},{2,1},{3,2},{4,7},{5,4},{6,5},{7,6},{8,11},{9,8},{10,9... | collective-permute-start | bytes 786440 | tf_op jit(solution)/shard_map/ppermute | solution.py:21
  7.9 1.2 copy-start.3
  9.1 1.2 copy-start.4
  10.3 1.2 copy-start.5
  11.6 1.2 copy-start.6
  14.4 1.3 copy-start.2
  15.8 0.8 copy-start.15
  16.6 0.8 copy-start.17
  17.4 0.8 copy-start.19
  18.2 0.8 copy-start.21
  19.0 4.6 %copy-start.22 = (bf16[32,4096]{1,0:T(8,128)(2,1)S(1)}, bf16[32,4096]{1,0:T(8,128)(2,1)}, u32[]{:S(2)}) copy-start(bf16[32,4096]{1,0:T(8,128)(2,1)} %param.13) | copy-start | bytes 786436
  19.0 75.7 %all-to-all-start.1 = ((bf16[4,4,4,128,128]{4,3,2,1,0:T(8,128)(2,1)}), bf16[4,4,4,128,128]{4,3,2,1,0:T(8,128)(2,1)S(1)}, u32[]{:S(2)}, u32[]{:S(2)}) async-start(bf16[4,4,4,128,128]{4,3,2,1,0:T(8,128)(2,1)} %copy-done.2), calls=%async_computation.1 | async-start | bytes 4194304 | tf_op jit(solution)/shard_map/all_to_all | solution.py:31
  23.6 9.6 %copy-start.20 = (bf16[4,4,128,128]{3,2,1,0:T(8,128)(2,1)S(1)}, bf16[4,4,128,128]{3,2,1,0:T(8,128)(2,1)}, u32[]{:S(2)}) copy-start(bf16[4,4,128,128]{3,2,1,0:T(8,128)(2,1)} %copy-done.19) | copy-start | bytes 1572868
  23.6 25.4 %copy-start.18 = (bf16[4,4,128,128]{3,2,1,0:T(8,128)(2,1)S(1)}, bf16[4,4,128,128]{3,2,1,0:T(8,128)(2,1)}, u32[]{:S(2)}) copy-start(bf16[4,4,128,128]{3,2,1,0:T(8,128)(2,1)} %copy-done.17) | copy-start | bytes 1572868
  23.6 59.1 %copy-start.16 = (bf16[4,4,128,128]{3,2,1,0:T(8,128)(2,1)S(1)}, bf16[4,4,128,128]{3,2,1,0:T(8,128)(2,1)}, u32[]{:S(2)}) copy-start(bf16[4,4,128,128]{3,2,1,0:T(8,128)(2,1)} %copy-done.15) | copy-start | bytes 1572868
  23.6 25.4 %collective-permute-start.5 = (bf16[4,4,128,128]{3,2,1,0:T(8,128)(2,1)}, bf16[4,4,128,128]{3,2,1,0:T(8,128)(2,1)S(1)}, u32[]{:S(2)}, u32[]{:S(2)}) collective-permute-start(bf16[4,4,128,128]{3,2,1,0:T(8,128)(2,1)} %copy-done.21), channel_id=1, source_target_pairs={{0,3},{1,0},{2,1},{3,2},{4,7},{5,4},{6,5},{7,6},{8,11},{9,8},{10,9... | collective-permute-start | bytes 1572872 | tf_op jit(solution)/shard_map/ppermute | solution.py:21
  28.5 55.8 %collective-permute-start.8 = (bf16[128,4096]{1,0:T(8,128)(2,1)S(1)}, bf16[128,4096]{1,0:T(8,128)(2,1)S(1)}, u32[]{:S(2)}, u32[]{:S(2)}) collective-permute-start(bf16[128,4096]{1,0:T(8,128)(2,1)S(1)} %constant_dynamic-update-slice_fusion.refs_0_), channel_id=1, source_target_pairs={{0,12},{1,13},{2,14},{3,15},{4,0},{5,1},{6,2},{7,3},{8,4},{9,5},{1... | collective-permute-start | bytes 3145736 | tf_op jit(solution)/shard_map/ppermute | solution.py:26
  31.6 53.8 %collective-permute-start.7 = (bf16[128,4096]{1,0:T(8,128)(2,1)S(1)}, bf16[128,4096]{1,0:T(8,128)(2,1)S(1)}, u32[]{:S(2)}, u32[]{:S(2)}) collective-permute-start(bf16[128,4096]{1,0:T(8,128)(2,1)S(1)} %constant_dynamic-update-slice_fusion.refs_0_), channel_id=1, source_target_pairs={{0,8},{1,9},{2,10},{3,11},{4,12},{5,13},{6,14},{7,15},{8,0},{9,1},... | collective-permute-start | bytes 3145736 | tf_op jit(solution)/shard_map/ppermute | solution.py:26
  32.2 61.5 %collective-permute-start.6 = (bf16[128,4096]{1,0:T(8,128)(2,1)S(1)}, bf16[128,4096]{1,0:T(8,128)(2,1)S(1)}, u32[]{:S(2)}, u32[]{:S(2)}) collective-permute-start(bf16[128,4096]{1,0:T(8,128)(2,1)S(1)} %constant_dynamic-update-slice_fusion.refs_0_), channel_id=1, source_target_pairs={{0,4},{1,5},{2,6},{3,7},{4,8},{5,9},{6,10},{7,11},{8,12},{9,13},{1... | collective-permute-start | bytes 3145736 | tf_op jit(solution)/shard_map/ppermute | solution.py:26
  33.2 49.5 %collective-permute-start.3 = (bf16[4,4,128,128]{3,2,1,0:T(8,128)(2,1)S(1)}, bf16[4,4,128,128]{3,2,1,0:T(8,128)(2,1)S(1)}, u32[]{:S(2)}, u32[]{:S(2)}) collective-permute-start(bf16[4,4,128,128]{3,2,1,0:T(8,128)(2,1)S(1)} %copy-done.20), channel_id=1, source_target_pairs={{0,2},{1,3},{2,0},{3,1},{4,6},{5,7},{6,4},{7,5},{8,10},{9,11},{10,... | collective-permute-start | bytes 1572872 | tf_op jit(solution)/shard_map/ppermute | solution.py:21
  49.0 33.7 %collective-permute-start.1 = (bf16[4,4,128,128]{3,2,1,0:T(8,128)(2,1)S(1)}, bf16[4,4,128,128]{3,2,1,0:T(8,128)(2,1)S(1)}, u32[]{:S(2)}, u32[]{:S(2)}) collective-permute-start(bf16[4,4,128,128]{3,2,1,0:T(8,128)(2,1)S(1)} %copy-done.18), channel_id=1, source_target_pairs={{0,1},{1,2},{2,3},{3,0},{4,5},{5,6},{6,7},{7,4},{8,9},{9,10},{10,1... | collective-permute-start | bytes 1572872 | tf_op jit(solution)/shard_map/ppermute | solution.py:21
  84.3 14.9 %copy-start.23 = (s32[16]{0:T(128)S(1)}, s32[16]{0:T(128)}, u32[]{:S(2)}) copy-start(s32[16]{0:T(128)} %param.14) | copy-start | bytes 196
  84.3 1.0 copy-start.7
  85.3 1.0 copy-start.9
  93.7 1.0 copy-start.11
  94.7 53.1 %all-to-all-start = ((bf16[4,4,4,128,128]{4,3,2,1,0:T(8,128)(2,1)}), bf16[4,4,4,128,128]{4,3,2,1,0:T(8,128)(2,1)}, u32[]{:S(2)}, u32[]{:S(2)}) async-start(bf16[4,4,4,128,128]{4,3,2,1,0:T(8,128)(2,1)} %pad_maximum_fusion), calls=%async_computation | async-start | bytes 4194304 | tf_op jit(solution)/shard_map/all_to_all | solution.py:31
  100.7 17.1 %collective-permute-start.12 = (bf16[4,4,128,128]{3,2,1,0:T(8,128)(2,1)}, bf16[4,4,128,128]{3,2,1,0:T(8,128)(2,1)}, u32[]{:S(2)}, u32[]{:S(2)}) collective-permute-start(bf16[4,4,128,128]{3,2,1,0:T(8,128)(2,1)} %get-tuple-element.27), channel_id=1, source_target_pairs={{0,1},{1,2},{2,3},{3,0},{4,5},{5,6},{6,7},{7,4},{8,9},{9,10},{10,1... | collective-permute-start | bytes 1572872 | tf_op jit(solution)/shard_map/ppermute | solution.py:21
  101.7 35.3 %collective-permute-start.13 = (bf16[4,4,128,128]{3,2,1,0:T(8,128)(2,1)}, bf16[4,4,128,128]{3,2,1,0:T(8,128)(2,1)}, u32[]{:S(2)}, u32[]{:S(2)}) collective-permute-start(bf16[4,4,128,128]{3,2,1,0:T(8,128)(2,1)} %get-tuple-element.28), channel_id=1, source_target_pairs={{0,2},{1,3},{2,0},{3,1},{4,6},{5,7},{6,4},{7,5},{8,10},{9,11},{10,... | collective-permute-start | bytes 1572872 | tf_op jit(solution)/shard_map/ppermute | solution.py:21
  103.1 33.9 %collective-permute-start.14 = (bf16[4,4,128,128]{3,2,1,0:T(8,128)(2,1)}, bf16[4,4,128,128]{3,2,1,0:T(8,128)(2,1)}, u32[]{:S(2)}, u32[]{:S(2)}) collective-permute-start(bf16[4,4,128,128]{3,2,1,0:T(8,128)(2,1)} %get-tuple-element.29), channel_id=1, source_target_pairs={{0,3},{1,0},{2,1},{3,2},{4,7},{5,4},{6,5},{7,6},{8,11},{9,8},{10,9... | collective-permute-start | bytes 1572872 | tf_op jit(solution)/shard_map/ppermute | solution.py:21
  106.8 1.6 copy-start
  108.4 1.6 copy-start.1
  110.0 1.2 copy-start.8
  111.2 1.2 copy-start.10
  112.5 1.2 copy-start.12
  147.0 0.8 copy-start.13
  147.8 4.6 %copy-start.14 = (bf16[512,512]{1,0:T(8,128)(2,1)S(1)}, bf16[512,512]{1,0:T(8,128)(2,1)}, u32[]{:S(2)}) copy-start(bf16[512,512]{1,0:T(8,128)(2,1)} %copy-done.13) | copy-start | bytes 1572868
  147.8 46.6 %all-to-all-start.2 = ((bf16[4,4,2,128,128]{4,3,2,1,0:T(8,128)(2,1)}), bf16[4,4,2,128,128]{4,3,2,1,0:T(8,128)(2,1)S(1)}, u32[]{:S(2)}, u32[]{:S(2)}) async-start(bf16[4,4,2,128,128]{4,3,2,1,0:T(8,128)(2,1)} %shard_map.107), calls=%async_computation.2 | async-start | bytes 2097152 | tf_op jit(solution)/shard_map/all_to_all | solution.py:31
  162.0 22.3 %collective-permute-start.11 = (bf16[4,2,128,128]{3,2,1,0:T(8,128)(2,1)S(1)}, bf16[4,2,128,128]{3,2,1,0:T(8,128)(2,1)S(1)}, u32[]{:S(2)}, u32[]{:S(2)}) collective-permute-start(bf16[4,2,128,128]{3,2,1,0:T(8,128)(2,1)S(1)} %get-tuple-element.42), channel_id=1, source_target_pairs={{0,1},{1,2},{2,3},{3,0},{4,5},{5,6},{6,7},{7,4},{8,9},{9,10},{10,1... | collective-permute-start | bytes 786440 | tf_op jit(solution)/shard_map/ppermute | solution.py:21
  174.1 19.2 %collective-permute-start.10 = (bf16[4,2,128,128]{3,2,1,0:T(8,128)(2,1)S(1)}, bf16[4,2,128,128]{3,2,1,0:T(8,128)(2,1)S(1)}, u32[]{:S(2)}, u32[]{:S(2)}) collective-permute-start(bf16[4,2,128,128]{3,2,1,0:T(8,128)(2,1)S(1)} %get-tuple-element.43), channel_id=1, source_target_pairs={{0,2},{1,3},{2,0},{3,1},{4,6},{5,7},{6,4},{7,5},{8,10},{9,11},{10,... | collective-permute-start | bytes 786440 | tf_op jit(solution)/shard_map/ppermute | solution.py:21
  177.5 15.8 %collective-permute-start.9 = (bf16[4,2,128,128]{3,2,1,0:T(8,128)(2,1)S(1)}, bf16[4,2,128,128]{3,2,1,0:T(8,128)(2,1)S(1)}, u32[]{:S(2)}, u32[]{:S(2)}) collective-permute-start(bf16[4,2,128,128]{3,2,1,0:T(8,128)(2,1)S(1)} %get-tuple-element.44), channel_id=1, source_target_pairs={{0,3},{1,0},{2,1},{3,2},{4,7},{5,4},{6,5},{7,6},{8,11},{9,8},{10,9... | collective-permute-start | bytes 786440 | tf_op jit(solution)/shard_map/ppermute | solution.py:21
  194.4 35.0 %all-to-all-start.3 = ((bf16[4,4,2,128,128]{4,3,2,1,0:T(8,128)(2,1)}), bf16[4,4,2,128,128]{4,3,2,1,0:T(8,128)(2,1)S(1)}, u32[]{:S(2)}, u32[]{:S(2)}) async-start(bf16[4,4,2,128,128]{4,3,2,1,0:T(8,128)(2,1)} %pad_maximum_fusion.1), calls=%async_computation.3 | async-start | bytes 2097152 | tf_op jit(solution)/shard_map/all_to_all | solution.py:31
  199.0 12.7 %collective-permute-start.15 = (bf16[4,2,128,128]{3,2,1,0:T(8,128)(2,1)S(1)}, bf16[4,2,128,128]{3,2,1,0:T(8,128)(2,1)S(1)}, u32[]{:S(2)}, u32[]{:S(2)}) collective-permute-start(bf16[4,2,128,128]{3,2,1,0:T(8,128)(2,1)S(1)} %get-tuple-element.31), channel_id=1, source_target_pairs={{0,3},{1,0},{2,1},{3,2},{4,7},{5,4},{6,5},{7,6},{8,11},{9,8},{10,9... | collective-permute-start | bytes 786440 | tf_op jit(solution)/shard_map/ppermute | solution.py:21
  205.0 24.4 %collective-permute-start.16 = (bf16[4,2,128,128]{3,2,1,0:T(8,128)(2,1)S(1)}, bf16[4,2,128,128]{3,2,1,0:T(8,128)(2,1)S(1)}, u32[]{:S(2)}, u32[]{:S(2)}) collective-permute-start(bf16[4,2,128,128]{3,2,1,0:T(8,128)(2,1)S(1)} %get-tuple-element.32), channel_id=1, source_target_pairs={{0,2},{1,3},{2,0},{3,1},{4,6},{5,7},{6,4},{7,5},{8,10},{9,11},{10,... | collective-permute-start | bytes 786440 | tf_op jit(solution)/shard_map/ppermute | solution.py:21
  206.6 22.8 %collective-permute-start.17 = (bf16[4,2,128,128]{3,2,1,0:T(8,128)(2,1)S(1)}, bf16[4,2,128,128]{3,2,1,0:T(8,128)(2,1)S(1)}, u32[]{:S(2)}, u32[]{:S(2)}) collective-permute-start(bf16[4,2,128,128]{3,2,1,0:T(8,128)(2,1)S(1)} %get-tuple-element.33), channel_id=1, source_target_pairs={{0,1},{1,2},{2,3},{3,0},{4,5},{5,6},{6,7},{7,4},{8,9},{9,10},{10,1... | collective-permute-start | bytes 786440 | tf_op jit(solution)/shard_map/ppermute | solution.py:21

commit v4 on v3

--- a/solution.py
+++ b/solution.py
@@ -251,7 +251,7 @@
     text_y = {0: text_z, 2: shift_y(text_z, 2), 1: shift_y(text_z, 1), 3: shift_y(text_z, 3)}
     text_own = project([text_y[s] for s in side], key_weight, value_weight)
 
-    second_z = {t: shift_z(after(second_y[:, t], first_z[t]), t) for t in steps}
+    second_z = {t: shift_z(second_y[:, t], t) for t in steps}
     first_y = swap_y(after(jnp.stack([first_z[t] for t in side], axis=1), *[text_y[s] for s in steps]))
 
     near = jnp.arange(SIDE, dtype=jnp.int32)
@@ -274,7 +274,7 @@
         [second_y] + [second_z[t] for t in steps],
         [pl.BlockSpec((SIDE, None, *piece), lambda i: (0, 0, 0, 0, 0))]
         + [pl.BlockSpec((SIDE, *piece), lambda i: (0, 0, 0, 0))] * (SIDE - 1),
-        text_own,
+        after(text_own, first_heads),
         bias,
         1,
     )
@@ -284,7 +284,7 @@
     second_back = swap_y(second_heads)
     second_home = {0: second_back[:, 0]}
     for t in steps:
-        second_home[t] = shift_z(after(second_back[:, t], first_back[t]), -t)
+        second_home[t] = shift_z(second_back[:, t], -t)
     first_home = swap_y(
         after(jnp.stack([first_back[t] for t in side], axis=1), second_back)
     )

time: 233 us -> 222 us (0.953)
  the two profiles are of different devices: /device:TPU:2 before, /device:TPU:43 now
where the time goes in v4:
time: 222 us; the launch traced here: 221 us
  waiting for transfers between devices  124 us (56%)
  starting transfers between devices  40.8 us (18%)
  Pallas kernels  26.9 us (12%)
  local copies, waits for them, and re-layouts  24.9 us (11%)
  other arithmetic  3.15 us (1%)
    ppermute x15, waiting for transfers between devices, shift_z(): return lax.ppermute(array, 'seq', pairs)  103 us
    unnamed x55, local copies, waits for them, and re-layouts  21.2 us
    all_to_all x4, starting transfers between devices, swap_y(): lax.all_to_all(array, 'seq', split_axis=0, concat_axis=0, axis_index_grou...  19.6 us
    pallas_call x2, Pallas kernels, attend(): pl.pallas_call(functools.partial(attend_kernel, head=head, blocks=4), gri...  19.5 us
    ppermute x15, starting transfers between devices, shift_z(): return lax.ppermute(array, 'seq', pairs)  17 us
    all_to_all x4, waiting for transfers between devices, swap_y(): lax.all_to_all(array, 'seq', split_axis=0, concat_axis=0, axis_index_grou...  11.1 us
    ppermute x3, waiting for transfers between devices, shift_y(): return lax.ppermute(array, 'seq', pairs)  9.38 us
  transfers between devices with their start and end apart: 22, of which 14 were waited for; matrix products, arithmetic and copies ran while one was open for 4% of the time, Pallas kernels for 7%

profile of v4, /device:TPU:43, one launch (start us, length us, event | category | flops | bytes accessed | tf_op | source)
XLA Modules:
  0.0 221.1 jit_solution(7289565490554428255)
XLA Ops:
  0.6 3.1 %collective-permute-start.2 = (bf16[32,4096]{1,0:T(8,128)(2,1)}, bf16[32,4096]{1,0:T(8,128)(2,1)}, u32[]{:S(2)}, u32[]{:S(2)}) collective-permute-start(bf16[32,4096]{1,0:T(8,128)(2,1)} %param.13), channel_id=1, source_target_pairs={{0,2},{1,3},{2,0},{3,1},{4,6},{5,7},{6,4},{7,5},{8,10},{9,11},{10,... | collective-permute-start | bytes 786440 | tf_op jit(solution)/shard_map/ppermute | solution.py:21
  3.7 1.5 collective-permute-start.4
  5.3 1.2 copy-done.3
  6.5 1.2 copy-done.4
  7.7 1.2 copy-done.5
  8.9 1.2 copy-done.6
  10.1 1.6 shard_map.104
  11.8 1.4 copy-done.2
  16.3 4.5 %all-to-all-start.1 = ((bf16[4,4,4,128,128]{4,3,2,1,0:T(8,128)(2,1)}), bf16[4,4,4,128,128]{4,3,2,1,0:T(8,128)(2,1)S(1)}, u32[]{:S(2)}, u32[]{:S(2)}) async-start(bf16[4,4,4,128,128]{4,3,2,1,0:T(8,128)(2,1)} %copy-done.2), calls=%async_computation.1 | async-start | bytes 4194304 | tf_op jit(solution)/shard_map/all_to_all | solution.py:31
  20.8 4.8 %collective-permute-done.4 = bf16[32,4096]{1,0:T(8,128)(2,1)} collective-permute-done((bf16[32,4096]{1,0:T(8,128)(2,1)}, bf16[32,4096]{1,0:T(8,128)(2,1)}, u32[]{:S(2)}, u32[]{:S(2)}) %collective-permute-start.4) | collective-permute-done | bytes 262176 | tf_op jit(solution)/shard_map/ppermute | solution.py:21
  25.6 12.1 %collective-permute-done = bf16[32,4096]{1,0:T(8,128)(2,1)} collective-permute-done((bf16[32,4096]{1,0:T(8,128)(2,1)}, bf16[32,4096]{1,0:T(8,128)(2,1)}, u32[]{:S(2)}, u32[]{:S(2)}) %collective-permute-start) | collective-permute-done | bytes 262176 | tf_op jit(solution)/shard_map/ppermute | solution.py:21
  38.7 1.0 constant_dynamic-update-slice_fusion.1
  39.6 1.0 constant_dynamic-update-slice_fusion.refs_0_
  40.9 2.3 %collective-permute-start.7 = (bf16[128,4096]{1,0:T(8,128)(2,1)S(1)}, bf16[128,4096]{1,0:T(8,128)(2,1)S(1)}, u32[]{:S(2)}, u32[]{:S(2)}) collective-permute-start(bf16[128,4096]{1,0:T(8,128)(2,1)S(1)} %constant_dynamic-update-slice_fusion.refs_0_), channel_id=1, source_target_pairs={{0,8},{1,9},{2,10},{3,11},{4,12},{5,13},{6,14},{7,15},{8,0},{9,1},... | collective-permute-start | bytes 3145736 | tf_op jit(solution)/shard_map/ppermute | solution.py:26
  43.2 1.6 collective-permute-start.6
  44.8 2.3 %collective-permute-start.1 = (bf16[4,4,128,128]{3,2,1,0:T(8,128)(2,1)S(1)}, bf16[4,4,128,128]{3,2,1,0:T(8,128)(2,1)S(1)}, u32[]{:S(2)}, u32[]{:S(2)}) collective-permute-start(bf16[4,4,128,128]{3,2,1,0:T(8,128)(2,1)S(1)} %copy-done.19), channel_id=1, source_target_pairs={{0,1},{1,2},{2,3},{3,0},{4,5},{5,6},{6,7},{7,4},{8,9},{9,10},{10,1... | collective-permute-start | bytes 1572872 | tf_op jit(solution)/shard_map/ppermute | solution.py:21
  47.1 19.1 %collective-permute-done.3 = bf16[4,4,128,128]{3,2,1,0:T(8,128)(2,1)S(1)} collective-permute-done((bf16[4,4,128,128]{3,2,1,0:T(8,128)(2,1)S(1)}, bf16[4,4,128,128]{3,2,1,0:T(8,128)(2,1)S(1)}, u32[]{:S(2)}, u32[]{:S(2)}) %collective-permute-start.3) | collective-permute-done | bytes 524320 | tf_op jit(solution)/shard_map/ppermute | solution.py:21
  66.2 11.2 %collective-permute-done.1 = bf16[4,4,128,128]{3,2,1,0:T(8,128)(2,1)S(1)} collective-permute-done((bf16[4,4,128,128]{3,2,1,0:T(8,128)(2,1)S(1)}, bf16[4,4,128,128]{3,2,1,0:T(8,128)(2,1)S(1)}, u32[]{:S(2)}, u32[]{:S(2)}) %collective-permute-start.1) | collective-permute-done | bytes 524320 | tf_op jit(solution)/shard_map/ppermute | solution.py:21
  77.4 1.6 pad_maximum_fusion
  79.0 1.0 copy-done.7
  80.0 9.4 %collective-permute-done.7.refs_2_ = bf16[128,4096]{1,0:T(8,128)(2,1)S(1)} collective-permute-done((bf16[128,4096]{1,0:T(8,128)(2,1)S(1)}, bf16[128,4096]{1,0:T(8,128)(2,1)S(1)}, u32[]{:S(2)}, u32[]{:S(2)}) %collective-permute-start.7) | collective-permute-done | bytes 1048608 | tf_op jit(solution)/shard_map/ppermute | solution.py:26
  91.4 6.7 %all-to-all-start = ((bf16[4,4,4,128,128]{4,3,2,1,0:T(8,128)(2,1)}), bf16[4,4,4,128,128]{4,3,2,1,0:T(8,128)(2,1)}, u32[]{:S(2)}, u32[]{:S(2)}) async-start(bf16[4,4,4,128,128]{4,3,2,1,0:T(8,128)(2,1)} %pad_maximum_fusion), calls=%async_computation | async-start | bytes 4194304 | tf_op jit(solution)/shard_map/all_to_all | solution.py:31
  99.2 1.2 slice_bitcast_fusion
  100.4 3.4 %collective-permute-start.13 = (bf16[4,4,128,128]{3,2,1,0:T(8,128)(2,1)}, bf16[4,4,128,128]{3,2,1,0:T(8,128)(2,1)}, u32[]{:S(2)}, u32[]{:S(2)}) collective-permute-start(bf16[4,4,128,128]{3,2,1,0:T(8,128)(2,1)} %get-tuple-element.25), channel_id=1, source_target_pairs={{0,2},{1,3},{2,0},{3,1},{4,6},{5,7},{6,4},{7,5},{8,10},{9,11},{10,... | collective-permute-start | bytes 1572872 | tf_op jit(solution)/shard_map/ppermute | solution.py:21
  103.8 1.6 copy-done.1
  105.4 1.2 copy-done.10
  106.6 1.2 copy-done.12
  107.8 3.4 %shard_map.105.refs_1_.refs_4_ = bf16[512,512]{1,0:T(8,128)(2,1)S(1)} custom-call(bf16[128,4096]{1,0:T(8,128)(2,1)S(1)} %constant_dynamic-update-slice_fusion.refs_0_, bf16[128,4096]{1,0:T(8,128)(2,1)S(1)} %copy-done.12, bf16[128,4096]{1,0:T(8,128)(2,1)S(1)} %copy-done.10, bf16[128,4096]{1,0:T(8,128)(2,1)S(1)} %copy-done.8, bf16[4096,256]{1,0:T(8,128)(2,1)S(1)} %copy-done, ...), custom_call_target="tpu_custom_call" | custom-call | flops 2147483648 | bytes 8388608 | tf_op jit(solution)/shard_map/pallas_call | solution.py:202
  112.0 11.1 %all-to-all-done.refs_0_ = bf16[4,4,4,128,128]{4,3,2,1,0:T(8,128)(2,1)} async-done(((bf16[4,4,4,128,128]{4,3,2,1,0:T(8,128)(2,1)}), bf16[4,4,4,128,128]{4,3,2,1,0:T(8,128)(2,1)}, u32[]{:S(2)}, u32[]{:S(2)}) %all-to-all-start) | async-done | bytes 2097184 | tf_op jit(solution)/shard_map/all_to_all | solution.py:31
  123.1 1.0 copy-done.14
  124.1 9.5 %shard_map.106 = bf16[4,4,2,128,128]{4,3,2,1,0:T(8,128)(2,1)S(1)} custom-call(bf16[4,4,4,128,128]{4,3,2,1,0:T(8,128)(2,1)} %all-to-all-done.refs_0_, bf16[512,512]{1,0:T(8,128)(2,1)S(1)} %copy-done.14, f32[1,512]{1,0:T(1,128)S(1)} %select_n.53.refs_2_.refs_5_), custom_call_target="tpu_custom_call" | custom-call | flops 5368709120 | bytes 3145728 | tf_op jit(solution)/shard_map/pallas_call | solution.py:150
  133.6 1.3 collective-permute-done.13.refs_2_
  134.9 11.2 %collective-permute-done.12.refs_1_ = bf16[4,4,128,128]{3,2,1,0:T(8,128)(2,1)} collective-permute-done((bf16[4,4,128,128]{3,2,1,0:T(8,128)(2,1)}, bf16[4,4,128,128]{3,2,1,0:T(8,128)(2,1)}, u32[]{:S(2)}, u32[]{:S(2)}) %collective-permute-start.12) | collective-permute-done | bytes 524320 | tf_op jit(solution)/shard_map/ppermute | solution.py:21
  146.2 10.0 %shard_map.107 = bf16[4,4,2,128,128]{4,3,2,1,0:T(8,128)(2,1)} custom-call(bf16[4,4,4,128,128]{4,3,2,1,0:T(8,128)(2,1)S(1)} %all-to-all-done.1.refs_0_, bf16[4,4,128,128]{3,2,1,0:T(8,128)(2,1)} %collective-permute-done.12.refs_1_, bf16[4,4,128,128]{3,2,1,0:T(8,128)(2,1)} %collective-permute-done.13.refs_2_, ...), custom_call_target="tpu_custom_call" | custom-call | flops 5368709120 | bytes 3145728 | tf_op jit(solution)/shard_map/pallas_call | solution.py:150
  156.2 4.2 %all-to-all-start.2 = ((bf16[4,4,2,128,128]{4,3,2,1,0:T(8,128)(2,1)}), bf16[4,4,2,128,128]{4,3,2,1,0:T(8,128)(2,1)S(1)}, u32[]{:S(2)}, u32[]{:S(2)}) async-start(bf16[4,4,2,128,128]{4,3,2,1,0:T(8,128)(2,1)} %shard_map.107), calls=%async_computation.2 | async-start | bytes 2097152 | tf_op jit(solution)/shard_map/all_to_all | solution.py:31
  160.5 2.3 %collective-permute-start.11 = (bf16[4,2,128,128]{3,2,1,0:T(8,128)(2,1)S(1)}, bf16[4,2,128,128]{3,2,1,0:T(8,128)(2,1)S(1)}, u32[]{:S(2)}, u32[]{:S(2)}) collective-permute-start(bf16[4,2,128,128]{3,2,1,0:T(8,128)(2,1)S(1)} %get-tuple-element.32), channel_id=1, source_target_pairs={{0,1},{1,2},{2,3},{3,0},{4,5},{5,6},{6,7},{7,4},{8,9},{9,10},{10,1... | collective-permute-start | bytes 786440 | tf_op jit(solution)/shard_map/ppermute | solution.py:21
  162.8 3.0 %collective-permute-start.10 = (bf16[4,2,128,128]{3,2,1,0:T(8,128)(2,1)S(1)}, bf16[4,2,128,128]{3,2,1,0:T(8,128)(2,1)S(1)}, u32[]{:S(2)}, u32[]{:S(2)}) collective-permute-start(bf16[4,2,128,128]{3,2,1,0:T(8,128)(2,1)S(1)} %get-tuple-element.33), channel_id=1, source_target_pairs={{0,2},{1,3},{2,0},{3,1},{4,6},{5,7},{6,4},{7,5},{8,10},{9,11},{10,... | collective-permute-start | bytes 786440 | tf_op jit(solution)/shard_map/ppermute | solution.py:21
  165.8 2.6 %collective-permute-done.11 = bf16[4,2,128,128]{3,2,1,0:T(8,128)(2,1)S(1)} collective-permute-done((bf16[4,2,128,128]{3,2,1,0:T(8,128)(2,1)S(1)}, bf16[4,2,128,128]{3,2,1,0:T(8,128)(2,1)S(1)}, u32[]{:S(2)}, u32[]{:S(2)}) %collective-permute-start.11) | collective-permute-done | bytes 262176 | tf_op jit(solution)/shard_map/ppermute | solution.py:21
  168.4 15.8 %collective-permute-done.10 = bf16[4,2,128,128]{3,2,1,0:T(8,128)(2,1)S(1)} collective-permute-done((bf16[4,2,128,128]{3,2,1,0:T(8,128)(2,1)S(1)}, bf16[4,2,128,128]{3,2,1,0:T(8,128)(2,1)S(1)}, u32[]{:S(2)}, u32[]{:S(2)}) %collective-permute-start.10) | collective-permute-done | bytes 262176 | tf_op jit(solution)/shard_map/ppermute | solution.py:21
  184.2 3.6 %collective-permute-done.9 = bf16[4,2,128,128]{3,2,1,0:T(8,128)(2,1)S(1)} collective-permute-done((bf16[4,2,128,128]{3,2,1,0:T(8,128)(2,1)S(1)}, bf16[4,2,128,128]{3,2,1,0:T(8,128)(2,1)S(1)}, u32[]{:S(2)}, u32[]{:S(2)}) %collective-permute-start.9) | collective-permute-done | bytes 262176 | tf_op jit(solution)/shard_map/ppermute | solution.py:21
  187.8 1.1 pad_maximum_fusion.1
  189.9 4.2 %all-to-all-start.3 = ((bf16[4,4,2,128,128]{4,3,2,1,0:T(8,128)(2,1)}), bf16[4,4,2,128,128]{4,3,2,1,0:T(8,128)(2,1)S(1)}, u32[]{:S(2)}, u32[]{:S(2)}) async-start(bf16[4,4,2,128,128]{4,3,2,1,0:T(8,128)(2,1)} %pad_maximum_fusion.1), calls=%async_computation.3 | async-start | bytes 2097152 | tf_op jit(solution)/shard_map/all_to_all | solution.py:31
  194.1 1.3 slice_bitcast_fusion.3
  195.6 1.4 collective-permute-start.15
  197.0 4.4 %collective-permute-done.17.refs_4_ = bf16[4,2,128,128]{3,2,1,0:T(8,128)(2,1)S(1)} collective-permute-done((bf16[4,2,128,128]{3,2,1,0:T(8,128)(2,1)S(1)}, bf16[4,2,128,128]{3,2,1,0:T(8,128)(2,1)S(1)}, u32[]{:S(2)}, u32[]{:S(2)}) %collective-permute-start.17) | collective-permute-done | bytes 262176 | tf_op jit(solution)/shard_map/ppermute | solution.py:21
  201.4 14.9 %collective-permute-done.16.refs_3_ = bf16[4,2,128,128]{3,2,1,0:T(8,128)(2,1)S(1)} collective-permute-done((bf16[4,2,128,128]{3,2,1,0:T(8,128)(2,1)S(1)}, bf16[4,2,128,128]{3,2,1,0:T(8,128)(2,1)S(1)}, u32[]{:S(2)}, u32[]{:S(2)}) %collective-permute-start.16) | collective-permute-done | bytes 262176 | tf_op jit(solution)/shard_map/ppermute | solution.py:21
  216.3 2.3 %collective-permute-done.15.refs_2_ = bf16[4,2,128,128]{3,2,1,0:T(8,128)(2,1)S(1)} collective-permute-done((bf16[4,2,128,128]{3,2,1,0:T(8,128)(2,1)S(1)}, bf16[4,2,128,128]{3,2,1,0:T(8,128)(2,1)S(1)}, u32[]{:S(2)}, u32[]{:S(2)}) %collective-permute-start.15) | collective-permute-done | bytes 262176 | tf_op jit(solution)/shard_map/ppermute | solution.py:21
  218.6 2.5 %shard_map.108 = (bf16[128,4096]{1,0:T(8,128)(2,1)}, bf16[128,4096]{1,0:T(8,128)(2,1)}) custom-call(s32[2]{0:T(128)S(1)} %pad_add_fusion.place_ref, bf16[4,4,2,128,128]{4,3,2,1,0:T(8,128)(2,1)S(1)} %all-to-all-done.3.refs_0_, bf16[4,2,128,128]{3,2,1,0:T(8,128)(2,1)S(1)} %get-tuple-element.30.refs_1_, ...), custom_call_target="tpu_custom_call" | custom-call | bytes 4194304 | tf_op jit(solution)/shard_map/pallas_call | solution.py:86
  (69 shorter events, 9.0 us)
Async XLA Ops:
  0.6 38.0 %collective-permute-start.2 = (bf16[32,4096]{1,0:T(8,128)(2,1)}, bf16[32,4096]{1,0:T(8,128)(2,1)}, u32[]{:S(2)}, u32[]{:S(2)}) collective-permute-start(bf16[32,4096]{1,0:T(8,128)(2,1)} %param.13), channel_id=1, source_target_pairs={{0,2},{1,3},{2,0},{3,1},{4,6},{5,7},{6,4},{7,5},{8,10},{9,11},{10,... | collective-permute-start | bytes 786440 | tf_op jit(solution)/shard_map/ppermute | solution.py:21
  3.7 34.0 %collective-permute-start = (bf16[32,4096]{1,0:T(8,128)(2,1)}, bf16[32,4096]{1,0:T(8,128)(2,1)}, u32[]{:S(2)}, u32[]{:S(2)}) collective-permute-start(bf16[32,4096]{1,0:T(8,128)(2,1)} %param.13), channel_id=1, source_target_pairs={{0,1},{1,2},{2,3},{3,0},{4,5},{5,6},{6,7},{7,4},{8,9},{9,10},{10,1... | collective-permute-start | bytes 786440 | tf_op jit(solution)/shard_map/ppermute | solution.py:21
  3.7 21.9 %collective-permute-start.4 = (bf16[32,4096]{1,0:T(8,128)(2,1)}, bf16[32,4096]{1,0:T(8,128)(2,1)}, u32[]{:S(2)}, u32[]{:S(2)}) collective-permute-start(bf16[32,4096]{1,0:T(8,128)(2,1)} %param.13), channel_id=1, source_target_pairs={{0,3},{1,0},{2,1},{3,2},{4,7},{5,4},{6,5},{7,6},{8,11},{9,8},{10,9... | collective-permute-start | bytes 786440 | tf_op jit(solution)/shard_map/ppermute | solution.py:21
  5.2 1.2 copy-start.3
  6.5 1.2 copy-start.4
  7.7 1.2 copy-start.5
  8.9 1.2 copy-start.6
  11.8 1.4 copy-start.2
  13.1 0.8 copy-start.16
  13.9 0.8 copy-start.18
  14.7 0.8 copy-start.20
  15.5 0.8 copy-start.22
  16.3 4.5 %copy-start.24 = (bf16[32,4096]{1,0:T(8,128)(2,1)S(1)}, bf16[32,4096]{1,0:T(8,128)(2,1)}, u32[]{:S(2)}) copy-start(bf16[32,4096]{1,0:T(8,128)(2,1)} %param.13) | copy-start | bytes 786436
  16.3 75.0 %all-to-all-start.1 = ((bf16[4,4,4,128,128]{4,3,2,1,0:T(8,128)(2,1)}), bf16[4,4,4,128,128]{4,3,2,1,0:T(8,128)(2,1)S(1)}, u32[]{:S(2)}, u32[]{:S(2)}) async-start(bf16[4,4,4,128,128]{4,3,2,1,0:T(8,128)(2,1)} %copy-done.2), calls=%async_computation.1 | async-start | bytes 4194304 | tf_op jit(solution)/shard_map/all_to_all | solution.py:31
  20.8 24.0 %copy-start.21 = (bf16[4,4,128,128]{3,2,1,0:T(8,128)(2,1)S(1)}, bf16[4,4,128,128]{3,2,1,0:T(8,128)(2,1)}, u32[]{:S(2)}) copy-start(bf16[4,4,128,128]{3,2,1,0:T(8,128)(2,1)} %copy-done.20) | copy-start | bytes 1572868
  20.8 24.0 %copy-start.19 = (bf16[4,4,128,128]{3,2,1,0:T(8,128)(2,1)S(1)}, bf16[4,4,128,128]{3,2,1,0:T(8,128)(2,1)}, u32[]{:S(2)}) copy-start(bf16[4,4,128,128]{3,2,1,0:T(8,128)(2,1)} %copy-done.18) | copy-start | bytes 1572868
  20.8 56.6 %copy-start.17 = (bf16[4,4,128,128]{3,2,1,0:T(8,128)(2,1)S(1)}, bf16[4,4,128,128]{3,2,1,0:T(8,128)(2,1)}, u32[]{:S(2)}) copy-start(bf16[4,4,128,128]{3,2,1,0:T(8,128)(2,1)} %copy-done.16) | copy-start | bytes 1572868
  25.6 19.2 %collective-permute-start.5 = (bf16[4,4,128,128]{3,2,1,0:T(8,128)(2,1)}, bf16[4,4,128,128]{3,2,1,0:T(8,128)(2,1)S(1)}, u32[]{:S(2)}, u32[]{:S(2)}) collective-permute-start(bf16[4,4,128,128]{3,2,1,0:T(8,128)(2,1)} %copy-done.22), channel_id=1, source_target_pairs={{0,3},{1,0},{2,1},{3,2},{4,7},{5,4},{6,5},{7,6},{8,11},{9,8},{10,9... | collective-permute-start | bytes 1572872 | tf_op jit(solution)/shard_map/ppermute | solution.py:21
  40.6 38.4 %collective-permute-start.8 = (bf16[128,4096]{1,0:T(8,128)(2,1)S(1)}, bf16[128,4096]{1,0:T(8,128)(2,1)S(1)}, u32[]{:S(2)}, u32[]{:S(2)}) collective-permute-start(bf16[128,4096]{1,0:T(8,128)(2,1)S(1)} %constant_dynamic-update-slice_fusion.refs_0_), channel_id=1, source_target_pairs={{0,12},{1,13},{2,14},{3,15},{4,0},{5,1},{6,2},{7,3},{8,4},{9,5},{1... | collective-permute-start | bytes 3145736 | tf_op jit(solution)/shard_map/ppermute | solution.py:26
  40.9 48.6 %collective-permute-start.7 = (bf16[128,4096]{1,0:T(8,128)(2,1)S(1)}, bf16[128,4096]{1,0:T(8,128)(2,1)S(1)}, u32[]{:S(2)}, u32[]{:S(2)}) collective-permute-start(bf16[128,4096]{1,0:T(8,128)(2,1)S(1)} %constant_dynamic-update-slice_fusion.refs_0_), channel_id=1, source_target_pairs={{0,8},{1,9},{2,10},{3,11},{4,12},{5,13},{6,14},{7,15},{8,0},{9,1},... | collective-permute-start | bytes 3145736 | tf_op jit(solution)/shard_map/ppermute | solution.py:26
  43.2 47.2 %collective-permute-start.6 = (bf16[128,4096]{1,0:T(8,128)(2,1)S(1)}, bf16[128,4096]{1,0:T(8,128)(2,1)S(1)}, u32[]{:S(2)}, u32[]{:S(2)}) collective-permute-start(bf16[128,4096]{1,0:T(8,128)(2,1)S(1)} %constant_dynamic-update-slice_fusion.refs_0_), channel_id=1, source_target_pairs={{0,4},{1,5},{2,6},{3,7},{4,8},{5,9},{6,10},{7,11},{8,12},{9,13},{1... | collective-permute-start | bytes 3145736 | tf_op jit(solution)/shard_map/ppermute | solution.py:26
  44.8 21.4 %collective-permute-start.3 = (bf16[4,4,128,128]{3,2,1,0:T(8,128)(2,1)S(1)}, bf16[4,4,128,128]{3,2,1,0:T(8,128)(2,1)S(1)}, u32[]{:S(2)}, u32[]{:S(2)}) collective-permute-start(bf16[4,4,128,128]{3,2,1,0:T(8,128)(2,1)S(1)} %copy-done.21), channel_id=1, source_target_pairs={{0,2},{1,3},{2,0},{3,1},{4,6},{5,7},{6,4},{7,5},{8,10},{9,11},{10,... | collective-permute-start | bytes 1572872 | tf_op jit(solution)/shard_map/ppermute | solution.py:21
  44.8 32.6 %collective-permute-start.1 = (bf16[4,4,128,128]{3,2,1,0:T(8,128)(2,1)S(1)}, bf16[4,4,128,128]{3,2,1,0:T(8,128)(2,1)S(1)}, u32[]{:S(2)}, u32[]{:S(2)}) collective-permute-start(bf16[4,4,128,128]{3,2,1,0:T(8,128)(2,1)S(1)} %copy-done.19), channel_id=1, source_target_pairs={{0,1},{1,2},{2,3},{3,0},{4,5},{5,6},{6,7},{7,4},{8,9},{9,10},{10,1... | collective-permute-start | bytes 1572872 | tf_op jit(solution)/shard_map/ppermute | solution.py:21
  79.0 19.7 %copy-start.25 = (s32[16]{0:T(128)S(1)}, s32[16]{0:T(128)}, u32[]{:S(2)}) copy-start(s32[16]{0:T(128)} %param.14) | copy-start | bytes 196
  79.0 1.0 copy-start.7
  89.4 1.0 copy-start.9
  90.4 1.0 copy-start.11
  91.4 31.7 %all-to-all-start = ((bf16[4,4,4,128,128]{4,3,2,1,0:T(8,128)(2,1)}), bf16[4,4,4,128,128]{4,3,2,1,0:T(8,128)(2,1)}, u32[]{:S(2)}, u32[]{:S(2)}) async-start(bf16[4,4,4,128,128]{4,3,2,1,0:T(8,128)(2,1)} %pad_maximum_fusion), calls=%async_computation | async-start | bytes 4194304 | tf_op jit(solution)/shard_map/all_to_all | solution.py:31
  99.2 4.6 %copy-start = (bf16[4096,256]{1,0:T(8,128)(2,1)S(1)}, bf16[4096,256]{1,0:T(8,128)(2,1)}, u32[]{:S(2)}) copy-start(bf16[4096,256]{1,0:T(8,128)(2,1)} %refs_4_.1) | copy-start | bytes 6291460
  99.2 4.6 %copy-start.8 = (bf16[128,4096]{1,0:T(8,128)(2,1)S(1)}, bf16[128,4096]{1,0:T(8,128)(2,1)}, u32[]{:S(2)}) copy-start(bf16[128,4096]{1,0:T(8,128)(2,1)} %copy-done.7) | copy-start | bytes 3145732
  100.4 33.2 %collective-permute-start.14 = (bf16[4,4,128,128]{3,2,1,0:T(8,128)(2,1)}, bf16[4,4,128,128]{3,2,1,0:T(8,128)(2,1)}, u32[]{:S(2)}, u32[]{:S(2)}) collective-permute-start(bf16[4,4,128,128]{3,2,1,0:T(8,128)(2,1)} %get-tuple-element.24), channel_id=1, source_target_pairs={{0,3},{1,0},{2,1},{3,2},{4,7},{5,4},{6,5},{7,6},{8,11},{9,8},{10,9... | collective-permute-start | bytes 1572872 | tf_op jit(solution)/shard_map/ppermute | solution.py:21
  100.4 34.5 %collective-permute-start.13 = (bf16[4,4,128,128]{3,2,1,0:T(8,128)(2,1)}, bf16[4,4,128,128]{3,2,1,0:T(8,128)(2,1)}, u32[]{:S(2)}, u32[]{:S(2)}) collective-permute-start(bf16[4,4,128,128]{3,2,1,0:T(8,128)(2,1)} %get-tuple-element.25), channel_id=1, source_target_pairs={{0,2},{1,3},{2,0},{3,1},{4,6},{5,7},{6,4},{7,5},{8,10},{9,11},{10,... | collective-permute-start | bytes 1572872 | tf_op jit(solution)/shard_map/ppermute | solution.py:21
  103.8 42.4 %collective-permute-start.12 = (bf16[4,4,128,128]{3,2,1,0:T(8,128)(2,1)}, bf16[4,4,128,128]{3,2,1,0:T(8,128)(2,1)}, u32[]{:S(2)}, u32[]{:S(2)}) collective-permute-start(bf16[4,4,128,128]{3,2,1,0:T(8,128)(2,1)} %get-tuple-element.26), channel_id=1, source_target_pairs={{0,1},{1,2},{2,3},{3,0},{4,5},{5,6},{6,7},{7,4},{8,9},{9,10},{10,1... | collective-permute-start | bytes 1572872 | tf_op jit(solution)/shard_map/ppermute | solution.py:21
  103.8 1.6 copy-start.1
  105.4 1.2 copy-start.10
  106.6 1.2 copy-start.12
  111.2 0.8 copy-start.13
  123.1 1.0 copy-start.14
  124.1 22.0 %copy-start.15 = (bf16[512,512]{1,0:T(8,128)(2,1)S(1)}, bf16[512,512]{1,0:T(8,128)(2,1)}, u32[]{:S(2)}) copy-start(bf16[512,512]{1,0:T(8,128)(2,1)} %copy-done.13) | copy-start | bytes 1572868
  156.2 32.7 %all-to-all-start.2 = ((bf16[4,4,2,128,128]{4,3,2,1,0:T(8,128)(2,1)}), bf16[4,4,2,128,128]{4,3,2,1,0:T(8,128)(2,1)S(1)}, u32[]{:S(2)}, u32[]{:S(2)}) async-start(bf16[4,4,2,128,128]{4,3,2,1,0:T(8,128)(2,1)} %shard_map.107), calls=%async_computation.2 | async-start | bytes 2097152 | tf_op jit(solution)/shard_map/all_to_all | solution.py:31
  160.5 7.9 %collective-permute-start.11 = (bf16[4,2,128,128]{3,2,1,0:T(8,128)(2,1)S(1)}, bf16[4,2,128,128]{3,2,1,0:T(8,128)(2,1)S(1)}, u32[]{:S(2)}, u32[]{:S(2)}) collective-permute-start(bf16[4,2,128,128]{3,2,1,0:T(8,128)(2,1)S(1)} %get-tuple-element.32), channel_id=1, source_target_pairs={{0,1},{1,2},{2,3},{3,0},{4,5},{5,6},{6,7},{7,4},{8,9},{9,10},{10,1... | collective-permute-start | bytes 786440 | tf_op jit(solution)/shard_map/ppermute | solution.py:21
  162.8 21.4 %collective-permute-start.10 = (bf16[4,2,128,128]{3,2,1,0:T(8,128)(2,1)S(1)}, bf16[4,2,128,128]{3,2,1,0:T(8,128)(2,1)S(1)}, u32[]{:S(2)}, u32[]{:S(2)}) collective-permute-start(bf16[4,2,128,128]{3,2,1,0:T(8,128)(2,1)S(1)} %get-tuple-element.33), channel_id=1, source_target_pairs={{0,2},{1,3},{2,0},{3,1},{4,6},{5,7},{6,4},{7,5},{8,10},{9,11},{10,... | collective-permute-start | bytes 786440 | tf_op jit(solution)/shard_map/ppermute | solution.py:21
  165.8 22.0 %collective-permute-start.9 = (bf16[4,2,128,128]{3,2,1,0:T(8,128)(2,1)S(1)}, bf16[4,2,128,128]{3,2,1,0:T(8,128)(2,1)S(1)}, u32[]{:S(2)}, u32[]{:S(2)}) collective-permute-start(bf16[4,2,128,128]{3,2,1,0:T(8,128)(2,1)S(1)} %get-tuple-element.34), channel_id=1, source_target_pairs={{0,3},{1,0},{2,1},{3,2},{4,7},{5,4},{6,5},{7,6},{8,11},{9,8},{10,9... | collective-permute-start | bytes 786440 | tf_op jit(solution)/shard_map/ppermute | solution.py:21
  188.9 1.0 copy-start.23
  189.9 28.7 %all-to-all-start.3 = ((bf16[4,4,2,128,128]{4,3,2,1,0:T(8,128)(2,1)}), bf16[4,4,2,128,128]{4,3,2,1,0:T(8,128)(2,1)S(1)}, u32[]{:S(2)}, u32[]{:S(2)}) async-start(bf16[4,4,2,128,128]{4,3,2,1,0:T(8,128)(2,1)} %pad_maximum_fusion.1), calls=%async_computation.3 | async-start | bytes 2097152 | tf_op jit(solution)/shard_map/all_to_all | solution.py:31
  195.4 6.0 %collective-permute-start.17 = (bf16[4,2,128,128]{3,2,1,0:T(8,128)(2,1)S(1)}, bf16[4,2,128,128]{3,2,1,0:T(8,128)(2,1)S(1)}, u32[]{:S(2)}, u32[]{:S(2)}) collective-permute-start(bf16[4,2,128,128]{3,2,1,0:T(8,128)(2,1)S(1)} %get-tuple-element.27), channel_id=1, source_target_pairs={{0,1},{1,2},{2,3},{3,0},{4,5},{5,6},{6,7},{7,4},{8,9},{9,10},{10,1... | collective-permute-start | bytes 786440 | tf_op jit(solution)/shard_map/ppermute | solution.py:21
  195.5 20.8 %collective-permute-start.16 = (bf16[4,2,128,128]{3,2,1,0:T(8,128)(2,1)S(1)}, bf16[4,2,128,128]{3,2,1,0:T(8,128)(2,1)S(1)}, u32[]{:S(2)}, u32[]{:S(2)}) collective-permute-start(bf16[4,2,128,128]{3,2,1,0:T(8,128)(2,1)S(1)} %get-tuple-element.28), channel_id=1, source_target_pairs={{0,2},{1,3},{2,0},{3,1},{4,6},{5,7},{6,4},{7,5},{8,10},{9,11},{10,... | collective-permute-start | bytes 786440 | tf_op jit(solution)/shard_map/ppermute | solution.py:21
  195.6 23.0 %collective-permute-start.15 = (bf16[4,2,128,128]{3,2,1,0:T(8,128)(2,1)S(1)}, bf16[4,2,128,128]{3,2,1,0:T(8,128)(2,1)S(1)}, u32[]{:S(2)}, u32[]{:S(2)}) collective-permute-start(bf16[4,2,128,128]{3,2,1,0:T(8,128)(2,1)S(1)} %get-tuple-element.29), channel_id=1, source_target_pairs={{0,3},{1,0},{2,1},{3,2},{4,7},{5,4},{6,5},{7,6},{8,11},{9,8},{10,9... | collective-permute-start | bytes 786440 | tf_op jit(solution)/shard_map/ppermute | solution.py:21

commit v5 on v4

--- a/solution.py
+++ b/solution.py
@@ -248,11 +248,12 @@
     for t in steps:
         first_z[t] = shift_z(after(first[t], text_from[t]), t)
 
-    text_y = {0: text_z, 2: shift_y(text_z, 2), 1: shift_y(text_z, 1), 3: shift_y(text_z, 3)}
+    text_y = {0: text_z, 1: shift_y(text_z, 1), 3: shift_y(text_z, 3)}
+    text_y[2] = shift_y(after(text_z, second_y), 2)
     text_own = project([text_y[s] for s in side], key_weight, value_weight)
 
     second_z = {t: shift_z(second_y[:, t], t) for t in steps}
-    first_y = swap_y(after(jnp.stack([first_z[t] for t in side], axis=1), *[text_y[s] for s in steps]))
+    first_y = swap_y(after(jnp.stack([first_z[t] for t in side], axis=1), text_y[1], text_y[3]))
 
     near = jnp.arange(SIDE, dtype=jnp.int32)
     holder = ((y - near) % SIDE * SIDE)[:, None] + ((z - near) % SIDE)[None, :]

time: 222 us -> 229 us (1.032)
  the two profiles are of different devices: /device:TPU:43 before, /device:TPU:2 now
where the time goes in v5:
time: 229 us; the launch traced here: 227 us
  waiting for transfers between devices  122 us (53%)
  starting transfers between devices  50.3 us (22%)
  Pallas kernels  28 us (12%)
  local copies, waits for them, and re-layouts  22.6 us (10%)
  other arithmetic  3.14 us (1%)
    ppermute x15, waiting for transfers between devices, shift_z(): return lax.ppermute(array, 'seq', pairs)  84.3 us
    ppermute x3, waiting for transfers between devices, shift_y(): return lax.ppermute(array, 'seq', pairs)  37.7 us
    ppermute x15, starting transfers between devices, shift_z(): return lax.ppermute(array, 'seq', pairs)  26.3 us
    pallas_call x2, Pallas kernels, attend(): pl.pallas_call(functools.partial(attend_kernel, head=head, blocks=4), gri...  19.5 us
    unnamed x53, local copies, waits for them, and re-layouts  19 us
    all_to_all x4, starting transfers between devices, swap_y(): lax.all_to_all(array, 'seq', split_axis=0, concat_axis=0, axis_index_grou...  17 us
    ppermute x3, starting transfers between devices, shift_y(): return lax.ppermute(array, 'seq', pairs)  6.89 us
  transfers between devices with their start and end apart: 22, of which 9 were waited for; matrix products, arithmetic and copies ran while one was open for 4% of the time, Pallas kernels for 7%

profile of v5, /device:TPU:2, one launch (start us, length us, event | category | flops | bytes accessed | tf_op | source)
XLA Modules:
  0.0 227.5 jit_solution(7284548752975235454)
XLA Ops:
  0.6 4.7 %collective-permute-start.4 = (bf16[32,4096]{1,0:T(8,128)(2,1)}, bf16[32,4096]{1,0:T(8,128)(2,1)}, u32[]{:S(2)}, u32[]{:S(2)}) collective-permute-start(bf16[32,4096]{1,0:T(8,128)(2,1)} %param.13), channel_id=1, source_target_pairs={{0,3},{1,0},{2,1},{3,2},{4,7},{5,4},{6,5},{7,6},{8,11},{9,8},{10,9... | collective-permute-start | bytes 786440 | tf_op jit(solution)/shard_map/ppermute | solution.py:21
  6.1 1.2 copy-done.3
  7.3 1.2 copy-done.4
  8.5 1.2 copy-done.5
  9.8 1.2 copy-done.6
  11.0 1.6 shard_map.104
  12.6 1.3 copy-done.2
  14.8 0.8 copy-done.16
  15.6 0.8 copy-done.18
  17.1 4.6 %all-to-all-start.1 = ((bf16[4,4,4,128,128]{4,3,2,1,0:T(8,128)(2,1)}), bf16[4,4,4,128,128]{4,3,2,1,0:T(8,128)(2,1)S(1)}, u32[]{:S(2)}, u32[]{:S(2)}) async-start(bf16[4,4,4,128,128]{4,3,2,1,0:T(8,128)(2,1)} %copy-done.2), calls=%async_computation.1 | async-start | bytes 4194304 | tf_op jit(solution)/shard_map/all_to_all | solution.py:31
  21.8 1.5 collective-permute-done
  23.3 1.0 constant_dynamic-update-slice_fusion.2
  24.3 3.2 %collective-permute-done.2 = bf16[32,4096]{1,0:T(8,128)(2,1)} collective-permute-done((bf16[32,4096]{1,0:T(8,128)(2,1)}, bf16[32,4096]{1,0:T(8,128)(2,1)}, u32[]{:S(2)}, u32[]{:S(2)}) %collective-permute-start.2) | collective-permute-done | bytes 262176 | tf_op jit(solution)/shard_map/ppermute | solution.py:21
  27.5 1.0 constant_dynamic-update-slice_fusion.1
  28.4 1.0 constant_dynamic-update-slice_fusion.refs_0_
  29.4 1.7 collective-permute-start.6
  31.1 1.7 collective-permute-start.7
  32.7 4.3 %collective-permute-start.3 = (bf16[4,4,128,128]{3,2,1,0:T(8,128)(2,1)S(1)}, bf16[4,4,128,128]{3,2,1,0:T(8,128)(2,1)S(1)}, u32[]{:S(2)}, u32[]{:S(2)}) collective-permute-start(bf16[4,4,128,128]{3,2,1,0:T(8,128)(2,1)S(1)} %copy-done.19), channel_id=1, source_target_pairs={{0,2},{1,3},{2,0},{3,1},{4,6},{5,7},{6,4},{7,5},{8,10},{9,11},{10,... | collective-permute-start | bytes 1572872 | tf_op jit(solution)/shard_map/ppermute | solution.py:21
  37.0 1.9 collective-permute-start.1
  39.0 7.0 %collective-permute-done.5 = bf16[4,4,128,128]{3,2,1,0:T(8,128)(2,1)S(1)} collective-permute-done((bf16[4,4,128,128]{3,2,1,0:T(8,128)(2,1)S(1)}, bf16[4,4,128,128]{3,2,1,0:T(8,128)(2,1)S(1)}, u32[]{:S(2)}, u32[]{:S(2)}) %collective-permute-start.5) | collective-permute-done | bytes 524320 | tf_op jit(solution)/shard_map/ppermute | solution.py:21
  46.0 35.6 %collective-permute-done.3 = bf16[4,4,128,128]{3,2,1,0:T(8,128)(2,1)S(1)} collective-permute-done((bf16[4,4,128,128]{3,2,1,0:T(8,128)(2,1)S(1)}, bf16[4,4,128,128]{3,2,1,0:T(8,128)(2,1)S(1)}, u32[]{:S(2)}, u32[]{:S(2)}) %collective-permute-start.3) | collective-permute-done | bytes 524320 | tf_op jit(solution)/shard_map/ppermute | solution.py:21
  81.5 1.6 pad_maximum_fusion
  83.1 1.0 copy-done.7
  84.1 1.0 copy-done.9
  85.1 4.4 %all-to-all-start = ((bf16[4,4,4,128,128]{4,3,2,1,0:T(8,128)(2,1)}), bf16[4,4,4,128,128]{4,3,2,1,0:T(8,128)(2,1)}, u32[]{:S(2)}, u32[]{:S(2)}) async-start(bf16[4,4,4,128,128]{4,3,2,1,0:T(8,128)(2,1)} %pad_maximum_fusion), calls=%async_computation | async-start | bytes 4194304 | tf_op jit(solution)/shard_map/all_to_all | solution.py:31
  90.2 3.6 %collective-permute-start.8 = (bf16[128,4096]{1,0:T(8,128)(2,1)S(1)}, bf16[128,4096]{1,0:T(8,128)(2,1)}, u32[]{:S(2)}, u32[]{:S(2)}) collective-permute-start(bf16[128,4096]{1,0:T(8,128)(2,1)S(1)} %constant_dynamic-update-slice_fusion.refs_0_), channel_id=1, source_target_pairs={{0,8},{1,9},{2,10},{3,11},{4,12},{5,13},{6,14},{7,15},{8,0},{9,1},... | collective-permute-start | bytes 3145736 | tf_op jit(solution)/shard_map/ppermute | solution.py:26
  94.2 1.2 slice_bitcast_fusion
  95.5 3.8 %collective-permute-start.14 = (bf16[4,4,128,128]{3,2,1,0:T(8,128)(2,1)}, bf16[4,4,128,128]{3,2,1,0:T(8,128)(2,1)}, u32[]{:S(2)}, u32[]{:S(2)}) collective-permute-start(bf16[4,4,128,128]{3,2,1,0:T(8,128)(2,1)} %get-tuple-element.26), channel_id=1, source_target_pairs={{0,3},{1,0},{2,1},{3,2},{4,7},{5,4},{6,5},{7,6},{8,11},{9,8},{10,9... | collective-permute-start | bytes 1572872 | tf_op jit(solution)/shard_map/ppermute | solution.py:21
  99.3 37.7 %collective-permute-done.8.refs_2_ = bf16[128,4096]{1,0:T(8,128)(2,1)} collective-permute-done((bf16[128,4096]{1,0:T(8,128)(2,1)S(1)}, bf16[128,4096]{1,0:T(8,128)(2,1)}, u32[]{:S(2)}, u32[]{:S(2)}) %collective-permute-start.8) | collective-permute-done | bytes 1048608 | tf_op jit(solution)/shard_map/ppermute | solution.py:26
  137.0 1.6 copy-done.1
  138.6 1.2 copy-done.10
  139.8 4.4 %shard_map.105.refs_1_.refs_4_ = bf16[512,512]{1,0:T(8,128)(2,1)S(1)} custom-call(bf16[128,4096]{1,0:T(8,128)(2,1)S(1)} %constant_dynamic-update-slice_fusion.refs_0_, bf16[128,4096]{1,0:T(8,128)(2,1)S(1)} %copy-done.8, bf16[128,4096]{1,0:T(8,128)(2,1)} %collective-permute-done.8.refs_2_, bf16[128,4096]{1,0:T(8,128)(2,1)S(1)} %copy-done.10, ...), custom_call_target="tpu_custom_call" | custom-call | flops 2147483648 | bytes 8388608 | tf_op jit(solution)/shard_map/pallas_call | solution.py:202
  145.0 1.0 copy-done.12
  146.0 9.5 %shard_map.106 = bf16[4,4,2,128,128]{4,3,2,1,0:T(8,128)(2,1)S(1)} custom-call(bf16[4,4,4,128,128]{4,3,2,1,0:T(8,128)(2,1)} %all-to-all-done.refs_0_, bf16[512,512]{1,0:T(8,128)(2,1)S(1)} %copy-done.12, f32[1,512]{1,0:T(1,128)S(1)} %select_n.53.refs_2_.refs_5_), custom_call_target="tpu_custom_call" | custom-call | flops 5368709120 | bytes 3145728 | tf_op jit(solution)/shard_map/pallas_call | solution.py:150
  155.5 10.0 %shard_map.107 = bf16[4,4,2,128,128]{4,3,2,1,0:T(8,128)(2,1)} custom-call(bf16[4,4,4,128,128]{4,3,2,1,0:T(8,128)(2,1)S(1)} %all-to-all-done.1.refs_0_, bf16[4,4,128,128]{3,2,1,0:T(8,128)(2,1)} %collective-permute-done.12.refs_1_, bf16[4,4,128,128]{3,2,1,0:T(8,128)(2,1)} %collective-permute-done.13.refs_2_, ...), custom_call_target="tpu_custom_call" | custom-call | flops 5368709120 | bytes 3145728 | tf_op jit(solution)/shard_map/pallas_call | solution.py:150
  165.6 3.5 %all-to-all-start.2 = ((bf16[4,4,2,128,128]{4,3,2,1,0:T(8,128)(2,1)}), bf16[4,4,2,128,128]{4,3,2,1,0:T(8,128)(2,1)S(1)}, u32[]{:S(2)}, u32[]{:S(2)}) async-start(bf16[4,4,2,128,128]{4,3,2,1,0:T(8,128)(2,1)} %shard_map.107), calls=%async_computation.2 | async-start | bytes 2097152 | tf_op jit(solution)/shard_map/all_to_all | solution.py:31
  170.0 3.1 %collective-permute-start.9 = (bf16[4,2,128,128]{3,2,1,0:T(8,128)(2,1)S(1)}, bf16[4,2,128,128]{3,2,1,0:T(8,128)(2,1)S(1)}, u32[]{:S(2)}, u32[]{:S(2)}) collective-permute-start(bf16[4,2,128,128]{3,2,1,0:T(8,128)(2,1)S(1)} %get-tuple-element.36), channel_id=1, source_target_pairs={{0,3},{1,0},{2,1},{3,2},{4,7},{5,4},{6,5},{7,6},{8,11},{9,8},{10,9... | collective-permute-start | bytes 786440 | tf_op jit(solution)/shard_map/ppermute | solution.py:21
  173.1 7.3 %collective-permute-done.11 = bf16[4,2,128,128]{3,2,1,0:T(8,128)(2,1)S(1)} collective-permute-done((bf16[4,2,128,128]{3,2,1,0:T(8,128)(2,1)S(1)}, bf16[4,2,128,128]{3,2,1,0:T(8,128)(2,1)S(1)}, u32[]{:S(2)}, u32[]{:S(2)}) %collective-permute-start.11) | collective-permute-done | bytes 262176 | tf_op jit(solution)/shard_map/ppermute | solution.py:21
  180.4 7.6 %collective-permute-done.10 = bf16[4,2,128,128]{3,2,1,0:T(8,128)(2,1)S(1)} collective-permute-done((bf16[4,2,128,128]{3,2,1,0:T(8,128)(2,1)S(1)}, bf16[4,2,128,128]{3,2,1,0:T(8,128)(2,1)S(1)}, u32[]{:S(2)}, u32[]{:S(2)}) %collective-permute-start.10) | collective-permute-done | bytes 262176 | tf_op jit(solution)/shard_map/ppermute | solution.py:21
  188.0 1.1 pad_maximum_fusion.1
  189.1 1.0 copy-done.22
  190.1 4.5 %all-to-all-start.3 = ((bf16[4,4,2,128,128]{4,3,2,1,0:T(8,128)(2,1)}), bf16[4,4,2,128,128]{4,3,2,1,0:T(8,128)(2,1)S(1)}, u32[]{:S(2)}, u32[]{:S(2)}) async-start(bf16[4,4,2,128,128]{4,3,2,1,0:T(8,128)(2,1)} %pad_maximum_fusion.1), calls=%async_computation.3 | async-start | bytes 2097152 | tf_op jit(solution)/shard_map/all_to_all | solution.py:31
  194.6 1.3 slice_bitcast_fusion.3
  195.9 6.2 %collective-permute-start.15 = (bf16[4,2,128,128]{3,2,1,0:T(8,128)(2,1)S(1)}, bf16[4,2,128,128]{3,2,1,0:T(8,128)(2,1)S(1)}, u32[]{:S(2)}, u32[]{:S(2)}) collective-permute-start(bf16[4,2,128,128]{3,2,1,0:T(8,128)(2,1)S(1)} %get-tuple-element.31), channel_id=1, source_target_pairs={{0,3},{1,0},{2,1},{3,2},{4,7},{5,4},{6,5},{7,6},{8,11},{9,8},{10,9... | collective-permute-start | bytes 786440 | tf_op jit(solution)/shard_map/ppermute | solution.py:21
  202.0 0.8 collective-permute-start.16
  202.9 5.9 %collective-permute-done.15.refs_2_ = bf16[4,2,128,128]{3,2,1,0:T(8,128)(2,1)S(1)} collective-permute-done((bf16[4,2,128,128]{3,2,1,0:T(8,128)(2,1)S(1)}, bf16[4,2,128,128]{3,2,1,0:T(8,128)(2,1)S(1)}, u32[]{:S(2)}, u32[]{:S(2)}) %collective-permute-start.15) | collective-permute-done | bytes 262176 | tf_op jit(solution)/shard_map/ppermute | solution.py:21
  208.8 16.2 %collective-permute-done.16.refs_3_ = bf16[4,2,128,128]{3,2,1,0:T(8,128)(2,1)S(1)} collective-permute-done((bf16[4,2,128,128]{3,2,1,0:T(8,128)(2,1)S(1)}, bf16[4,2,128,128]{3,2,1,0:T(8,128)(2,1)S(1)}, u32[]{:S(2)}, u32[]{:S(2)}) %collective-permute-start.16) | collective-permute-done | bytes 262176 | tf_op jit(solution)/shard_map/ppermute | solution.py:21
  225.0 2.5 %shard_map.108 = (bf16[128,4096]{1,0:T(8,128)(2,1)}, bf16[128,4096]{1,0:T(8,128)(2,1)}) custom-call(s32[2]{0:T(128)S(1)} %pad_add_fusion.place_ref, bf16[4,4,2,128,128]{4,3,2,1,0:T(8,128)(2,1)S(1)} %all-to-all-done.3.refs_0_, bf16[4,2,128,128]{3,2,1,0:T(8,128)(2,1)S(1)} %get-tuple-element.32.refs_1_, ...), custom_call_target="tpu_custom_call" | custom-call | bytes 4194304 | tf_op jit(solution)/shard_map/pallas_call | solution.py:86
  (67 shorter events, 4.6 us)
Async XLA Ops:
  0.6 27.8 %collective-permute-start.4 = (bf16[32,4096]{1,0:T(8,128)(2,1)}, bf16[32,4096]{1,0:T(8,128)(2,1)}, u32[]{:S(2)}, u32[]{:S(2)}) collective-permute-start(bf16[32,4096]{1,0:T(8,128)(2,1)} %param.13), channel_id=1, source_target_pairs={{0,3},{1,0},{2,1},{3,2},{4,7},{5,4},{6,5},{7,6},{8,11},{9,8},{10,9... | collective-permute-start | bytes 786440 | tf_op jit(solution)/shard_map/ppermute | solution.py:21
  5.3 22.1 %collective-permute-start.2 = (bf16[32,4096]{1,0:T(8,128)(2,1)}, bf16[32,4096]{1,0:T(8,128)(2,1)}, u32[]{:S(2)}, u32[]{:S(2)}) collective-permute-start(bf16[32,4096]{1,0:T(8,128)(2,1)} %param.13), channel_id=1, source_target_pairs={{0,2},{1,3},{2,0},{3,1},{4,6},{5,7},{6,4},{7,5},{8,10},{9,11},{10,... | collective-permute-start | bytes 786440 | tf_op jit(solution)/shard_map/ppermute | solution.py:21
  5.3 18.0 %collective-permute-start = (bf16[32,4096]{1,0:T(8,128)(2,1)}, bf16[32,4096]{1,0:T(8,128)(2,1)}, u32[]{:S(2)}, u32[]{:S(2)}) collective-permute-start(bf16[32,4096]{1,0:T(8,128)(2,1)} %param.13), channel_id=1, source_target_pairs={{0,1},{1,2},{2,3},{3,0},{4,5},{5,6},{6,7},{7,4},{8,9},{9,10},{10,1... | collective-permute-start | bytes 786440 | tf_op jit(solution)/shard_map/ppermute | solution.py:21
  6.1 1.2 copy-start.3
  7.3 1.2 copy-start.4
  8.5 1.2 copy-start.5
  9.8 1.2 copy-start.6
  12.6 1.4 copy-start.2
  14.0 0.8 copy-start.14
  14.8 0.8 copy-start.16
  15.6 0.8 copy-start.18
  16.3 0.8 copy-start.20
  17.1 4.6 %copy-start.23 = (bf16[32,4096]{1,0:T(8,128)(2,1)S(1)}, bf16[32,4096]{1,0:T(8,128)(2,1)}, u32[]{:S(2)}) copy-start(bf16[32,4096]{1,0:T(8,128)(2,1)} %param.13) | copy-start | bytes 786436
  17.1 67.9 %all-to-all-start.1 = ((bf16[4,4,4,128,128]{4,3,2,1,0:T(8,128)(2,1)}), bf16[4,4,4,128,128]{4,3,2,1,0:T(8,128)(2,1)S(1)}, u32[]{:S(2)}, u32[]{:S(2)}) async-start(bf16[4,4,4,128,128]{4,3,2,1,0:T(8,128)(2,1)} %copy-done.2), calls=%async_computation.1 | async-start | bytes 4194304 | tf_op jit(solution)/shard_map/all_to_all | solution.py:31
  21.7 11.0 %copy-start.21 = (bf16[4,4,128,128]{3,2,1,0:T(8,128)(2,1)S(1)}, bf16[4,4,128,128]{3,2,1,0:T(8,128)(2,1)}, u32[]{:S(2)}) copy-start(bf16[4,4,128,128]{3,2,1,0:T(8,128)(2,1)} %copy-done.20) | copy-start | bytes 1572868
  21.7 11.0 %copy-start.19 = (bf16[4,4,128,128]{3,2,1,0:T(8,128)(2,1)S(1)}, bf16[4,4,128,128]{3,2,1,0:T(8,128)(2,1)}, u32[]{:S(2)}) copy-start(bf16[4,4,128,128]{3,2,1,0:T(8,128)(2,1)} %copy-done.18) | copy-start | bytes 1572868
  21.7 15.3 %copy-start.17 = (bf16[4,4,128,128]{3,2,1,0:T(8,128)(2,1)S(1)}, bf16[4,4,128,128]{3,2,1,0:T(8,128)(2,1)}, u32[]{:S(2)}) copy-start(bf16[4,4,128,128]{3,2,1,0:T(8,128)(2,1)} %copy-done.16) | copy-start | bytes 1572868
  21.8 59.8 %copy-start.15 = (bf16[4,4,128,128]{3,2,1,0:T(8,128)(2,1)S(1)}, bf16[4,4,128,128]{3,2,1,0:T(8,128)(2,1)}, u32[]{:S(2)}) copy-start(bf16[4,4,128,128]{3,2,1,0:T(8,128)(2,1)} %copy-done.14) | copy-start | bytes 1572868
  29.4 53.7 %collective-permute-start.6 = (bf16[128,4096]{1,0:T(8,128)(2,1)S(1)}, bf16[128,4096]{1,0:T(8,128)(2,1)S(1)}, u32[]{:S(2)}, u32[]{:S(2)}) collective-permute-start(bf16[128,4096]{1,0:T(8,128)(2,1)S(1)} %constant_dynamic-update-slice_fusion.refs_0_), channel_id=1, source_target_pairs={{0,4},{1,5},{2,6},{3,7},{4,8},{5,9},{6,10},{7,11},{8,12},{9,13},{1... | collective-permute-start | bytes 3145736 | tf_op jit(solution)/shard_map/ppermute | solution.py:26
  31.1 53.0 %collective-permute-start.7 = (bf16[128,4096]{1,0:T(8,128)(2,1)S(1)}, bf16[128,4096]{1,0:T(8,128)(2,1)S(1)}, u32[]{:S(2)}, u32[]{:S(2)}) collective-permute-start(bf16[128,4096]{1,0:T(8,128)(2,1)S(1)} %constant_dynamic-update-slice_fusion.refs_0_), channel_id=1, source_target_pairs={{0,12},{1,13},{2,14},{3,15},{4,0},{5,1},{6,2},{7,3},{8,4},{9,5},{1... | collective-permute-start | bytes 3145736 | tf_op jit(solution)/shard_map/ppermute | solution.py:26
  32.7 13.2 %collective-permute-start.5 = (bf16[4,4,128,128]{3,2,1,0:T(8,128)(2,1)S(1)}, bf16[4,4,128,128]{3,2,1,0:T(8,128)(2,1)S(1)}, u32[]{:S(2)}, u32[]{:S(2)}) collective-permute-start(bf16[4,4,128,128]{3,2,1,0:T(8,128)(2,1)S(1)} %copy-done.21), channel_id=1, source_target_pairs={{0,3},{1,0},{2,1},{3,2},{4,7},{5,4},{6,5},{7,6},{8,11},{9,8},{10,9... | collective-permute-start | bytes 1572872 | tf_op jit(solution)/shard_map/ppermute | solution.py:21
  32.7 48.8 %collective-permute-start.3 = (bf16[4,4,128,128]{3,2,1,0:T(8,128)(2,1)S(1)}, bf16[4,4,128,128]{3,2,1,0:T(8,128)(2,1)S(1)}, u32[]{:S(2)}, u32[]{:S(2)}) collective-permute-start(bf16[4,4,128,128]{3,2,1,0:T(8,128)(2,1)S(1)} %copy-done.19), channel_id=1, source_target_pairs={{0,2},{1,3},{2,0},{3,1},{4,6},{5,7},{6,4},{7,5},{8,10},{9,11},{10,... | collective-permute-start | bytes 1572872 | tf_op jit(solution)/shard_map/ppermute | solution.py:21
  37.0 44.5 %collective-permute-start.1 = (bf16[4,4,128,128]{3,2,1,0:T(8,128)(2,1)S(1)}, bf16[4,4,128,128]{3,2,1,0:T(8,128)(2,1)S(1)}, u32[]{:S(2)}, u32[]{:S(2)}) collective-permute-start(bf16[4,4,128,128]{3,2,1,0:T(8,128)(2,1)S(1)} %copy-done.17), channel_id=1, source_target_pairs={{0,1},{1,2},{2,3},{3,0},{4,5},{5,6},{6,7},{7,4},{8,9},{9,10},{10,1... | collective-permute-start | bytes 1572872 | tf_op jit(solution)/shard_map/ppermute | solution.py:21
  83.1 10.7 %copy-start.24 = (s32[16]{0:T(128)S(1)}, s32[16]{0:T(128)}, u32[]{:S(2)}) copy-start(s32[16]{0:T(128)} %param.14) | copy-start | bytes 196
  83.1 1.0 copy-start.7
  84.1 1.0 copy-start.9
  85.1 59.9 %all-to-all-start = ((bf16[4,4,4,128,128]{4,3,2,1,0:T(8,128)(2,1)}), bf16[4,4,4,128,128]{4,3,2,1,0:T(8,128)(2,1)}, u32[]{:S(2)}, u32[]{:S(2)}) async-start(bf16[4,4,4,128,128]{4,3,2,1,0:T(8,128)(2,1)} %pad_maximum_fusion), calls=%async_computation | async-start | bytes 4194304 | tf_op jit(solution)/shard_map/all_to_all | solution.py:31
  90.2 46.8 %collective-permute-start.8 = (bf16[128,4096]{1,0:T(8,128)(2,1)S(1)}, bf16[128,4096]{1,0:T(8,128)(2,1)}, u32[]{:S(2)}, u32[]{:S(2)}) collective-permute-start(bf16[128,4096]{1,0:T(8,128)(2,1)S(1)} %constant_dynamic-update-slice_fusion.refs_0_), channel_id=1, source_target_pairs={{0,8},{1,9},{2,10},{3,11},{4,12},{5,13},{6,14},{7,15},{8,0},{9,1},... | collective-permute-start | bytes 3145736 | tf_op jit(solution)/shard_map/ppermute | solution.py:26
  94.2 42.8 %copy-start = (bf16[4096,256]{1,0:T(8,128)(2,1)S(1)}, bf16[4096,256]{1,0:T(8,128)(2,1)}, u32[]{:S(2)}) copy-start(bf16[4096,256]{1,0:T(8,128)(2,1)} %refs_4_.1) | copy-start | bytes 6291460
  94.2 42.8 %copy-start.8 = (bf16[128,4096]{1,0:T(8,128)(2,1)S(1)}, bf16[128,4096]{1,0:T(8,128)(2,1)}, u32[]{:S(2)}) copy-start(bf16[128,4096]{1,0:T(8,128)(2,1)} %copy-done.7) | copy-start | bytes 3145732
  95.5 60.0 %collective-permute-start.12 = (bf16[4,4,128,128]{3,2,1,0:T(8,128)(2,1)}, bf16[4,4,128,128]{3,2,1,0:T(8,128)(2,1)}, u32[]{:S(2)}, u32[]{:S(2)}) collective-permute-start(bf16[4,4,128,128]{3,2,1,0:T(8,128)(2,1)} %get-tuple-element.28), channel_id=1, source_target_pairs={{0,1},{1,2},{2,3},{3,0},{4,5},{5,6},{6,7},{7,4},{8,9},{9,10},{10,1... | collective-permute-start | bytes 1572872 | tf_op jit(solution)/shard_map/ppermute | solution.py:21
  95.5 60.0 %collective-permute-start.13 = (bf16[4,4,128,128]{3,2,1,0:T(8,128)(2,1)}, bf16[4,4,128,128]{3,2,1,0:T(8,128)(2,1)}, u32[]{:S(2)}, u32[]{:S(2)}) collective-permute-start(bf16[4,4,128,128]{3,2,1,0:T(8,128)(2,1)} %get-tuple-element.27), channel_id=1, source_target_pairs={{0,2},{1,3},{2,0},{3,1},{4,6},{5,7},{6,4},{7,5},{8,10},{9,11},{10,... | collective-permute-start | bytes 1572872 | tf_op jit(solution)/shard_map/ppermute | solution.py:21
  95.5 60.0 %collective-permute-start.14 = (bf16[4,4,128,128]{3,2,1,0:T(8,128)(2,1)}, bf16[4,4,128,128]{3,2,1,0:T(8,128)(2,1)}, u32[]{:S(2)}, u32[]{:S(2)}) collective-permute-start(bf16[4,4,128,128]{3,2,1,0:T(8,128)(2,1)} %get-tuple-element.26), channel_id=1, source_target_pairs={{0,3},{1,0},{2,1},{3,2},{4,7},{5,4},{6,5},{7,6},{8,11},{9,8},{10,9... | collective-permute-start | bytes 1572872 | tf_op jit(solution)/shard_map/ppermute | solution.py:21
  137.0 1.6 copy-start.1
  138.6 1.2 copy-start.10
  144.2 0.8 copy-start.11
  145.0 1.0 copy-start.12
  146.0 9.5 %copy-start.13 = (bf16[512,512]{1,0:T(8,128)(2,1)S(1)}, bf16[512,512]{1,0:T(8,128)(2,1)}, u32[]{:S(2)}) copy-start(bf16[512,512]{1,0:T(8,128)(2,1)} %copy-done.11) | copy-start | bytes 1572868
  165.6 23.5 %all-to-all-start.2 = ((bf16[4,4,2,128,128]{4,3,2,1,0:T(8,128)(2,1)}), bf16[4,4,2,128,128]{4,3,2,1,0:T(8,128)(2,1)S(1)}, u32[]{:S(2)}, u32[]{:S(2)}) async-start(bf16[4,4,2,128,128]{4,3,2,1,0:T(8,128)(2,1)} %shard_map.107), calls=%async_computation.2 | async-start | bytes 2097152 | tf_op jit(solution)/shard_map/all_to_all | solution.py:31
  169.2 11.2 %collective-permute-start.11 = (bf16[4,2,128,128]{3,2,1,0:T(8,128)(2,1)S(1)}, bf16[4,2,128,128]{3,2,1,0:T(8,128)(2,1)S(1)}, u32[]{:S(2)}, u32[]{:S(2)}) collective-permute-start(bf16[4,2,128,128]{3,2,1,0:T(8,128)(2,1)S(1)} %get-tuple-element.34), channel_id=1, source_target_pairs={{0,1},{1,2},{2,3},{3,0},{4,5},{5,6},{6,7},{7,4},{8,9},{9,10},{10,1... | collective-permute-start | bytes 786440 | tf_op jit(solution)/shard_map/ppermute | solution.py:21
  169.3 18.7 %collective-permute-start.10 = (bf16[4,2,128,128]{3,2,1,0:T(8,128)(2,1)S(1)}, bf16[4,2,128,128]{3,2,1,0:T(8,128)(2,1)S(1)}, u32[]{:S(2)}, u32[]{:S(2)}) collective-permute-start(bf16[4,2,128,128]{3,2,1,0:T(8,128)(2,1)S(1)} %get-tuple-element.35), channel_id=1, source_target_pairs={{0,2},{1,3},{2,0},{3,1},{4,6},{5,7},{6,4},{7,5},{8,10},{9,11},{10,... | collective-permute-start | bytes 786440 | tf_op jit(solution)/shard_map/ppermute | solution.py:21
  170.0 18.0 %collective-permute-start.9 = (bf16[4,2,128,128]{3,2,1,0:T(8,128)(2,1)S(1)}, bf16[4,2,128,128]{3,2,1,0:T(8,128)(2,1)S(1)}, u32[]{:S(2)}, u32[]{:S(2)}) collective-permute-start(bf16[4,2,128,128]{3,2,1,0:T(8,128)(2,1)S(1)} %get-tuple-element.36), channel_id=1, source_target_pairs={{0,3},{1,0},{2,1},{3,2},{4,7},{5,4},{6,5},{7,6},{8,11},{9,8},{10,9... | collective-permute-start | bytes 786440 | tf_op jit(solution)/shard_map/ppermute | solution.py:21
  189.1 1.0 copy-start.22
  190.1 34.9 %all-to-all-start.3 = ((bf16[4,4,2,128,128]{4,3,2,1,0:T(8,128)(2,1)}), bf16[4,4,2,128,128]{4,3,2,1,0:T(8,128)(2,1)S(1)}, u32[]{:S(2)}, u32[]{:S(2)}) async-start(bf16[4,4,2,128,128]{4,3,2,1,0:T(8,128)(2,1)} %pad_maximum_fusion.1), calls=%async_computation.3 | async-start | bytes 2097152 | tf_op jit(solution)/shard_map/all_to_all | solution.py:31
  195.9 12.9 %collective-permute-start.15 = (bf16[4,2,128,128]{3,2,1,0:T(8,128)(2,1)S(1)}, bf16[4,2,128,128]{3,2,1,0:T(8,128)(2,1)S(1)}, u32[]{:S(2)}, u32[]{:S(2)}) collective-permute-start(bf16[4,2,128,128]{3,2,1,0:T(8,128)(2,1)S(1)} %get-tuple-element.31), channel_id=1, source_target_pairs={{0,3},{1,0},{2,1},{3,2},{4,7},{5,4},{6,5},{7,6},{8,11},{9,8},{10,9... | collective-permute-start | bytes 786440 | tf_op jit(solution)/shard_map/ppermute | solution.py:21
  202.0 23.0 %collective-permute-start.16 = (bf16[4,2,128,128]{3,2,1,0:T(8,128)(2,1)S(1)}, bf16[4,2,128,128]{3,2,1,0:T(8,128)(2,1)S(1)}, u32[]{:S(2)}, u32[]{:S(2)}) collective-permute-start(bf16[4,2,128,128]{3,2,1,0:T(8,128)(2,1)S(1)} %get-tuple-element.30), channel_id=1, source_target_pairs={{0,2},{1,3},{2,0},{3,1},{4,6},{5,7},{6,4},{7,5},{8,10},{9,11},{10,... | collective-permute-start | bytes 786440 | tf_op jit(solution)/shard_map/ppermute | solution.py:21
  202.9 22.2 %collective-permute-start.17 = (bf16[4,2,128,128]{3,2,1,0:T(8,128)(2,1)S(1)}, bf16[4,2,128,128]{3,2,1,0:T(8,128)(2,1)S(1)}, u32[]{:S(2)}, u32[]{:S(2)}) collective-permute-start(bf16[4,2,128,128]{3,2,1,0:T(8,128)(2,1)S(1)} %get-tuple-element.29), channel_id=1, source_target_pairs={{0,1},{1,2},{2,3},{3,0},{4,5},{5,6},{6,7},{7,4},{8,9},{9,10},{10,1... | collective-permute-start | bytes 786440 | tf_op jit(solution)/shard_map/ppermute | solution.py:21

commit v6 on v4

--- a/solution.py
+++ b/solution.py
@@ -251,8 +251,10 @@
     text_y = {0: text_z, 2: shift_y(text_z, 2), 1: shift_y(text_z, 1), 3: shift_y(text_z, 3)}
     text_own = project([text_y[s] for s in side], key_weight, value_weight)
 
-    second_z = {t: shift_z(second_y[:, t], t) for t in steps}
-    first_y = swap_y(after(jnp.stack([first_z[t] for t in side], axis=1), *[text_y[s] for s in steps]))
+    cuts = {t: second_y[:, t] for t in steps}
+    second_z = {t: shift_z(cuts[t], t) for t in steps}
+    together = jnp.stack([first_z[t] for t in side], axis=1)
+    first_y = swap_y(after(together, *[text_y[s] for s in steps], *cuts.values()))
 
     near = jnp.arange(SIDE, dtype=jnp.int32)
     holder = ((y - near) % SIDE * SIDE)[:, None] + ((z - near) % SIDE)[None, :]
@@ -286,7 +288,7 @@
     for t in steps:
         second_home[t] = shift_z(second_back[:, t], -t)
     first_home = swap_y(
-        after(jnp.stack([first_back[t] for t in side], axis=1), second_back)
+        after(jnp.stack([first_back[t] for t in side], axis=1), second_home[1])
     )
     self_out, cross_out = join(
         place, first_home, [second_home[t] for t in side], video_query.shape

time: 222 us -> 221 us (level)
  the two profiles are of different devices: /device:TPU:43 before, /device:TPU:2 now
where the time goes in v6:
time: 221 us; the launch traced here: 219 us
  waiting for transfers between devices  102 us (46%)
  starting transfers between devices  64.1 us (29%)
  Pallas kernels  27.5 us (12%)
  local copies, waits for them, and re-layouts  20.6 us (9%)
  other arithmetic  3.15 us (1%)
    ppermute x15, waiting for transfers between devices, shift_z(): return lax.ppermute(array, 'seq', pairs)  73.6 us
    ppermute x15, starting transfers between devices, shift_z(): return lax.ppermute(array, 'seq', pairs)  41.2 us
    all_to_all x4, waiting for transfers between devices, swap_y(): lax.all_to_all(array, 'seq', split_axis=0, concat_axis=0, axis_index_grou...  20.2 us
    pallas_call x2, Pallas kernels, attend(): pl.pallas_call(functools.partial(attend_kernel, head=head, blocks=4), gri...  18.7 us
    all_to_all x4, starting transfers between devices, swap_y(): lax.all_to_all(array, 'seq', split_axis=0, concat_axis=0, axis_index_grou...  18.2 us
    unnamed x43, local copies, waits for them, and re-layouts  17.4 us
    ppermute x3, waiting for transfers between devices, shift_y(): return lax.ppermute(array, 'seq', pairs)  8.3 us
    ppermute x3, starting transfers between devices, shift_y(): return lax.ppermute(array, 'seq', pairs)  4.69 us
  transfers between devices with their start and end apart: 22, of which 9 were waited for; matrix products, arithmetic and copies ran while one was open for 4% of the time, Pallas kernels for 7%

profile of v6, /device:TPU:2, one launch (start us, length us, event | category | flops | bytes accessed | tf_op | source)
XLA Modules:
  0.0 218.8 jit_solution(721751111097509864)
XLA Ops:
  0.6 3.4 %collective-permute-start.2 = (bf16[32,4096]{1,0:T(8,128)(2,1)}, bf16[32,4096]{1,0:T(8,128)(2,1)}, u32[]{:S(2)}, u32[]{:S(2)}) collective-permute-start(bf16[32,4096]{1,0:T(8,128)(2,1)} %param.13), channel_id=1, source_target_pairs={{0,2},{1,3},{2,0},{3,1},{4,6},{5,7},{6,4},{7,5},{8,10},{9,11},{10,... | collective-permute-start | bytes 786440 | tf_op jit(solution)/shard_map/ppermute | solution.py:21
  4.0 1.9 collective-permute-start
  5.9 1.9 collective-permute-start.4
  7.9 1.2 copy-done.3
  9.1 1.2 copy-done.4
  10.3 1.2 copy-done.5
  11.6 1.2 copy-done.6
  12.8 1.6 shard_map.104
  14.4 1.3 copy-done.2
  15.8 0.8 copy-done.11
  16.6 0.8 copy-done.13
  19.0 4.6 %all-to-all-start = ((bf16[4,4,4,128,128]{4,3,2,1,0:T(8,128)(2,1)}), bf16[4,4,4,128,128]{4,3,2,1,0:T(8,128)(2,1)S(1)}, u32[]{:S(2)}, u32[]{:S(2)}) async-start(bf16[4,4,4,128,128]{4,3,2,1,0:T(8,128)(2,1)} %copy-done.2), calls=%async_computation | async-start | bytes 4194304 | tf_op jit(solution)/shard_map/all_to_all | solution.py:31
  23.6 1.9 collective-permute-start.5
  25.5 1.0 constant_dynamic-update-slice_fusion.2
  26.5 1.0 constant_dynamic-update-slice_fusion.1
  27.5 1.0 constant_dynamic-update-slice_fusion.refs_0_
  28.5 3.1 %collective-permute-start.8 = (bf16[128,4096]{1,0:T(8,128)(2,1)S(1)}, bf16[128,4096]{1,0:T(8,128)(2,1)}, u32[]{:S(2)}, u32[]{:S(2)}) collective-permute-start(bf16[128,4096]{1,0:T(8,128)(2,1)S(1)} %constant_dynamic-update-slice_fusion.refs_0_), channel_id=1, source_target_pairs={{0,12},{1,13},{2,14},{3,15},{4,0},{5,1},{6,2},{7,3},{8,4},{9,5},{1... | collective-permute-start | bytes 3145736 | tf_op jit(solution)/shard_map/ppermute | solution.py:26
  32.2 1.0 collective-permute-start.6
  33.2 15.8 %collective-permute-start.3 = (bf16[4,4,128,128]{3,2,1,0:T(8,128)(2,1)S(1)}, bf16[4,4,128,128]{3,2,1,0:T(8,128)(2,1)S(1)}, u32[]{:S(2)}, u32[]{:S(2)}) collective-permute-start(bf16[4,4,128,128]{3,2,1,0:T(8,128)(2,1)S(1)} %copy-done.16), channel_id=1, source_target_pairs={{0,2},{1,3},{2,0},{3,1},{4,6},{5,7},{6,4},{7,5},{8,10},{9,11},{10,... | collective-permute-start | bytes 1572872 | tf_op jit(solution)/shard_map/ppermute | solution.py:21
  49.0 33.7 %collective-permute-done.3 = bf16[4,4,128,128]{3,2,1,0:T(8,128)(2,1)S(1)} collective-permute-done((bf16[4,4,128,128]{3,2,1,0:T(8,128)(2,1)S(1)}, bf16[4,4,128,128]{3,2,1,0:T(8,128)(2,1)S(1)}, u32[]{:S(2)}, u32[]{:S(2)}) %collective-permute-start.3) | collective-permute-done | bytes 524320 | tf_op jit(solution)/shard_map/ppermute | solution.py:21
  82.7 1.6 pad_maximum_fusion
  84.3 1.2 slice_bitcast_fusion
  85.5 8.3 %collective-permute-done.6.refs_1_ = bf16[128,4096]{1,0:T(8,128)(2,1)} collective-permute-done((bf16[128,4096]{1,0:T(8,128)(2,1)S(1)}, bf16[128,4096]{1,0:T(8,128)(2,1)}, u32[]{:S(2)}, u32[]{:S(2)}) %collective-permute-start.6) | collective-permute-done | bytes 1048608 | tf_op jit(solution)/shard_map/ppermute | solution.py:26
  93.8 4.6 %all-to-all-start.1 = ((bf16[4,4,4,128,128]{4,3,2,1,0:T(8,128)(2,1)}), bf16[4,4,4,128,128]{4,3,2,1,0:T(8,128)(2,1)}, u32[]{:S(2)}, u32[]{:S(2)}) async-start(bf16[4,4,4,128,128]{4,3,2,1,0:T(8,128)(2,1)} %pad_maximum_fusion), calls=%async_computation.1 | async-start | bytes 4194304 | tf_op jit(solution)/shard_map/all_to_all | solution.py:31
  99.8 2.2 %collective-permute-start.13 = (bf16[4,4,128,128]{3,2,1,0:T(8,128)(2,1)}, bf16[4,4,128,128]{3,2,1,0:T(8,128)(2,1)}, u32[]{:S(2)}, u32[]{:S(2)}) collective-permute-start(bf16[4,4,128,128]{3,2,1,0:T(8,128)(2,1)} %get-tuple-element.25), channel_id=1, source_target_pairs={{0,2},{1,3},{2,0},{3,1},{4,6},{5,7},{6,4},{7,5},{8,10},{9,11},{10,... | collective-permute-start | bytes 1572872 | tf_op jit(solution)/shard_map/ppermute | solution.py:21
  102.1 1.9 collective-permute-start.12
  104.0 1.6 copy-done
  105.6 1.6 copy-done.1
  107.2 4.7 %shard_map.105.refs_1_.refs_4_ = bf16[512,512]{1,0:T(8,128)(2,1)S(1)} custom-call(bf16[128,4096]{1,0:T(8,128)(2,1)S(1)} %constant_dynamic-update-slice_fusion.refs_0_, bf16[128,4096]{1,0:T(8,128)(2,1)} %collective-permute-done.6.refs_1_, bf16[128,4096]{1,0:T(8,128)(2,1)} %collective-permute-done.7.refs_2_, bf16[128,4096]{1,0:T(8,128)(2,1)} %collective-permute-done.8.refs_3_, ...), custom_call_target="tpu_custom_call" | custom-call | flops 2147483648 | bytes 8388608 | tf_op jit(solution)/shard_map/pallas_call | solution.py:202
  112.7 10.4 %all-to-all-done.1.refs_0_ = bf16[4,4,4,128,128]{4,3,2,1,0:T(8,128)(2,1)} async-done(((bf16[4,4,4,128,128]{4,3,2,1,0:T(8,128)(2,1)}), bf16[4,4,4,128,128]{4,3,2,1,0:T(8,128)(2,1)}, u32[]{:S(2)}, u32[]{:S(2)}) %all-to-all-start.1) | async-done | bytes 2097184 | tf_op jit(solution)/shard_map/all_to_all | solution.py:31
  123.0 1.0 copy-done.9
  124.1 9.5 %shard_map.106 = bf16[4,4,2,128,128]{4,3,2,1,0:T(8,128)(2,1)S(1)} custom-call(bf16[4,4,4,128,128]{4,3,2,1,0:T(8,128)(2,1)} %all-to-all-done.1.refs_0_, bf16[512,512]{1,0:T(8,128)(2,1)S(1)} %copy-done.9, f32[1,512]{1,0:T(1,128)S(1)} %select_n.53.refs_2_.refs_5_), custom_call_target="tpu_custom_call" | custom-call | flops 5368709120 | bytes 3145728 | tf_op jit(solution)/shard_map/pallas_call | solution.py:150
  133.6 14.5 %collective-permute-done.13.refs_2_ = bf16[4,4,128,128]{3,2,1,0:T(8,128)(2,1)} collective-permute-done((bf16[4,4,128,128]{3,2,1,0:T(8,128)(2,1)}, bf16[4,4,128,128]{3,2,1,0:T(8,128)(2,1)}, u32[]{:S(2)}, u32[]{:S(2)}) %collective-permute-start.13) | collective-permute-done | bytes 524320 | tf_op jit(solution)/shard_map/ppermute | solution.py:21
  148.1 9.2 %shard_map.107 = bf16[4,4,2,128,128]{4,3,2,1,0:T(8,128)(2,1)S(1)} custom-call(bf16[4,4,4,128,128]{4,3,2,1,0:T(8,128)(2,1)S(1)} %all-to-all-done.refs_0_, bf16[4,4,128,128]{3,2,1,0:T(8,128)(2,1)} %collective-permute-done.12.refs_1_, bf16[4,4,128,128]{3,2,1,0:T(8,128)(2,1)} %collective-permute-done.13.refs_2_, ...), custom_call_target="tpu_custom_call" | custom-call | flops 5368709120 | bytes 3145728 | tf_op jit(solution)/shard_map/pallas_call | solution.py:150
  157.4 1.0 copy-done.7
  158.3 4.5 %all-to-all-start.2 = ((bf16[4,4,2,128,128]{4,3,2,1,0:T(8,128)(2,1)}), bf16[4,4,2,128,128]{4,3,2,1,0:T(8,128)(2,1)S(1)}, u32[]{:S(2)}, u32[]{:S(2)}) async-start(bf16[4,4,2,128,128]{4,3,2,1,0:T(8,128)(2,1)} %copy-done.7), calls=%async_computation.2 | async-start | bytes 2097152 | tf_op jit(solution)/shard_map/all_to_all | solution.py:31
  162.8 0.8 slice_bitcast_fusion.10
  163.6 3.8 %collective-permute-start.9 = (bf16[4,2,128,128]{3,2,1,0:T(8,128)(2,1)S(1)}, bf16[4,2,128,128]{3,2,1,0:T(8,128)(2,1)S(1)}, u32[]{:S(2)}, u32[]{:S(2)}) collective-permute-start(bf16[4,2,128,128]{3,2,1,0:T(8,128)(2,1)S(1)} %get-tuple-element.34), channel_id=1, source_target_pairs={{0,3},{1,0},{2,1},{3,2},{4,7},{5,4},{6,5},{7,6},{8,11},{9,8},{10,9... | collective-permute-start | bytes 786440 | tf_op jit(solution)/shard_map/ppermute | solution.py:21
  167.4 9.8 %all-to-all-done.2 = bf16[4,4,2,128,128]{4,3,2,1,0:T(8,128)(2,1)S(1)} async-done(((bf16[4,4,2,128,128]{4,3,2,1,0:T(8,128)(2,1)}), bf16[4,4,2,128,128]{4,3,2,1,0:T(8,128)(2,1)S(1)}, u32[]{:S(2)}, u32[]{:S(2)}) %all-to-all-start.2) | async-done | bytes 1048608 | tf_op jit(solution)/shard_map/all_to_all | solution.py:31
  177.4 6.8 %collective-permute-done.10 = bf16[4,2,128,128]{3,2,1,0:T(8,128)(2,1)S(1)} collective-permute-done((bf16[4,2,128,128]{3,2,1,0:T(8,128)(2,1)S(1)}, bf16[4,2,128,128]{3,2,1,0:T(8,128)(2,1)S(1)}, u32[]{:S(2)}, u32[]{:S(2)}) %collective-permute-start.10) | collective-permute-done | bytes 262176 | tf_op jit(solution)/shard_map/ppermute | solution.py:21
  184.2 1.1 pad_maximum_fusion.1
  185.3 3.2 %collective-permute-done.15.refs_2_ = bf16[4,2,128,128]{3,2,1,0:T(8,128)(2,1)S(1)} collective-permute-done((bf16[4,2,128,128]{3,2,1,0:T(8,128)(2,1)S(1)}, bf16[4,2,128,128]{3,2,1,0:T(8,128)(2,1)S(1)}, u32[]{:S(2)}, u32[]{:S(2)}) %collective-permute-start.15) | collective-permute-done | bytes 262176 | tf_op jit(solution)/shard_map/ppermute | solution.py:21
  188.5 4.5 %all-to-all-start.3 = ((bf16[4,4,2,128,128]{4,3,2,1,0:T(8,128)(2,1)}), bf16[4,4,2,128,128]{4,3,2,1,0:T(8,128)(2,1)S(1)}, u32[]{:S(2)}, u32[]{:S(2)}) async-start(bf16[4,4,2,128,128]{4,3,2,1,0:T(8,128)(2,1)} %pad_maximum_fusion.1), calls=%async_computation.3 | async-start | bytes 2097152 | tf_op jit(solution)/shard_map/all_to_all | solution.py:31
  193.0 6.2 %collective-permute-start.17 = (bf16[4,2,128,128]{3,2,1,0:T(8,128)(2,1)S(1)}, bf16[4,2,128,128]{3,2,1,0:T(8,128)(2,1)S(1)}, u32[]{:S(2)}, u32[]{:S(2)}) collective-permute-start(bf16[4,2,128,128]{3,2,1,0:T(8,128)(2,1)S(1)} %get-tuple-element.27), channel_id=1, source_target_pairs={{0,1},{1,2},{2,3},{3,0},{4,5},{5,6},{6,7},{7,4},{8,9},{9,10},{10,1... | collective-permute-start | bytes 786440 | tf_op jit(solution)/shard_map/ppermute | solution.py:21
  199.2 1.7 collective-permute-start.16
  200.9 6.8 %collective-permute-done.17.refs_4_ = bf16[4,2,128,128]{3,2,1,0:T(8,128)(2,1)S(1)} collective-permute-done((bf16[4,2,128,128]{3,2,1,0:T(8,128)(2,1)S(1)}, bf16[4,2,128,128]{3,2,1,0:T(8,128)(2,1)S(1)}, u32[]{:S(2)}, u32[]{:S(2)}) %collective-permute-start.17) | collective-permute-done | bytes 262176 | tf_op jit(solution)/shard_map/ppermute | solution.py:21
  207.7 8.6 %collective-permute-done.16.refs_3_ = bf16[4,2,128,128]{3,2,1,0:T(8,128)(2,1)S(1)} collective-permute-done((bf16[4,2,128,128]{3,2,1,0:T(8,128)(2,1)S(1)}, bf16[4,2,128,128]{3,2,1,0:T(8,128)(2,1)S(1)}, u32[]{:S(2)}, u32[]{:S(2)}) %collective-permute-start.16) | collective-permute-done | bytes 262176 | tf_op jit(solution)/shard_map/ppermute | solution.py:21
  216.3 2.5 %shard_map.108 = (bf16[128,4096]{1,0:T(8,128)(2,1)}, bf16[128,4096]{1,0:T(8,128)(2,1)}) custom-call(s32[2]{0:T(128)S(1)} %pad_add_fusion.place_ref, bf16[4,4,2,128,128]{4,3,2,1,0:T(8,128)(2,1)S(1)} %all-to-all-done.3.refs_0_, bf16[4,2,128,128]{3,2,1,0:T(8,128)(2,1)S(1)} %get-tuple-element.29.refs_1_, ...), custom_call_target="tpu_custom_call" | custom-call | bytes 4194304 | tf_op jit(solution)/shard_map/pallas_call | solution.py:86
  (57 shorter events, 4.1 us)
Async XLA Ops:
  0.6 25.9 %collective-permute-start.2 = (bf16[32,4096]{1,0:T(8,128)(2,1)}, bf16[32,4096]{1,0:T(8,128)(2,1)}, u32[]{:S(2)}, u32[]{:S(2)}) collective-permute-start(bf16[32,4096]{1,0:T(8,128)(2,1)} %param.13), channel_id=1, source_target_pairs={{0,2},{1,3},{2,0},{3,1},{4,6},{5,7},{6,4},{7,5},{8,10},{9,11},{10,... | collective-permute-start | bytes 786440 | tf_op jit(solution)/shard_map/ppermute | solution.py:21
  4.0 21.5 %collective-permute-start = (bf16[32,4096]{1,0:T(8,128)(2,1)}, bf16[32,4096]{1,0:T(8,128)(2,1)}, u32[]{:S(2)}, u32[]{:S(2)}) collective-permute-start(bf16[32,4096]{1,0:T(8,128)(2,1)} %param.13), channel_id=1, source_target_pairs={{0,1},{1,2},{2,3},{3,0},{4,5},{5,6},{6,7},{7,4},{8,9},{9,10},{10,1... | collective-permute-start | bytes 786440 | tf_op jit(solution)/shard_map/ppermute | solution.py:21
  5.9 17.7 %collective-permute-start.4 = (bf16[32,4096]{1,0:T(8,128)(2,1)}, bf16[32,4096]{1,0:T(8,128)(2,1)}, u32[]{:S(2)}, u32[]{:S(2)}) collective-permute-start(bf16[32,4096]{1,0:T(8,128)(2,1)} %param.13), channel_id=1, source_target_pairs={{0,3},{1,0},{2,1},{3,2},{4,7},{5,4},{6,5},{7,6},{8,11},{9,8},{10,9... | collective-permute-start | bytes 786440 | tf_op jit(solution)/shard_map/ppermute | solution.py:21
  7.9 1.2 copy-start.3
  9.1 1.2 copy-start.4
  10.3 1.2 copy-start.5
  11.6 1.2 copy-start.6
  14.4 1.3 copy-start.2
  15.8 0.8 copy-start.11
  16.6 0.8 copy-start.13
  17.4 0.8 copy-start.15
  18.2 0.8 copy-start.17
  19.0 4.6 %copy-start.18 = (bf16[32,4096]{1,0:T(8,128)(2,1)S(1)}, bf16[32,4096]{1,0:T(8,128)(2,1)}, u32[]{:S(2)}) copy-start(bf16[32,4096]{1,0:T(8,128)(2,1)} %param.13) | copy-start | bytes 786436
  19.0 65.3 %all-to-all-start = ((bf16[4,4,4,128,128]{4,3,2,1,0:T(8,128)(2,1)}), bf16[4,4,4,128,128]{4,3,2,1,0:T(8,128)(2,1)S(1)}, u32[]{:S(2)}, u32[]{:S(2)}) async-start(bf16[4,4,4,128,128]{4,3,2,1,0:T(8,128)(2,1)} %copy-done.2), calls=%async_computation | async-start | bytes 4194304 | tf_op jit(solution)/shard_map/all_to_all | solution.py:31
  23.6 9.6 %copy-start.16 = (bf16[4,4,128,128]{3,2,1,0:T(8,128)(2,1)S(1)}, bf16[4,4,128,128]{3,2,1,0:T(8,128)(2,1)}, u32[]{:S(2)}) copy-start(bf16[4,4,128,128]{3,2,1,0:T(8,128)(2,1)} %copy-done.15) | copy-start | bytes 1572868
  23.6 25.4 %copy-start.14 = (bf16[4,4,128,128]{3,2,1,0:T(8,128)(2,1)S(1)}, bf16[4,4,128,128]{3,2,1,0:T(8,128)(2,1)}, u32[]{:S(2)}) copy-start(bf16[4,4,128,128]{3,2,1,0:T(8,128)(2,1)} %copy-done.13) | copy-start | bytes 1572868
  23.6 59.1 %copy-start.12 = (bf16[4,4,128,128]{3,2,1,0:T(8,128)(2,1)S(1)}, bf16[4,4,128,128]{3,2,1,0:T(8,128)(2,1)}, u32[]{:S(2)}) copy-start(bf16[4,4,128,128]{3,2,1,0:T(8,128)(2,1)} %copy-done.11) | copy-start | bytes 1572868
  23.6 25.3 %collective-permute-start.5 = (bf16[4,4,128,128]{3,2,1,0:T(8,128)(2,1)}, bf16[4,4,128,128]{3,2,1,0:T(8,128)(2,1)S(1)}, u32[]{:S(2)}, u32[]{:S(2)}) collective-permute-start(bf16[4,4,128,128]{3,2,1,0:T(8,128)(2,1)} %copy-done.17), channel_id=1, source_target_pairs={{0,3},{1,0},{2,1},{3,2},{4,7},{5,4},{6,5},{7,6},{8,11},{9,8},{10,9... | collective-permute-start | bytes 1572872 | tf_op jit(solution)/shard_map/ppermute | solution.py:21
  28.5 57.1 %collective-permute-start.8 = (bf16[128,4096]{1,0:T(8,128)(2,1)S(1)}, bf16[128,4096]{1,0:T(8,128)(2,1)}, u32[]{:S(2)}, u32[]{:S(2)}) collective-permute-start(bf16[128,4096]{1,0:T(8,128)(2,1)S(1)} %constant_dynamic-update-slice_fusion.refs_0_), channel_id=1, source_target_pairs={{0,12},{1,13},{2,14},{3,15},{4,0},{5,1},{6,2},{7,3},{8,4},{9,5},{1... | collective-permute-start | bytes 3145736 | tf_op jit(solution)/shard_map/ppermute | solution.py:26
  31.6 54.0 %collective-permute-start.7 = (bf16[128,4096]{1,0:T(8,128)(2,1)S(1)}, bf16[128,4096]{1,0:T(8,128)(2,1)}, u32[]{:S(2)}, u32[]{:S(2)}) collective-permute-start(bf16[128,4096]{1,0:T(8,128)(2,1)S(1)} %constant_dynamic-update-slice_fusion.refs_0_), channel_id=1, source_target_pairs={{0,8},{1,9},{2,10},{3,11},{4,12},{5,13},{6,14},{7,15},{8,0},{9,1},... | collective-permute-start | bytes 3145736 | tf_op jit(solution)/shard_map/ppermute | solution.py:26
  32.2 61.6 %collective-permute-start.6 = (bf16[128,4096]{1,0:T(8,128)(2,1)S(1)}, bf16[128,4096]{1,0:T(8,128)(2,1)}, u32[]{:S(2)}, u32[]{:S(2)}) collective-permute-start(bf16[128,4096]{1,0:T(8,128)(2,1)S(1)} %constant_dynamic-update-slice_fusion.refs_0_), channel_id=1, source_target_pairs={{0,4},{1,5},{2,6},{3,7},{4,8},{5,9},{6,10},{7,11},{8,12},{9,13},{1... | collective-permute-start | bytes 3145736 | tf_op jit(solution)/shard_map/ppermute | solution.py:26
  33.2 49.5 %collective-permute-start.3 = (bf16[4,4,128,128]{3,2,1,0:T(8,128)(2,1)S(1)}, bf16[4,4,128,128]{3,2,1,0:T(8,128)(2,1)S(1)}, u32[]{:S(2)}, u32[]{:S(2)}) collective-permute-start(bf16[4,4,128,128]{3,2,1,0:T(8,128)(2,1)S(1)} %copy-done.16), channel_id=1, source_target_pairs={{0,2},{1,3},{2,0},{3,1},{4,6},{5,7},{6,4},{7,5},{8,10},{9,11},{10,... | collective-permute-start | bytes 1572872 | tf_op jit(solution)/shard_map/ppermute | solution.py:21
  49.0 33.7 %collective-permute-start.1 = (bf16[4,4,128,128]{3,2,1,0:T(8,128)(2,1)S(1)}, bf16[4,4,128,128]{3,2,1,0:T(8,128)(2,1)S(1)}, u32[]{:S(2)}, u32[]{:S(2)}) collective-permute-start(bf16[4,4,128,128]{3,2,1,0:T(8,128)(2,1)S(1)} %copy-done.14), channel_id=1, source_target_pairs={{0,1},{1,2},{2,3},{3,0},{4,5},{5,6},{6,7},{7,4},{8,9},{9,10},{10,1... | collective-permute-start | bytes 1572872 | tf_op jit(solution)/shard_map/ppermute | solution.py:21
  93.8 5.3 %copy-start.19 = (s32[16]{0:T(128)S(1)}, s32[16]{0:T(128)}, u32[]{:S(2)}) copy-start(s32[16]{0:T(128)} %param.14) | copy-start | bytes 196
  93.8 29.2 %all-to-all-start.1 = ((bf16[4,4,4,128,128]{4,3,2,1,0:T(8,128)(2,1)}), bf16[4,4,4,128,128]{4,3,2,1,0:T(8,128)(2,1)}, u32[]{:S(2)}, u32[]{:S(2)}) async-start(bf16[4,4,4,128,128]{4,3,2,1,0:T(8,128)(2,1)} %pad_maximum_fusion), calls=%async_computation.1 | async-start | bytes 4194304 | tf_op jit(solution)/shard_map/all_to_all | solution.py:31
  99.5 34.0 %collective-permute-start.14 = (bf16[4,4,128,128]{3,2,1,0:T(8,128)(2,1)}, bf16[4,4,128,128]{3,2,1,0:T(8,128)(2,1)}, u32[]{:S(2)}, u32[]{:S(2)}) collective-permute-start(bf16[4,4,128,128]{3,2,1,0:T(8,128)(2,1)} %get-tuple-element.24), channel_id=1, source_target_pairs={{0,3},{1,0},{2,1},{3,2},{4,7},{5,4},{6,5},{7,6},{8,11},{9,8},{10,9... | collective-permute-start | bytes 1572872 | tf_op jit(solution)/shard_map/ppermute | solution.py:21
  99.8 48.3 %collective-permute-start.13 = (bf16[4,4,128,128]{3,2,1,0:T(8,128)(2,1)}, bf16[4,4,128,128]{3,2,1,0:T(8,128)(2,1)}, u32[]{:S(2)}, u32[]{:S(2)}) collective-permute-start(bf16[4,4,128,128]{3,2,1,0:T(8,128)(2,1)} %get-tuple-element.25), channel_id=1, source_target_pairs={{0,2},{1,3},{2,0},{3,1},{4,6},{5,7},{6,4},{7,5},{8,10},{9,11},{10,... | collective-permute-start | bytes 1572872 | tf_op jit(solution)/shard_map/ppermute | solution.py:21
  102.1 46.0 %collective-permute-start.12 = (bf16[4,4,128,128]{3,2,1,0:T(8,128)(2,1)}, bf16[4,4,128,128]{3,2,1,0:T(8,128)(2,1)}, u32[]{:S(2)}, u32[]{:S(2)}) collective-permute-start(bf16[4,4,128,128]{3,2,1,0:T(8,128)(2,1)} %get-tuple-element.26), channel_id=1, source_target_pairs={{0,1},{1,2},{2,3},{3,0},{4,5},{5,6},{6,7},{7,4},{8,9},{9,10},{10,1... | collective-permute-start | bytes 1572872 | tf_op jit(solution)/shard_map/ppermute | solution.py:21
  104.0 1.6 copy-start
  105.6 1.6 copy-start.1
  111.9 0.8 copy-start.8
  123.0 1.0 copy-start.9
  124.1 24.0 %copy-start.10 = (bf16[512,512]{1,0:T(8,128)(2,1)S(1)}, bf16[512,512]{1,0:T(8,128)(2,1)}, u32[]{:S(2)}) copy-start(bf16[512,512]{1,0:T(8,128)(2,1)} %copy-done.8) | copy-start | bytes 1572868
  157.4 1.0 copy-start.7
  158.3 18.9 %all-to-all-start.2 = ((bf16[4,4,2,128,128]{4,3,2,1,0:T(8,128)(2,1)}), bf16[4,4,2,128,128]{4,3,2,1,0:T(8,128)(2,1)S(1)}, u32[]{:S(2)}, u32[]{:S(2)}) async-start(bf16[4,4,2,128,128]{4,3,2,1,0:T(8,128)(2,1)} %copy-done.7), calls=%async_computation.2 | async-start | bytes 2097152 | tf_op jit(solution)/shard_map/all_to_all | solution.py:31
  163.6 13.8 %collective-permute-start.11 = (bf16[4,2,128,128]{3,2,1,0:T(8,128)(2,1)}, bf16[4,2,128,128]{3,2,1,0:T(8,128)(2,1)S(1)}, u32[]{:S(2)}, u32[]{:S(2)}) collective-permute-start(bf16[4,2,128,128]{3,2,1,0:T(8,128)(2,1)} %get-tuple-element.32), channel_id=1, source_target_pairs={{0,1},{1,2},{2,3},{3,0},{4,5},{5,6},{6,7},{7,4},{8,9},{9,10},{10,1... | collective-permute-start | bytes 786440 | tf_op jit(solution)/shard_map/ppermute | solution.py:21
  163.6 20.6 %collective-permute-start.10 = (bf16[4,2,128,128]{3,2,1,0:T(8,128)(2,1)S(1)}, bf16[4,2,128,128]{3,2,1,0:T(8,128)(2,1)S(1)}, u32[]{:S(2)}, u32[]{:S(2)}) collective-permute-start(bf16[4,2,128,128]{3,2,1,0:T(8,128)(2,1)S(1)} %get-tuple-element.33), channel_id=1, source_target_pairs={{0,2},{1,3},{2,0},{3,1},{4,6},{5,7},{6,4},{7,5},{8,10},{9,11},{10,... | collective-permute-start | bytes 786440 | tf_op jit(solution)/shard_map/ppermute | solution.py:21
  163.6 20.6 %collective-permute-start.9 = (bf16[4,2,128,128]{3,2,1,0:T(8,128)(2,1)S(1)}, bf16[4,2,128,128]{3,2,1,0:T(8,128)(2,1)S(1)}, u32[]{:S(2)}, u32[]{:S(2)}) collective-permute-start(bf16[4,2,128,128]{3,2,1,0:T(8,128)(2,1)S(1)} %get-tuple-element.34), channel_id=1, source_target_pairs={{0,3},{1,0},{2,1},{3,2},{4,7},{5,4},{6,5},{7,6},{8,11},{9,8},{10,9... | collective-permute-start | bytes 786440 | tf_op jit(solution)/shard_map/ppermute | solution.py:21
  177.3 11.1 %collective-permute-start.15 = (bf16[4,2,128,128]{3,2,1,0:T(8,128)(2,1)S(1)}, bf16[4,2,128,128]{3,2,1,0:T(8,128)(2,1)S(1)}, u32[]{:S(2)}, u32[]{:S(2)}) collective-permute-start(bf16[4,2,128,128]{3,2,1,0:T(8,128)(2,1)S(1)} %get-tuple-element.30), channel_id=1, source_target_pairs={{0,3},{1,0},{2,1},{3,2},{4,7},{5,4},{6,5},{7,6},{8,11},{9,8},{10,9... | collective-permute-start | bytes 786440 | tf_op jit(solution)/shard_map/ppermute | solution.py:21
  188.5 27.9 %all-to-all-start.3 = ((bf16[4,4,2,128,128]{4,3,2,1,0:T(8,128)(2,1)}), bf16[4,4,2,128,128]{4,3,2,1,0:T(8,128)(2,1)S(1)}, u32[]{:S(2)}, u32[]{:S(2)}) async-start(bf16[4,4,2,128,128]{4,3,2,1,0:T(8,128)(2,1)} %pad_maximum_fusion.1), calls=%async_computation.3 | async-start | bytes 2097152 | tf_op jit(solution)/shard_map/all_to_all | solution.py:31
  193.0 14.7 %collective-permute-start.17 = (bf16[4,2,128,128]{3,2,1,0:T(8,128)(2,1)S(1)}, bf16[4,2,128,128]{3,2,1,0:T(8,128)(2,1)S(1)}, u32[]{:S(2)}, u32[]{:S(2)}) collective-permute-start(bf16[4,2,128,128]{3,2,1,0:T(8,128)(2,1)S(1)} %get-tuple-element.27), channel_id=1, source_target_pairs={{0,1},{1,2},{2,3},{3,0},{4,5},{5,6},{6,7},{7,4},{8,9},{9,10},{10,1... | collective-permute-start | bytes 786440 | tf_op jit(solution)/shard_map/ppermute | solution.py:21
  199.2 17.1 %collective-permute-start.16 = (bf16[4,2,128,128]{3,2,1,0:T(8,128)(2,1)S(1)}, bf16[4,2,128,128]{3,2,1,0:T(8,128)(2,1)S(1)}, u32[]{:S(2)}, u32[]{:S(2)}) collective-permute-start(bf16[4,2,128,128]{3,2,1,0:T(8,128)(2,1)S(1)} %get-tuple-element.28), channel_id=1, source_target_pairs={{0,2},{1,3},{2,0},{3,1},{4,6},{5,7},{6,4},{7,5},{8,10},{9,11},{10,... | collective-permute-start | bytes 786440 | tf_op jit(solution)/shard_map/ppermute | solution.py:21
